TPU v7x, 128 devices: a whole 4x4x4 slice. The times are simulated.
128 devices in a mesh: sp: 64 (over y, x_hi, z, core), tp: 2 (over x_lo).
Axes of the slice: x: 4 (x_hi: 2, x_lo: 2; x = x_hi * 2 + x_lo), y: 4, z: 4, core: 2. Of those that a mesh axis runs over, the one named last changes fastest.
Arguments:
- layer_input: bfloat16 [16384, 1152], P(('sp', 'tp')), may hold values from -6 to 6
- segment_ids: int32 [16384], replicated, may hold values from 0 to 3, as said below
- positions: int32 [16384], replicated, may hold values from 0 to 16383, as said below
- w_query: bfloat16 [1152, 1024], P(None, 'tp'), may hold values from -0.1875 to 0.1875
- w_key: bfloat16 [1152, 256], replicated, may hold values from -0.1875 to 0.1875
- w_value: bfloat16 [1152, 256], replicated, may hold values from -0.1875 to 0.1875
- w_out: bfloat16 [1024, 1152], P('tp'), may hold values from -0.1875 to 0.1875
- w_gate: bfloat16 [1152, 6912], P(None, 'tp'), may hold values from -0.1875 to 0.1875
- w_up: bfloat16 [1152, 6912], P(None, 'tp'), may hold values from -0.1875 to 0.1875
- w_down: bfloat16 [6912, 1152], P('tp'), may hold values from -0.078125 to 0.078125
- norm_attn: float32 [1152], replicated, may hold values from 0.5 to 1.5
- norm_query: float32 [256], replicated, may hold values from 0.1 to 1.9
- norm_key: float32 [256], replicated, may hold values from 0.1 to 1.9
- norm_post: float32 [1152], replicated, may hold values from 0.5 to 1.5
- norm_ffn: float32 [1152], replicated, may hold values from 0.5 to 1.5
- norm_out: float32 [1152], replicated, may hold values from 0.5 to 1.5
- cotangent: bfloat16 [16384, 1152], P(('sp', 'tp')), may hold values from -6 to 6
Outputs:
- layer_output: bfloat16 [16384, 1152], P(('sp', 'tp'))
- d_input: bfloat16 [16384, 1152], P(('sp', 'tp'))
- d_w_query: float32 [1152, 1024], P('sp', 'tp')
- d_w_key: float32 [1152, 256], replicated
- d_w_value: float32 [1152, 256], replicated
- d_w_out: float32 [1024, 1152], P('tp', 'sp')
- d_w_gate: float32 [1152, 6912], P('sp', 'tp')
- d_w_up: float32 [1152, 6912], P('sp', 'tp')
- d_w_down: float32 [6912, 1152], P('tp', 'sp')
- d_norm_attn: float32 [1152], replicated
- d_norm_query: float32 [256], replicated
- d_norm_key: float32 [256], replicated
- d_norm_post: float32 [1152], replicated
- d_norm_ffn: float32 [1152], replicated
- d_norm_out: float32 [1152], replicated
Inputs may be any that keep to these rules, and one draw needn't show every extreme that they name: `segment_ids`: segment numbers never fall along the tokens and every number names at least one token; one document, whose number varies, covers all but at most (3) * (32) tokens. The first token of every document has position 0, and positions rise by 1 or 2 from one token to the next within a document.
All inputs are finite; a program needn't handle non-finite values.
Results may differ from a plain program's by a relative error of at most 0.02.
Values may be sent and summed in bfloat16 or wider, within the bound.
A program may use at most 448 MiB of HBM per device.

v0:
```python
import math

import jax
import jax.numpy as jnp
from jax import lax
from jax.sharding import PartitionSpec as P

EPS = 1e-06
THETA = 1000000.0
NEG = -1e30


def rms_scale(tensor, scaling):
    return tensor * lax.rsqrt(jnp.mean(tensor * tensor, axis=-1, keepdims=True) + EPS) * scaling


def angles(token_pos, head_size):
    middle = head_size // 2
    frequency = THETA ** (-2.0 * jnp.arange(middle, dtype=jnp.float32) / head_size)
    turned = token_pos.astype(jnp.float32)[:, None] * frequency[None, :]
    return (jnp.cos(turned), jnp.sin(turned))


def rotary(tensor, cosine, sine):
    middle = tensor.shape[-1] // 2
    lower_half = tensor[..., :middle]
    upper_half = tensor[..., middle:]
    return jnp.concatenate(
        [lower_half * cosine - upper_half * sine, upper_half * cosine + lower_half * sine], axis=-1
    )


def rounded(tensor):
    return lax.optimization_barrier(tensor.astype(jnp.bfloat16)).astype(jnp.float32)


def contract(left_op, right_op, left_dim, right_dim):
    return lax.dot_general(
        left_op,
        right_op,
        (((left_dim,), (right_dim,)), ((), ())),
        preferred_element_type=jnp.float32,
    )


def glu_piece(gate_in, up_in):
    return jax.nn.gelu(gate_in, approximate=True) * up_in


def shards(
    layer_input,
    segment_ids,
    positions,
    w_query,
    w_key,
    w_value,
    w_out,
    w_gate,
    w_up,
    w_down,
    norm_attn,
    norm_query,
    norm_key,
    norm_post,
    norm_ffn,
    norm_out,
    cotangent,
):
    own_rows = layer_input.shape[0]
    tp_ways = lax.axis_size("tp")
    group_rows = own_rows * tp_ways
    total_rows = segment_ids.shape[0]
    head_size = w_key.shape[1]
    local_heads = w_query.shape[1] // head_size
    query_rows = local_heads * group_rows
    scale_factor = head_size ** (-0.5)
    block_keys = math.gcd(total_rows, 1024)
    block_count = total_rows // block_keys
    group_start = lax.axis_index("sp") * group_rows
    own_start = group_start + lax.axis_index("tp") * own_rows
    last_query = group_start + group_rows - 1
    cos_group, sin_group = angles(
        lax.dynamic_slice_in_dim(positions, group_start, group_rows), head_size
    )
    cos_own, sin_own = angles(lax.dynamic_slice_in_dim(positions, own_start, own_rows), head_size)
    query_segs = jnp.tile(
        lax.dynamic_slice_in_dim(segment_ids, group_start, group_rows), local_heads
    )
    query_index = group_start + jnp.tile(jnp.arange(group_rows, dtype=jnp.int32), local_heads)

    def query_piece(pre_rot, scaling):
        return rotary(rms_scale(pre_rot, scaling), cos_group[:, None, :], sin_group[:, None, :])

    def key_piece(pre_rot, scaling):
        return rotary(rms_scale(pre_rot, scaling), cos_own, sin_own)

    input_f = layer_input.astype(jnp.float32)
    h_attn = rms_scale(input_f, norm_attn).astype(jnp.bfloat16)
    h_group = lax.all_gather(h_attn, "tp", axis=0, tiled=True)
    q_pre = jnp.dot(h_group, w_query, preferred_element_type=jnp.float32).reshape(
        group_rows, local_heads, head_size
    )
    q_rot = query_piece(q_pre, norm_query).astype(jnp.bfloat16)
    q_flat = q_rot.transpose(1, 0, 2).reshape(query_rows, head_size)
    k_pre = jnp.dot(h_attn, w_key, preferred_element_type=jnp.float32)
    k_rot = key_piece(k_pre, norm_key).astype(jnp.bfloat16)
    v_own = jnp.dot(h_attn, w_value, preferred_element_type=jnp.float32).astype(jnp.bfloat16)
    keys_all, values_all = (
        lax.all_gather(k_rot, ("sp", "tp"), axis=0, tiled=True),
        lax.all_gather(v_own, ("sp", "tp"), axis=0, tiled=True),
    )

    def block_scores(start):
        key_block = lax.dynamic_slice_in_dim(keys_all, start, block_keys)
        value_block = lax.dynamic_slice_in_dim(values_all, start, block_keys)
        raw = contract(q_flat, key_block, 1, 1) * scale_factor
        key_segs = lax.dynamic_slice_in_dim(segment_ids, start, block_keys)
        key_index = start + jnp.arange(block_keys, dtype=jnp.int32)
        allowed = (query_segs[:, None] == key_segs[None, :]) & (
            query_index[:, None] >= key_index[None, :]
        )
        return (jnp.where(allowed, raw, NEG), allowed, key_block, value_block)

    def stats_step(block, stats):

        def stats_visit(stats_in):
            top, total = stats_in
            scores, allowed, key_block, value_block = block_scores(block * block_keys)
            new_top = jnp.maximum(top, jnp.max(scores, axis=1))
            weights = jnp.where(allowed, jnp.exp(scores - new_top[:, None]), 0.0)
            return (new_top, total * jnp.exp(top - new_top) + jnp.sum(weights, axis=1))

        def keep_stats(stats_in):
            return stats_in

        return lax.cond(block * block_keys <= last_query, stats_visit, keep_stats, stats)

    start_stats = (jnp.full((query_rows,), NEG, jnp.float32), jnp.zeros((query_rows,), jnp.float32))
    top_final, total_final = lax.fori_loop(0, block_count, stats_step, start_stats)
    log_total = top_final + jnp.log(total_final)

    def output_step(block, accum):

        def output_visit(accum_in):
            scores, allowed, key_block, value_block = block_scores(block * block_keys)
            probs = jnp.where(allowed, jnp.exp(scores - log_total[:, None]), 0.0).astype(
                jnp.bfloat16
            )
            return accum_in + jnp.dot(probs, value_block, preferred_element_type=jnp.float32)

        def keep_accum(accum_in):
            return accum_in

        return lax.cond(block * block_keys <= last_query, output_visit, keep_accum, accum)

    attended = lax.fori_loop(
        0, block_count, output_step, jnp.zeros((query_rows, head_size), jnp.float32)
    )
    o_cat = (
        attended.astype(jnp.bfloat16)
        .reshape(local_heads, group_rows, head_size)
        .transpose(1, 0, 2)
        .reshape(group_rows, local_heads * head_size)
    )
    attn_out = lax.psum_scatter(
        jnp.dot(o_cat, w_out, preferred_element_type=jnp.float32).astype(jnp.bfloat16),
        "tp",
        scatter_dimension=0,
        tiled=True,
    ).astype(jnp.float32)
    mid = input_f + rms_scale(attn_out, norm_post)
    h_ffn = rms_scale(mid, norm_ffn).astype(jnp.bfloat16)
    h_ffn_group = lax.all_gather(h_ffn, "tp", axis=0, tiled=True)
    gate = jnp.dot(h_ffn_group, w_gate, preferred_element_type=jnp.float32)
    upper = jnp.dot(h_ffn_group, w_up, preferred_element_type=jnp.float32)
    act = glu_piece(gate, upper).astype(jnp.bfloat16)
    ffn_out = lax.psum_scatter(
        jnp.dot(act, w_down, preferred_element_type=jnp.float32).astype(jnp.bfloat16),
        "tp",
        scatter_dimension=0,
        tiled=True,
    ).astype(jnp.float32)
    layer_output = (mid + rms_scale(ffn_out, norm_out)).astype(jnp.bfloat16)
    grad_out = cotangent.astype(jnp.float32)
    _, pull_out = jax.vjp(rms_scale, ffn_out, norm_out)
    d_ffn_out, d_norm_out = pull_out(grad_out)
    d_ffn_group = lax.all_gather(d_ffn_out.astype(jnp.bfloat16), "tp", axis=0, tiled=True)
    d_act = contract(d_ffn_group, w_down, 1, 1)
    d_w_down = contract(act, d_ffn_group, 0, 0)
    _, pull_glu = jax.vjp(glu_piece, gate, upper)
    d_gate, d_upper = pull_glu(d_act)
    d_gate = d_gate.astype(jnp.bfloat16)
    d_upper = d_upper.astype(jnp.bfloat16)
    d_w_gate = contract(h_ffn_group, d_gate, 0, 0)
    d_w_up = contract(h_ffn_group, d_upper, 0, 0)
    d_h_ffn = lax.psum_scatter(
        (contract(d_gate, w_gate, 1, 1) + contract(d_upper, w_up, 1, 1)).astype(jnp.bfloat16),
        "tp",
        scatter_dimension=0,
        tiled=True,
    ).astype(jnp.float32)
    _, pull_ffn = jax.vjp(rms_scale, mid, norm_ffn)
    d_mid_norm, d_norm_ffn = pull_ffn(d_h_ffn)
    d_mid = grad_out + d_mid_norm
    _, pull_post = jax.vjp(rms_scale, attn_out, norm_post)
    d_attn_out, d_norm_post = pull_post(d_mid)
    d_attn_group = lax.all_gather(d_attn_out.astype(jnp.bfloat16), "tp", axis=0, tiled=True)
    d_o_cat = contract(d_attn_group, w_out, 1, 1)
    d_w_out = contract(o_cat, d_attn_group, 0, 0)
    d_heads = (
        d_o_cat.reshape(group_rows, local_heads, head_size)
        .transpose(1, 0, 2)
        .reshape(query_rows, head_size)
        .astype(jnp.bfloat16)
    )
    delta = jnp.sum(d_heads.astype(jnp.float32) * attended, axis=1)

    def grad_step(block, grads_in):

        def grad_visit(pair_in):
            d_query, d_kv = pair_in
            start = block * block_keys
            scores, allowed, key_block, value_block = block_scores(start)
            probs_f = jnp.where(allowed, jnp.exp(scores - log_total[:, None]), 0.0)
            probs = probs_f.astype(jnp.bfloat16)
            d_probs = contract(d_heads, value_block, 1, 1)
            d_scores = (probs_f * (d_probs - delta[:, None]) * scale_factor).astype(jnp.bfloat16)
            d_query = d_query + jnp.dot(d_scores, key_block, preferred_element_type=jnp.float32)
            d_key_block = contract(d_scores, q_flat, 0, 0)
            d_value_block = contract(probs, d_heads, 0, 0)
            d_kv = lax.dynamic_update_slice_in_dim(
                d_kv, jnp.concatenate([d_key_block, d_value_block], axis=1), start, 0
            )
            return (d_query, d_kv)

        def keep_grads(pair_in):
            return pair_in

        return lax.cond(block * block_keys <= last_query, grad_visit, keep_grads, grads_in)

    start_grads = (
        jnp.zeros((query_rows, head_size), jnp.float32),
        jnp.zeros((total_rows, 2 * head_size), jnp.float32),
    )
    d_query_all, d_kv_all = lax.fori_loop(0, block_count, grad_step, start_grads)
    mine = lax.psum_scatter(d_kv_all, ("sp", "tp"), scatter_dimension=0, tiled=True)
    d_key_rot = rounded(mine[:, :head_size])
    d_value = mine[:, head_size:].astype(jnp.bfloat16)
    _, pull_key = jax.vjp(key_piece, k_pre, norm_key)
    d_k_pre, d_norm_key = pull_key(d_key_rot)
    d_k_pre = d_k_pre.astype(jnp.bfloat16)
    d_q_rot = rounded(d_query_all).reshape(local_heads, group_rows, head_size).transpose(1, 0, 2)
    _, pull_query = jax.vjp(query_piece, q_pre, norm_query)
    d_q_pre, d_norm_query = pull_query(d_q_rot)
    d_q_pre = d_q_pre.reshape(group_rows, local_heads * head_size).astype(jnp.bfloat16)
    d_h_query = lax.psum_scatter(
        contract(d_q_pre, w_query, 1, 1).astype(jnp.bfloat16), "tp", scatter_dimension=0, tiled=True
    ).astype(jnp.float32)
    d_h_attn = d_h_query + contract(d_k_pre, w_key, 1, 1) + contract(d_value, w_value, 1, 1)
    d_w_query = contract(h_group, d_q_pre, 0, 0)
    d_w_key = contract(h_attn, d_k_pre, 0, 0)
    d_w_value = contract(h_attn, d_value, 0, 0)
    _, pull_attn = jax.vjp(rms_scale, input_f, norm_attn)
    d_input_norm, d_norm_attn = pull_attn(d_h_attn)
    d_input = (d_mid + d_input_norm).astype(jnp.bfloat16)
    sharded = (
        lax.psum_scatter(d_w_query, "sp", scatter_dimension=0, tiled=True),
        lax.psum_scatter(d_w_out, "sp", scatter_dimension=1, tiled=True),
        lax.psum_scatter(d_w_gate, "sp", scatter_dimension=0, tiled=True),
        lax.psum_scatter(d_w_up, "sp", scatter_dimension=0, tiled=True),
        lax.psum_scatter(d_w_down, "sp", scatter_dimension=1, tiled=True),
    )
    shared = lax.psum(
        (
            d_w_key,
            d_w_value,
            d_norm_attn,
            d_norm_query,
            d_norm_key,
            d_norm_post,
            d_norm_ffn,
            d_norm_out,
        ),
        ("sp", "tp"),
    )
    return (
        layer_output,
        d_input,
        sharded[0],
        shared[0],
        shared[1],
        sharded[1],
        sharded[2],
        sharded[3],
        sharded[4],
        shared[2],
        shared[3],
        shared[4],
        shared[5],
        shared[6],
        shared[7],
    )


def solution(mesh):
    in_specs = (
        P(("sp", "tp"), None),
        P(),
        P(),
        P(None, "tp"),
        P(),
        P(),
        P("tp", None),
        P(None, "tp"),
        P(None, "tp"),
        P("tp", None),
        P(),
        P(),
        P(),
        P(),
        P(),
        P(),
        P(("sp", "tp"), None),
    )
    out_specs = (
        P(("sp", "tp"), None),
        P(("sp", "tp"), None),
        P("sp", "tp"),
        P(),
        P(),
        P("tp", "sp"),
        P("sp", "tp"),
        P("sp", "tp"),
        P("tp", "sp"),
        P(),
        P(),
        P(),
        P(),
        P(),
        P(),
    )
    return jax.shard_map(shards, mesh=mesh, in_specs=in_specs, out_specs=out_specs, check_vma=False)
```

profile of v0, /device:TPU:1, one launch (start us, length us, event | category | flops | bytes accessed | tf_op | source)
XLA Modules:
  0.0 2536.3 jit_solution(12370087791244501289)
XLA Ops:
  16.0 8.9 all_gather.19
  30.3 299.6 %all-gather.3.cloned.1.call-done = bf16[16384,256]{1,0:T(8,128)(2,1)} async-done(((bf16[128,256]{1,0:T(8,128)(2,1)}), bf16[16384,256]{1,0:T(8,128)(2,1)}) %all-gather.3.cloned.1.call-update) | async-done | bytes 8388624 | tf_op jit(solution)/shard_map/all_gather | solution.py:109
  334.3 309.9 %all-gather.5.cloned.1.call-done = bf16[16384,256]{1,0:T(8,128)(2,1)} async-done(((bf16[128,256]{1,0:T(8,128)(2,1)}), bf16[16384,256]{1,0:T(8,128)(2,1)}) %all-gather.5.cloned.1.call-update) | async-done | bytes 8388624 | tf_op jit(solution)/shard_map/all_gather | solution.py:110
  650.1 65.9 %reduce-scatter.10.cloned.1.call-done = bf16[128,1152]{1,0:T(8,128)(2,1)} async-done(((bf16[256,1152]{1,0:T(8,128)(2,1)}), bf16[128,1152]{1,0:T(8,128)(2,1)}) %reduce-scatter.10.cloned.1.call-update) | async-done | bytes 294928 | tf_op jit(solution)/shard_map/reduce_scatter | solution.py:165
  719.6 8.7 all_gather.21
  734.3 9.0 multiply_convert_fusion.1
  747.9 19.7 reduce-scatter.12.cloned.1.call-done
  771.9 8.7 all_gather.22
  780.7 10.1 multiply_convert_fusion
  793.4 7.9 fusion.121
  804.9 9.5 fusion.122
  829.7 8.6 all_gather.23
  839.9 11.2 broadcast_in_dim.49
  851.1 9.1 while.51
  851.1 8.3 conditional.11
  860.2 33.6 %copy.65 = f32[16384,512]{1,0:T(8,128)} copy(f32[16384,512]{0,1:T(8,128)} %get-tuple-element.673) | data formatting | bytes 67108864 | tf_op jit(solution)/shard_map/while | solution.py:245
  901.2 318.2 %fusion.112 = (f32[24,512]{1,0:T(8,128)S(1)}, f32[512,24]{0,1:T(8,128)S(1)}) fusion(f32[1152,512]{1,0:T(8,128)} %fusion.118, f32[512,1152]{0,1:T(8,128)} %fusion.120), kind=kCustom, calls=%all-reduce-scatter.2 | all-reduce-scatter fusion | flops 1572865 | bytes 4817408
  1232.7 14.7 collective-permute-start.9
  1317.2 11.6 collective-permute-start.16
  1335.5 282.2 %all-reduce.20.cloned.1.call-done = (f32[1152,3456]{1,0:T(8,128)}, f32[1152,3456]{1,0:T(8,128)}, f32[3456,1152]{0,1:T(8,128)}) async-done(((f32[1152,3456]{1,0:T(8,128)}, f32[1152,3456]{1,0:T(8,128)}, f32[3456,1152]{0,1:T(8,128)}), (f32[1152,3456]{1,0:T(8,128)}, f32[1152,3456]{1,0:T(8,128)}, f32[3456,1152]{0,1:T(8,128)})) %all-reduce.20.cloned.1.call-update) | async-done | bytes 47775760
  1621.5 725.1 %reduce-scatter.18.cloned.1.call-done = f32[128,512]{1,0:T(8,128)} async-done(((f32[16384,512]{1,0:T(8,128)}), f32[128,512]{1,0:T(8,128)}) %reduce-scatter.18.cloned.1.call-update) | async-done | bytes 262160 | tf_op jit(solution)/shard_map/reduce_scatter | solution.py:246
  2351.1 16.9 reduce-scatter.16.cloned.1.call-done
  2369.8 66.8 %all-reduce.11 = (f32[1152]{0:T(1024)}, f32[256]{0:T(256)}, f32[256]{0:T(256)}, f32[1152]{0:T(1024)}, f32[1152]{0:T(1024)}, /*index=5*/f32[1152]{0:T(1024)}) all-reduce(f32[1152]{0:T(1024)S(1)} %get-tuple-element.778, f32[256]{0:T(256)S(1)} %copy-done.53, ...), channel_id=1, replica_groups=mesh['sp'=64,'tp'=2] {'sp','tp'}, use_global_device_ids=true, to_apply=%region_40.41 | all-reduce | flops 5120 | bytes 40960 | tf_op jit(solution)/shard_map/psum | solution.py:273
  2437.5 88.2 %all-reduce.18.cloned.1.call-done = (f32[1152,256]{1,0:T(8,128)}, f32[1152,256]{1,0:T(8,128)}) async-done(((f32[1152,256]{1,0:T(8,128)}, f32[1152,256]{1,0:T(8,128)}), (f32[1152,256]{1,0:T(8,128)}, f32[1152,256]{1,0:T(8,128)})) %all-reduce.18.cloned.1.call-update) | async-done | bytes 2359312 | tf_op jit(solution)/shard_map/psum | solution.py:273
  (436 shorter events, 197.7 us)
Async XLA Ops:
  7.2 322.7 %all-gather.3.cloned.1.call-start = ((), (), s32[]{:S(2)}) async-start(), calls=%async_computation.5 | async-start | bytes 8454144 | tf_op jit(solution)/shard_map/all_gather | solution.py:109
  14.9 629.2 %all-gather.5.cloned.1.call-start = ((), (), s32[]{:S(2)}) async-start(), calls=%async_computation.6 | async-start | bytes 8454144 | tf_op jit(solution)/shard_map/all_gather | solution.py:110
  15.9 700.1 %reduce-scatter.10.cloned.1.call-start = ((), (), s32[]{:S(2)}) async-start(), calls=%async_computation.7 | async-start | bytes 884736 | tf_op jit(solution)/shard_map/reduce_scatter | solution.py:165
  650.0 117.7 %reduce-scatter.12.cloned.1.call-start = ((), (), s32[]{:S(2)}) async-start(), calls=%async_computation.8 | async-start | bytes 884736 | tf_op jit(solution)/shard_map/reduce_scatter | solution.py:177
  747.9 76.7 %reduce-scatter.14.cloned.1.call-start = ((), (), s32[]{:S(2)}) async-start(), calls=%async_computation.9 | async-start | bytes 884736 | tf_op jit(solution)/shard_map/reduce_scatter | solution.py:196
  804.8 812.9 %all-reduce.20.cloned.1.call-start = ((), (), s32[]{:S(2)}) async-start(), calls=%async_computation.13 | async-start | bytes 95551488
  822.3 1524.3 %reduce-scatter.18.cloned.1.call-start = ((), (), s32[]{:S(2)}) async-start(), calls=%async_computation.11 | async-start | bytes 33816576 | tf_op jit(solution)/shard_map/reduce_scatter | solution.py:246
  893.9 1474.0 %reduce-scatter.16.cloned.1.call-start = ((), (), s32[]{:S(2)}) async-start(), calls=%async_computation.10 | async-start | bytes 884736 | tf_op jit(solution)/shard_map/reduce_scatter | solution.py:256
  1223.3 24.0 collective-permute-start.13
  1228.7 19.9 collective-permute-start.12
  1230.0 20.3 collective-permute-start.11
  1231.3 23.5 collective-permute-start.10
  1232.7 23.5 collective-permute-start.9
  1250.3 16.5 collective-permute-start.6
  1256.2 15.9 collective-permute-start.4
  1287.4 16.9 collective-permute-start.24
  1290.1 16.7 collective-permute-start.23
  1292.2 18.7 collective-permute-start.22
  1294.4 22.8 collective-permute-start.21
  1297.7 1228.0 %all-reduce.18.cloned.1.call-start = ((), (), s32[]{:S(2)}) async-start(), calls=%async_computation.12 | async-start | bytes 4718592 | tf_op jit(solution)/shard_map/psum | solution.py:273
  1300.0 29.5 %collective-permute-start.20 = (f32[512,24]{0,1:T(8,128)S(1)}, f32[512,24]{0,1:T(8,128)S(1)}, u32[]{:S(2)}, u32[]{:S(2)}) collective-permute-start(f32[512,24]{0,1:T(8,128)S(1)} %get-tuple-element.862), channel_id=1, source_target_pairs={{0,10},{2,12},{4,14},{6,16},{8,18},{10,20},{12,22},{14,24},{16,26}... | collective-permute-start | bytes 147464
  1304.3 25.2 collective-permute-start.19
  1306.8 22.7 collective-permute-start.18
  1310.9 18.6 collective-permute-start.17
  (85 other events, 9878.1 us)
Sparse Core Ops, SparseCore 0:
  15.1 314.7 all-gather.2
  332.2 311.9 all-gather.4
  650.1 65.7 reduce-scatter.9
  748.0 19.6 reduce-scatter.11
  804.9 19.6 reduce-scatter.13
  827.4 790.1 all-reduce.19
  1620.2 726.3 reduce-scatter.17
  2349.1 18.8 reduce-scatter.15
  2373.4 152.2 all-reduce.17
where the time goes:
time: 2550 us; the launch traced here: 2540 us
  waiting for transfers between devices  1810 us (71%)
  blocking collectives  420 us (16%)
  starting transfers between devices  104 us (4%)
  matrix products  84.4 us (3%)
  local copies, waits for them, and re-layouts  70.7 us (3%)
  other arithmetic  27.9 us (1%)
    reduce_scatter x1, waiting for transfers between devices, shards(): lax.psum_scatter(d_kv_all, ('sp', 'tp'), scatter_dimension=0, tiled=True)  725 us
    unnamed x1, blocking collectives  318 us
    all_gather x1, waiting for transfers between devices, shards(): lax.all_gather(v_own, ('sp', 'tp'), axis=0, tiled=True)  310 us
    all_gather x1, waiting for transfers between devices, shards(): lax.all_gather(k_rot, ('sp', 'tp'), axis=0, tiled=True)  300 us
    unnamed x42, waiting for transfers between devices  283 us
    unnamed x33, starting transfers between devices  103 us
    psum x1, waiting for transfers between devices, shards(): lax.psum((d_w_key, d_w_value, d_norm_attn, d_norm_query, d_norm_key, d_no...  88.2 us
    psum x1, blocking collectives, shards(): lax.psum((d_w_key, d_w_value, d_norm_attn, d_norm_query, d_norm_key, d_no...  66.8 us
  transfers between devices with their start and end apart: 41, of which 10 were waited for; matrix products, arithmetic and copies ran while one was open for 17% of the time, Pallas kernels for 0%

commit v1 on v0

v1 whole, which is shorter than its diff:
```python
import jax
import jax.numpy as jnp
import numpy as np
from jax import lax
from jax.experimental import pallas as pl
from jax.experimental.pallas import tpu as pltpu
from jax.sharding import PartitionSpec as P

EPS = 1e-06
THETA = 1000000.0
BF = jnp.bfloat16
F32 = jnp.float32
MESH = pl.DeviceIdType.MESH
IN_VMEM = pl.BlockSpec(memory_space=pltpu.VMEM)
VMEM_BYTES = 58 * 1024 * 1024

TOK = 128
D = 1152
HD = 256
HEADS = 4
ROWS = 2 * TOK
HID = 1728
HID_PAD = 1792
HALF = 1408
CUT = 768
CHUNK = 256


class Place:
    def __init__(self):
        sp = lax.axis_index("sp")
        self.core = lax.rem(sp, 2)
        self.z = lax.rem(lax.div(sp, 2), 4)
        self.y = lax.div(sp, 16)
        self.x = lax.rem(lax.div(sp, 8), 2) * 2 + lax.axis_index("tp")

    def device(self, **moved):
        x, y, z, core = (moved.get(name, getattr(self, name)) for name in ("x", "y", "z", "core"))
        return (((y * 2 + lax.div(x, 2)) * 4 + z) * 2 + core, lax.rem(x, 2))

    def step(self, axis, by):
        return lax.rem(getattr(self, axis) + by, 4)

    def toward(self, axis, by):
        return self.device(**{axis: self.step(axis, by)})

    def partner(self):
        return self.device(core=1 - self.core)


class Net:
    def __init__(self, send, recv):
        self.send, self.recv, self.used, self.started = send, recv, 0, []

    def copy(self, source, target, device):
        at = self.used
        self.used += 1
        return pltpu.make_async_remote_copy(
            src_ref=source,
            dst_ref=target,
            send_sem=self.send.at[at],
            recv_sem=self.recv.at[at],
            device_id=device,
            device_id_type=MESH,
        )

    def go(self, copy):
        copy.start()
        self.started.append(copy)

    def drain(self):
        for copy in self.started:
            copy.wait_send()
        self.started = []


def greet(devices):
    barrier = pltpu.get_barrier_semaphore()
    for device in devices:
        pl.semaphore_signal(barrier, inc=1, device_id=device, device_id_type=MESH)
    pl.semaphore_wait(barrier, len(devices))


def ring(place, axis):
    return [place.toward(axis, 1), place.toward(axis, 3)]


class RingGather:
    def __init__(self, net, place, axis, view, lo, hi):
        self.net = net
        me, nxt, prev = getattr(place, axis), place.step(axis, 1), place.step(axis, 3)
        right, left = ring(place, axis)
        self.to_right = net.copy(view(me), view(me), right)
        self.to_left = net.copy(view(me), view(me), left)
        self.on_right = net.copy(lo(prev), lo(prev), right)
        self.on_left = net.copy(hi(nxt), hi(nxt), left)

    def start(self):
        self.net.go(self.to_right)
        self.net.go(self.to_left)

    def forward(self):
        self.to_right.wait_recv()
        self.net.go(self.on_right)
        self.to_left.wait_recv()
        self.net.go(self.on_left)

    def finish(self):
        self.on_right.wait_recv()
        self.on_left.wait_recv()


def by_rows(ref, act, most=16):
    *lead, rows, _ = ref.shape
    block = most
    for spot in np.ndindex(*lead):

        def one(i, carry, spot=spot):
            act(spot, pl.ds(pl.multiple_of(i * block, block), block))
            return carry

        lax.fori_loop(0, rows // block, one, 0)


def add_to(target, other):
    def act(spot, rows):
        at = (*spot, rows, slice(None))
        target[at] = (target[at].astype(F32) + other[at].astype(F32)).astype(target.dtype)

    by_rows(target, act)


def sum_to(target, others):
    def act(spot, rows):
        at = (*spot, rows, slice(None))
        total = others[0][at].astype(F32)
        for other in others[1:]:
            total = total + other[at].astype(F32)
        target[at] = total.astype(target.dtype)

    by_rows(target, act)


class RingScatter:
    def __init__(self, net, place, axis, lo, hi, room):
        self.net, self.lo, self.hi = net, lo, hi
        self.me, self.nxt, self.opp, self.prev = (place.step(axis, by) for by in range(4))
        right, left = ring(place, axis)
        self.lo1, self.lo_l, self.lo_r, self.hi1, self.hi_l, self.hi_r = room
        self.a = net.copy(lo(self.opp), self.lo1, right)
        self.b = net.copy(hi(self.opp), self.hi1, left)
        self.c_hi = net.copy(hi(self.nxt), self.hi_l, right)
        self.d_lo = net.copy(lo(self.prev), self.lo_r, left)
        self.c_lo = net.copy(self.lo1, self.lo_l, right)
        self.d_hi = net.copy(self.hi1, self.hi_r, left)

    def start_far(self):
        self.net.go(self.a)
        self.net.go(self.b)

    def start_near(self):
        self.net.go(self.c_hi)
        self.net.go(self.d_lo)

    def middle(self):
        self.a.wait_recv()
        add_to(self.lo1, self.lo(self.nxt))
        self.net.go(self.c_lo)
        self.b.wait_recv()
        add_to(self.hi1, self.hi(self.prev))
        self.net.go(self.d_hi)

    def finish(self, lo_out, hi_out):
        self.c_hi.wait_recv()
        self.d_hi.wait_recv()
        sum_to(hi_out, [self.hi(self.me), self.hi_l, self.hi_r])
        self.d_lo.wait_recv()
        self.c_lo.wait_recv()
        sum_to(lo_out, [self.lo(self.me), self.lo_l, self.lo_r])

    @staticmethod
    def room_shapes(lo_shape, hi_shape):
        return [pltpu.VMEM(lo_shape, BF)] * 3 + [pltpu.VMEM(hi_shape, BF)] * 3


def params(call_id):
    return pltpu.CompilerParams(
        collective_id=call_id, has_side_effects=True, vmem_limit_bytes=VMEM_BYTES
    )


def sems(count):
    return [pltpu.SemaphoreType.DMA((count,)), pltpu.SemaphoreType.DMA((count,))]


def weight_kernel(w_ref, other_ref, send, recv):
    place, net = Place(), Net(send, recv)
    right, left = ring(place, "x")
    quarter = w_ref.shape[0] // 4
    greet([right, left, place.partner()])
    finish = swap_weight(place, net, w_ref, other_ref, quarter)
    finish()
    net.drain()


def swap_weight(place, net, w_ref, other_ref, quarter):
    right, left = ring(place, "x")
    core = place.core

    def rows(side):
        return pl.ds(pl.multiple_of((2 * side + core) * quarter, 16), quarter)

    def cores_rows(side):
        return other_ref.at[rows(side)]

    one = net.copy(w_ref.at[rows(0)], cores_rows(0), left)
    two = net.copy(w_ref.at[rows(1)], cores_rows(1), right)
    trades = [net.copy(cores_rows(side), cores_rows(side), place.partner()) for side in (0, 1)]
    net.go(one)
    net.go(two)

    def finish():
        for first, trade in zip((one, two), trades):
            first.wait_recv()
            net.go(trade)
        for trade in trades:
            trade.wait_recv()

    return finish


def fetch_weight(w, call_id):
    return pl.pallas_call(
        weight_kernel,
        out_shape=jax.ShapeDtypeStruct(w.shape, w.dtype),
        in_specs=[IN_VMEM],
        out_specs=IN_VMEM,
        scratch_shapes=sems(4),
        compiler_params=params(call_id),
    )(w)


PARTS = (
    (0, 48, 0, ("x", "y", "z")),
    (48, 48, 768, ("z", "x", "y")),
    (96, 32, 1536, ("y", "z", "x")),
)


def part_views(place, buf, part):
    _, rows, base, (first, second, third) = part
    at1, at2, at3 = (getattr(place, axis) for axis in (first, second, third))

    def block(lead, start, size):
        return buf.at[lead, pl.ds(pl.multiple_of(base + start, 16), size)]

    return (
        (first, lambda j: block(at3, (at2 * 4 + j) * rows, rows)),
        (second, lambda j: block(at3, j * 4 * rows, 4 * rows)),
        (third, lambda j: block(j, 0, 16 * rows)),
    )


def halves(view):
    return (lambda j: view(j).at[:, pl.ds(0, HD)]), (lambda j: view(j).at[:, pl.ds(HD, HD)])


def key_tokens():
    out = np.zeros((4, 2048), np.int32)
    for skip, rows, base, axes in PARTS:
        for j in range(4):
            for r in range(16 * rows):
                spot = {axes[2]: j, axes[1]: r // (4 * rows), axes[0]: (r // rows) % 4}
                x, y, z = spot["x"], spot["y"], spot["z"]
                token = ((y * 2 + x // 2) * 4 + z) * 512 + (x % 2) * 128 + skip + r % rows
                out[j, base + r] = token
    order = np.zeros((8, CHUNK), np.int64)
    for c in range(8):
        for i in range(4):
            start = 256 * c + 64 * i if c < 6 else 1536 + 128 * i + 64 * (c - 6)
            order[c, 64 * i : 64 * i + 64] = np.arange(start, start + 64)
    return out[:, order]


KEY_TOKENS = key_tokens()


def chunk_at(place, n, by):
    lead = jnp.where(
        n < 3, place.step("z", by), jnp.where(n < 6, place.step("y", by), place.step("x", by))
    )
    first_y = jnp.where(n < 3, n, jnp.where(n < 6, lead, (n - 6) * 2))
    last_y = jnp.where(n < 3, n + 1, jnp.where(n < 6, lead, (n - 6) * 2 + 1))
    start = jnp.where(n < 6, n * 256, 1536 + 64 * (n - 6))
    stride = jnp.where(n < 6, 64, 128)
    starts = [pl.multiple_of(start + stride * i, 16) for i in range(4)]
    skip = first_y > place.y
    holds_first = (lead == 0) & ((n == 0) | (n == 3) | (n == 6))
    final = (place.x == 3) & (place.y == 3) & (place.z == 3)
    plain = (last_y < place.y) & jnp.logical_not(holds_first) & jnp.logical_not(final)
    return lead, starts, skip, plain


def read_chunk(buf, lead, starts, column):
    return jnp.concatenate(
        [buf[lead, pl.ds(start, 64), pl.ds(column, HD)] for start in starts], axis=0
    )


def contract(left, right, left_dim, right_dim):
    return lax.dot_general(
        left, right, (((left_dim,), (right_dim,)), ((), ())), preferred_element_type=F32
    )


def forward_kernel(
    kv_ref,
    q_ref,
    w_ref,
    key_ref,
    last_ref,
    first_ref,
    buf,
    q_all,
    w_other,
    o_out,
    inv_out,
    o_sum,
    l_sum,
    o_got,
    l_got,
    send,
    recv,
):
    place, net = Place(), Net(send, recv)
    core = place.core
    partner = place.partner()
    greet(ring(place, "x") + ring(place, "y") + ring(place, "z") + [partner])
    mine = pl.ds(pl.multiple_of(core * TOK, TOK), TOK)
    theirs = pl.ds(pl.multiple_of((1 - core) * TOK, TOK), TOK)
    q_all[:, mine] = q_ref[...]
    stages = []
    for part in PARTS:
        skip, rows, _, _ = part
        views = part_views(place, buf, part)
        axis, view = views[0]
        own = view(getattr(place, axis))
        own[...] = kv_ref[pl.ds(skip, rows)]
        stages.append([RingGather(net, place, axis, view, *halves(view)) for axis, view in views])
    for rings in stages:
        rings[0].start()
    swap_q = net.copy(q_all.at[:, mine], q_all.at[:, mine], partner)
    net.go(swap_q)
    for h in range(HEADS):
        o_sum[h] = jnp.zeros((ROWS, HD), F32)
        l_sum[h] = jnp.zeros((ROWS, 128), F32)
    for level in (0, 1):
        for rings in stages:
            rings[level].forward()
        for rings in stages:
            rings[level].finish()
            rings[level + 1].start()
    finish_w = swap_weight(place, net, w_ref, w_other, w_ref.shape[0] // 4)
    swap_q.wait_recv()

    def attend(n, by):
        lead, starts, skip, plain = chunk_at(place, n, by)

        def run(masked):
            keys = read_chunk(buf, lead, starts, 0)
            values = read_chunk(buf, lead, starts, HD)
            if masked:
                token = key_ref[lead, pl.ds(n, 1)]
                allowed = (token <= last_ref[...]) & (token >= first_ref[...])
            for h in range(HEADS):
                weights = jnp.exp(contract(q_all[h], keys, 1, 1))
                if masked:
                    weights = jnp.where(allowed, weights, 0.0)
                l_sum[h] += weights[:, :128] + weights[:, 128:]
                o_sum[h] += jnp.dot(weights.astype(BF), values, preferred_element_type=F32)

        @pl.when(plain)
        def _():
            run(False)

        @pl.when(jnp.logical_not(plain) & jnp.logical_not(skip))
        def _():
            run(True)

    def visit(by):
        lax.fori_loop(0, 8, lambda n, c: (attend(n, by), c)[1], 0)

    visit(0)
    for rings in stages:
        rings[2].forward()
    finish_w()
    lax.fori_loop(0, 16, lambda n, c: (attend(lax.rem(n, 8), 1 + 2 * lax.div(n, 8)), c)[1], 0)
    for rings in stages:
        rings[2].finish()
    visit(2)
    swap_o = net.copy(o_sum.at[:, theirs], o_got, partner)
    swap_l = net.copy(l_sum.at[:, theirs], l_got, partner)
    net.go(swap_l)
    net.go(swap_o)
    swap_l.wait_recv()
    swap_o.wait_recv()
    for h in range(HEADS):
        total = jnp.sum(l_sum[h, mine] + l_got[h], axis=1, keepdims=True)
        inverse = 1.0 / total
        o_out[h] = (o_sum[h, mine] + o_got[h]) * inverse
        inv_out[h] = jnp.broadcast_to(inverse, (TOK, 128))
    net.drain()


def attention_forward(kv, q, w_out, key_rows, last, first, call_id):
    shape = jax.ShapeDtypeStruct
    return pl.pallas_call(
        forward_kernel,
        out_shape=(
            shape((4, 2048, 2 * HD), BF),
            shape((HEADS, ROWS, HD), BF),
            shape(w_out.shape, BF),
            shape((HEADS, TOK, HD), F32),
            shape((HEADS, TOK, 128), F32),
        ),
        in_specs=[IN_VMEM] * 6,
        out_specs=[IN_VMEM] * 5,
        scratch_shapes=[
            pltpu.VMEM((HEADS, ROWS, HD), F32),
            pltpu.VMEM((HEADS, ROWS, 128), F32),
            pltpu.VMEM((HEADS, TOK, HD), F32),
            pltpu.VMEM((HEADS, TOK, 128), F32),
            *sems(48),
        ],
        compiler_params=params(call_id),
    )(kv, q, w_out, key_rows, last, first)


def backward_kernel(
    buf,
    q_all,
    do_ref,
    delta_ref,
    key_ref,
    last_ref,
    first_ref,
    dq_out,
    dkv_out,
    do_all,
    delta_all,
    grads,
    dq_sum,
    dq_got,
    *rest,
):
    *rooms, send, recv = rest
    place, net = Place(), Net(send, recv)
    core, partner = place.core, place.partner()
    greet(ring(place, "x") + ring(place, "y") + ring(place, "z") + [partner])
    mine = pl.ds(pl.multiple_of(core * TOK, TOK), TOK)
    theirs = pl.ds(pl.multiple_of((1 - core) * TOK, TOK), TOK)
    do_all[:, mine] = do_ref[...]
    delta_all[core] = delta_ref[...]
    swap_do = net.copy(do_all.at[:, mine], do_all.at[:, mine], partner)
    swap_delta = net.copy(delta_all.at[core], delta_all.at[core], partner)
    net.go(swap_do)
    net.go(swap_delta)
    for h in range(HEADS):
        dq_sum[h] = jnp.zeros((HD, ROWS), F32)
    stages = []
    for i, part in enumerate(PARTS):
        views = part_views(place, grads, part)
        rings = []
        for level, (axis, view) in enumerate(views):
            at = 6 * (3 * i + level)
            rings.append(RingScatter(net, place, axis, *halves(view), rooms[at : at + 6]))
        stages.append((rings, views))
    swap_do.wait_recv()
    swap_delta.wait_recv()

    def differ(n, by):
        lead, starts, skip, plain = chunk_at(place, n, by)

        def store(column, value):
            value = value.astype(BF)
            for i, start in enumerate(starts):
                grads[lead, pl.ds(start, 64), pl.ds(column, HD)] = value[64 * i : 64 * i + 64]

        def run(masked):
            keys = read_chunk(buf, lead, starts, 0)
            values = read_chunk(buf, lead, starts, HD)
            if masked:
                token = key_ref[lead, n]
                allowed = (token <= last_ref[...]) & (token >= first_ref[...])
            d_keys = d_values = None
            for h in range(HEADS):
                probs = jnp.exp(contract(keys, q_all[h], 1, 1))
                if masked:
                    probs = jnp.where(allowed, probs, 0.0)
                delta = jnp.concatenate(
                    [delta_all[0, pl.ds(h, 1)], delta_all[1, pl.ds(h, 1)]], axis=1
                )
                d_scores = (probs * (contract(values, do_all[h], 1, 1) - delta)).astype(BF)
                value_term = jnp.dot(probs.astype(BF), do_all[h], preferred_element_type=F32)
                key_term = jnp.dot(d_scores, q_all[h], preferred_element_type=F32)
                d_values = value_term if h == 0 else d_values + value_term
                d_keys = key_term if h == 0 else d_keys + key_term
                dq_sum[h] += contract(keys, d_scores, 0, 0)
            store(0, d_keys)
            store(HD, d_values)

        @pl.when(plain)
        def _():
            run(False)

        @pl.when(jnp.logical_not(plain) & jnp.logical_not(skip))
        def _():
            run(True)

        @pl.when(skip)
        def _():
            for start in starts:
                grads[lead, pl.ds(start, 64)] = jnp.zeros((64, 2 * HD), BF)

    def visit(by):
        lax.fori_loop(0, 8, lambda n, c: (differ(n, by), c)[1], 0)

    visit(2)
    for rings, _ in stages:
        rings[2].start_far()
    lax.fori_loop(0, 16, lambda n, c: (differ(lax.rem(n, 8), 1 + 2 * lax.div(n, 8)), c)[1], 0)
    for rings, _ in stages:
        rings[2].start_near()
    for rings, _ in stages:
        rings[2].middle()
    visit(0)
    swap_dq = net.copy(dq_sum.at[:, :, theirs], dq_got, partner)
    net.go(swap_dq)
    for level in (2, 1, 0):
        for (rings, views), part in zip(stages, PARTS):
            axis, view = views[level]
            lo, hi = halves(view)
            me = getattr(place, axis)
            skip, rows, _, _ = part
            if level:
                rings[level].finish(lo(me), hi(me))
                rings[level - 1].start_far()
                rings[level - 1].start_near()
            else:
                out = dkv_out.at[pl.ds(skip, rows)]
                rings[level].finish(out.at[:, pl.ds(0, HD)], out.at[:, pl.ds(HD, HD)])
        if level:
            for rings, _ in stages:
                rings[level - 1].middle()
    swap_dq.wait_recv()
    for h in range(HEADS):
        dq_out[h] = dq_sum[h, :, mine] + dq_got[h]
    net.drain()


def attention_backward(kv_all, q_all, d_heads, delta, key_columns, last, first, call_id):
    shape = jax.ShapeDtypeStruct
    rooms = []
    for _, rows, _, _ in PARTS:
        for blocks in (1, 4, 16):
            rooms += RingScatter.room_shapes((blocks * rows, HD), (blocks * rows, HD))
    return pl.pallas_call(
        backward_kernel,
        out_shape=(shape((HEADS, HD, TOK), F32), shape((TOK, 2 * HD), F32)),
        in_specs=[IN_VMEM] * 7,
        out_specs=[IN_VMEM] * 2,
        scratch_shapes=[
            pltpu.VMEM((HEADS, ROWS, HD), BF),
            pltpu.VMEM((2, 8, TOK), F32),
            pltpu.VMEM((4, 2048, 2 * HD), BF),
            pltpu.VMEM((HEADS, HD, ROWS), F32),
            pltpu.VMEM((HEADS, HD, TOK), F32),
            *rooms,
            *sems(64),
        ],
        compiler_params=params(call_id),
    )(kv_all, q_all, d_heads, delta, key_columns, last, first)


def x_gather_kernel(rows_ref, out_ref, send, recv):
    place, net = Place(), Net(send, recv)
    greet(ring(place, "x"))
    out_ref[place.x] = rows_ref[...]
    line = RingGather(
        net,
        place,
        "x",
        lambda j: out_ref.at[j],
        lambda j: out_ref.at[j, pl.ds(0, TOK // 2)],
        lambda j: out_ref.at[j, pl.ds(TOK // 2, TOK // 2)],
    )
    line.start()
    line.forward()
    line.finish()
    net.drain()


def x_gather(rows, call_id):
    return pl.pallas_call(
        x_gather_kernel,
        out_shape=jax.ShapeDtypeStruct((4, TOK, D), BF),
        in_specs=[IN_VMEM],
        out_specs=IN_VMEM,
        scratch_shapes=sems(4),
        compiler_params=params(call_id),
    )(rows)


def x_scatter_kernel(terms_ref, out_ref, *rest):
    *room, send, recv = rest
    place, net = Place(), Net(send, recv)
    greet(ring(place, "x"))
    half = TOK // 2
    line = RingScatter(
        net,
        place,
        "x",
        lambda j: terms_ref.at[j, pl.ds(0, half)],
        lambda j: terms_ref.at[j, pl.ds(half, half)],
        room,
    )
    line.start_far()
    line.start_near()
    line.middle()
    line.finish(out_ref.at[pl.ds(0, half)], out_ref.at[pl.ds(half, half)])
    net.drain()


def x_scatter(terms, call_id):
    half = (TOK // 2, D)
    return pl.pallas_call(
        x_scatter_kernel,
        out_shape=jax.ShapeDtypeStruct((TOK, D), F32),
        in_specs=[IN_VMEM],
        out_specs=IN_VMEM,
        scratch_shapes=[*RingScatter.room_shapes(half, half), *sems(6)],
        compiler_params=params(call_id),
    )(terms)


def ffn_grads_kernel(terms_ref, out_ref, got, snd, rcv, *rest):
    *rooms, send, recv, send2, recv2, here = rest
    place, net = Place(), Net(send, recv)
    core, partner = place.core, place.partner()
    x_hi, x_lo = lax.div(place.x, 2), lax.rem(place.x, 2)
    r, c = lax.div(place.z, 2), lax.rem(place.z, 2)
    friends = []
    for k in range(1, 16):
        spot = lax.rem(x_hi * 8 + place.z * 2 + core + k, 16)
        friends.append(
            place.device(
                x=lax.div(spot, 8) * 2 + x_lo, z=lax.rem(lax.div(spot, 2), 4), core=lax.rem(spot, 2)
            )
        )
    greet(friends + ring(place, "y"))
    swaps = [net.copy(terms_ref.at[1 - core, y], got.at[y], partner) for y in range(4)]
    for swap in swaps:
        net.go(swap)

    def left(lead):
        return lead.at[..., pl.ds(0, CUT)]

    def right(lead):
        return lead.at[..., pl.ds(CUT, HALF - CUT)]

    y_first = RingScatter(
        net, place, "y", lambda j: left(got.at[j, 0]), lambda j: left(got.at[j, 1]), rooms[0:6]
    )

    def z_spot(j):
        return got.at[:, lax.div(j, 2), lax.rem(j, 2)]

    z_first = RingScatter(
        net,
        place,
        "z",
        lambda j: right(z_spot(j).at[pl.ds(0, 2)]),
        lambda j: right(z_spot(j).at[pl.ds(2, 2)]),
        rooms[6:12],
    )

    def then_z(j):
        return got.at[place.y, lax.div(j, 2), lax.rem(j, 2)]

    z_second = RingScatter(
        net,
        place,
        "z",
        lambda j: then_z(j).at[:, pl.ds(0, 384)],
        lambda j: then_z(j).at[:, pl.ds(384, 384)],
        rooms[12:18],
    )

    def then_y(j):
        return got.at[j, r, c]

    y_second = RingScatter(
        net,
        place,
        "y",
        lambda j: then_y(j).at[:, pl.ds(768, 384)],
        lambda j: then_y(j).at[:, pl.ds(1152, 256)],
        rooms[18:24],
    )
    for y, swap in enumerate(swaps):
        swap.wait_recv()
        add_to(got.at[y], terms_ref.at[core, y])
    first, second = (y_first, z_first), (z_second, y_second)
    for line in first:
        line.start_far()
        line.start_near()
    for line in first:
        line.middle()
    me = place.y
    y_first.finish(left(got.at[me, 0]), left(got.at[me, 1]))
    z_second.start_far()
    z_second.start_near()
    own = z_spot(place.z)
    z_first.finish(right(own.at[pl.ds(0, 2)]), right(own.at[pl.ds(2, 2)]))
    y_second.start_far()
    y_second.start_near()
    for line in second:
        line.middle()
    done = got.at[place.y, r, c]
    z_second.finish(done.at[:, pl.ds(0, 384)], done.at[:, pl.ds(384, 384)])
    y_second.finish(done.at[:, pl.ds(768, 384)], done.at[:, pl.ds(1152, 256)])
    total = done[...].astype(F32)
    rest_rows = jnp.zeros((14, HALF), F32)
    for k in range(8):
        snd[k] = jnp.concatenate([total[18 * k : 18 * k + 18], rest_rows], axis=0).astype(BF)
    slot = x_hi * 4 + core * 2 + c
    own_spot = place.z * 2 + core
    stays = r == x_hi
    for k in range(8):
        copy = pltpu.make_async_remote_copy(
            src_ref=snd.at[k],
            dst_ref=rcv.at[slot],
            send_sem=send2.at[k],
            recv_sem=recv2.at[slot],
            device_id=place.device(x=r * 2 + x_lo, z=k // 2, core=k % 2),
            device_id_type=MESH,
        )
        is_here = stays & (own_spot == k)

        @pl.when(jnp.logical_not(is_here))
        def _(copy=copy):
            copy.start()

        @pl.when(is_here)
        def _(k=k):
            keep = pltpu.make_async_copy(snd.at[k], rcv.at[slot], here.at[0])
            keep.start()
            keep.wait()

    for m in range(8):
        arrival = pltpu.make_async_remote_copy(
            src_ref=snd.at[m],
            dst_ref=rcv.at[m],
            send_sem=send2.at[m],
            recv_sem=recv2.at[m],
            device_id=partner,
            device_id_type=MESH,
        )

        @pl.when(jnp.logical_not(stays & (slot == m)))
        def _(arrival=arrival):
            arrival.wait_recv()

        @pl.when(jnp.logical_not(stays & (own_spot == m)))
        def _(arrival=arrival):
            arrival.wait_send()

    out_ref[...] = rcv[...]
    net.drain()


def ffn_grads(terms, call_id):
    rooms = [
        *RingScatter.room_shapes((2, 144, CUT), (2, 144, CUT)),
        *RingScatter.room_shapes((2, 144, HALF - CUT), (2, 144, HALF - CUT)),
        *RingScatter.room_shapes((144, 384), (144, 384)),
        *RingScatter.room_shapes((144, 384), (144, 256)),
    ]
    return pl.pallas_call(
        ffn_grads_kernel,
        out_shape=jax.ShapeDtypeStruct((8, 32, HALF), BF),
        in_specs=[IN_VMEM],
        out_specs=IN_VMEM,
        scratch_shapes=[
            pltpu.VMEM((4, 2, 2, 144, HALF), BF),
            pltpu.VMEM((8, 32, HALF), BF),
            pltpu.VMEM((8, 32, HALF), BF),
            *rooms,
            *sems(32),
            *sems(8),
            pltpu.SemaphoreType.DMA((1,)),
        ],
        compiler_params=params(call_id),
    )(terms)


LANES = 384
ORDERS = (("x", "y", "z"), ("y", "z", "x"), ("z", "x", "y"))


def small_grads_kernel(terms_ref, gains_ref, out_ref, gains_out, got, sums, gain_got, *rest):
    *rooms, send, recv = rest
    place, net = Place(), Net(send, recv)
    core, partner = place.core, place.partner()
    greet(ring(place, "x") + ring(place, "y") + ring(place, "z") + [partner])
    swap = net.copy(terms_ref.at[1 - core], got, partner)
    gain_got[0, core] = gains_ref[...]
    gain_swap = net.copy(gain_got.at[0, core], gain_got.at[0, core], partner)
    net.go(gain_swap)
    net.go(swap)

    def gain_ring(level, axis):
        return RingGather(
            net,
            place,
            axis,
            lambda j: gain_got.at[level, j],
            lambda j: gain_got.at[level, j, :, pl.ds(0, 512)],
            lambda j: gain_got.at[level, j, :, pl.ds(512, 640)],
        )

    gain_lines = [gain_ring(1, "x"), gain_ring(2, "y"), gain_ring(3, "z")]
    gain_swap.wait_recv()
    gain_got[1, place.x] = gain_got[0, 0] + gain_got[0, 1]
    gain_lines[0].start()

    rows = out_ref.at[core]
    scatters, gathers = [], []
    for p, (first, second, third) in enumerate(ORDERS):
        lanes = pl.ds(LANES * p, LANES)
        at1, at2, at3 = (getattr(place, axis) for axis in (first, second, third))

        def views(ref, lanes=lanes, at1=at1):
            def piece(start, size):
                return ref.at[pl.ds(pl.multiple_of(start, 16), size), lanes]

            return (
                lambda j: piece(320 * j, 320),
                lambda j: piece(320 * j, 160),
                lambda j: piece(320 * j + 160, 160),
                lambda j: piece(320 * at1 + 80 * j, 80),
                lambda j: piece(320 * at1 + 80 * j, 48),
                lambda j: piece(320 * at1 + 80 * j + 48, 32),
            )

        _, lo1, hi1, term2, lo2, hi2 = views(got)
        room = rooms[12 * p : 12 * p + 12]
        scatters.append(
            (
                (RingScatter(net, place, first, lo1, hi1, room[:6]), lo1, hi1, at1),
                (RingScatter(net, place, second, lo2, hi2, room[6:]), lo2, hi2, at2),
            )
        )
        spot = sums.at[p]
        last = RingGather(
            net,
            place,
            third,
            lambda j, spot=spot: spot.at[j],
            lambda j, spot=spot: spot.at[j, pl.ds(0, 48)],
            lambda j, spot=spot: spot.at[j, pl.ds(48, 32)],
        )
        whole1, whole_lo1, whole_hi1, whole2, whole_lo2, whole_hi2 = views(rows)
        gathers.append(
            (
                last,
                RingGather(net, place, second, whole2, whole_lo2, whole_hi2),
                RingGather(net, place, first, whole1, whole_lo1, whole_hi1),
                term2(at2),
                whole2(at2),
                at3,
            )
        )
    swap.wait_recv()
    add_to(got, terms_ref.at[core])
    for level in (0, 1):
        for pair in scatters:
            pair[level][0].start_far()
            pair[level][0].start_near()
        for pair in scatters:
            pair[level][0].middle()
        gain_lines[level].forward()
        for pair in scatters:
            line, lo, hi, at = pair[level]
            line.finish(lo(at), hi(at))
        gain_lines[level].finish()
        nxt = place.y if level == 0 else place.z
        gain_got[level + 2, nxt] = (gain_got[level + 1, 0] + gain_got[level + 1, 1]) + (
            gain_got[level + 1, 2] + gain_got[level + 1, 3]
        )
        gain_lines[level + 1].start()
    for p, (last, _, _, term, _, at3) in enumerate(gathers):
        sums[p, at3] = term[...]
        last.start()
    for last, *_ in gathers:
        last.forward()
    gain_lines[2].forward()
    for p, (last, second, _, _, own, _) in enumerate(gathers):
        last.finish()
        sum_to(own, [sums.at[p, j] for j in range(4)])
        second.start()
    for _, second, *_ in gathers:
        second.forward()
    for _, second, first, *_ in gathers:
        second.finish()
        first.start()
    for _, _, first, *_ in gathers:
        first.forward()
    gain_lines[2].finish()
    gains_out[...] = (gain_got[3, 0] + gain_got[3, 1]) + (gain_got[3, 2] + gain_got[3, 3])
    for _, _, first, *_ in gathers:
        first.finish()
    final = net.copy(rows, rows, partner)
    net.go(final)
    final.wait_recv()
    net.drain()


def small_grads(terms, gains, call_id):
    shape = jax.ShapeDtypeStruct
    rooms = []
    for _ in ORDERS:
        rooms += RingScatter.room_shapes((160, LANES), (160, LANES))
        rooms += RingScatter.room_shapes((48, LANES), (32, LANES))
    return pl.pallas_call(
        small_grads_kernel,
        out_shape=(shape(terms.shape, BF), shape(gains.shape, F32)),
        in_specs=[IN_VMEM] * 2,
        out_specs=[IN_VMEM] * 2,
        scratch_shapes=[
            pltpu.VMEM((1280, D), BF),
            pltpu.VMEM((3, 4, 80, LANES), BF),
            pltpu.VMEM((4, 4, 8, D), F32),
            *rooms,
            *sems(96),
        ],
        compiler_params=params(call_id),
    )(terms, gains)


def rms_scale(tensor, scaling):
    return tensor * lax.rsqrt(jnp.mean(tensor * tensor, axis=-1, keepdims=True) + EPS) * scaling


def angles(token_pos):
    middle = HD // 2
    frequency = THETA ** (-2.0 * jnp.arange(middle, dtype=F32) / HD)
    turned = token_pos.astype(F32)[:, None] * frequency[None, :]
    return (jnp.cos(turned), jnp.sin(turned))


def rotary(tensor, cosine, sine):
    middle = tensor.shape[-1] // 2
    lower_half = tensor[..., :middle]
    upper_half = tensor[..., middle:]
    return jnp.concatenate(
        [lower_half * cosine - upper_half * sine, upper_half * cosine + lower_half * sine], axis=-1
    )


def glu_piece(gate_in, up_in):
    return jax.nn.gelu(gate_in, approximate=True) * up_in


def shards(
    layer_input,
    segment_ids,
    positions,
    w_query,
    w_key,
    w_value,
    w_out,
    w_gate,
    w_up,
    w_down,
    norm_attn,
    norm_query,
    norm_key,
    norm_post,
    norm_ffn,
    norm_out,
    cotangent,
):
    sp, tp = lax.axis_index("sp"), lax.axis_index("tp")
    core, x_hi = lax.rem(sp, 2), lax.rem(lax.div(sp, 8), 2)
    own_start = (sp * 2 + tp) * TOK
    chip_start = lax.div(sp, 2) * 512 + tp * TOK

    firsts = jnp.sum(
        (segment_ids[None, :] < jnp.arange(4, dtype=jnp.int32)[:, None]).astype(jnp.int32), axis=1
    )
    row_token = chip_start + jnp.concatenate([jnp.arange(TOK), 256 + jnp.arange(TOK)]).astype(
        jnp.int32
    )
    row_segs = jnp.concatenate(
        [
            lax.dynamic_slice_in_dim(segment_ids, chip_start, TOK),
            lax.dynamic_slice_in_dim(segment_ids, chip_start + 256, TOK),
        ]
    )
    row_first = jnp.zeros_like(row_token)
    for k in range(4):
        row_first = jnp.where(row_segs == k, firsts[k], row_first)
    key_rows = jnp.asarray(KEY_TOKENS) + core * 256
    cosine, sine = angles(lax.dynamic_slice_in_dim(positions, own_start, TOK))

    def query_piece(pre_rot, scaling):
        return rotary(rms_scale(pre_rot, scaling), cosine[:, None, :], sine[:, None, :])

    def key_piece(pre_rot, scaling):
        return rotary(rms_scale(pre_rot, scaling), cosine, sine)

    wq_other = fetch_weight(w_query, 1)
    wq_both = jnp.concatenate([w_query, wq_other], axis=1)
    input_f = layer_input.astype(F32)
    h_attn = rms_scale(input_f, norm_attn).astype(BF)
    q_pre = jnp.dot(h_attn, wq_both, preferred_element_type=F32).reshape(TOK, HEADS, HD)
    q_rot = query_piece(q_pre, norm_query).astype(BF)
    q_scaled = (q_rot * BF(HD**-0.5)).transpose(1, 0, 2)
    k_pre = jnp.dot(h_attn, w_key, preferred_element_type=F32)
    k_rot = key_piece(k_pre, norm_key).astype(BF)
    v_own = jnp.dot(h_attn, w_value, preferred_element_type=F32).astype(BF)
    kv_own = jnp.concatenate([k_rot, v_own], axis=1)
    kv_all, q_all, wo_other, o_heads, inverse = attention_forward(
        kv_own, q_scaled, w_out, key_rows, row_token[:, None], row_first[:, None], 2
    )
    wo_both = jnp.concatenate([w_out, wo_other], axis=0)
    o_cat = o_heads.transpose(1, 0, 2).astype(BF).reshape(TOK, HEADS * HD)
    attn_out = jnp.dot(o_cat, wo_both, preferred_element_type=F32)
    mid = input_f + rms_scale(attn_out, norm_post)
    h_ffn = rms_scale(mid, norm_ffn).astype(BF)

    def units(weight, dim):
        part = lax.dynamic_slice_in_dim(weight, x_hi * HID, HID, axis=dim)
        pads = [(0, 0), (0, 0)]
        pads[dim] = (0, HID_PAD - HID)
        return jnp.pad(part, pads)

    gate_w, up_w, down_w = units(w_gate, 1), units(w_up, 1), units(w_down, 0)
    h_line = x_gather(h_ffn, 3).reshape(4 * TOK, D)
    gate = jnp.dot(h_line, gate_w, preferred_element_type=F32)
    upper = jnp.dot(h_line, up_w, preferred_element_type=F32)
    act = glu_piece(gate, upper).astype(BF)
    ffn_term = jnp.dot(act, down_w, preferred_element_type=F32).astype(BF)
    ffn_out = x_scatter(ffn_term.reshape(4, TOK, D), 4)
    layer_output = (mid + rms_scale(ffn_out, norm_out)).astype(BF)
    grad_out = cotangent.astype(F32)
    _, pull_out = jax.vjp(rms_scale, ffn_out, norm_out)
    d_ffn_out, d_norm_out = pull_out(grad_out)
    d_ffn_line = x_gather(d_ffn_out.astype(BF), 5).reshape(4 * TOK, D)
    d_act = contract(d_ffn_line, down_w, 1, 1)
    _, pull_glu = jax.vjp(glu_piece, gate, upper)
    d_gate, d_upper = pull_glu(d_act)
    d_gate = d_gate.astype(BF)
    d_upper = d_upper.astype(BF)
    d_h_term = (contract(d_gate, gate_w, 1, 1) + contract(d_upper, up_w, 1, 1)).astype(BF)
    d_h_ffn = x_scatter(d_h_term.reshape(4, TOK, D), 6)
    d_w_gate = contract(h_line, d_gate, 0, 0).astype(BF)
    d_w_up = contract(h_line, d_upper, 0, 0).astype(BF)
    d_w_down = contract(d_ffn_line, act, 0, 0).astype(BF)
    wide = jnp.concatenate(
        [
            d_w_gate.reshape(D, 2, 896),
            d_w_up.reshape(D, 2, 896),
            d_w_down.reshape(D, 2, 896),
            jnp.zeros((D, 2, 128), BF),
        ],
        axis=2,
    )
    terms = wide.reshape(4, 2, 144, 2, 2, HALF).transpose(3, 0, 1, 4, 2, 5)
    ffn_done = ffn_grads(terms, 7)
    ffn_done = (
        ffn_done.reshape(2, 2, 2, 32, HALF)[:, :, :, :18]
        .transpose(3, 0, 1, 2, 4)
        .reshape(18, 2, 2, 2 * HALF)
        .astype(F32)
    )

    def home(which):
        part = ffn_done[..., 896 * which : 896 * (which + 1)].reshape(18, 2, HID_PAD)
        return part[:, :, :HID].reshape(18, 2 * HID)

    _, pull_ffn = jax.vjp(rms_scale, mid, norm_ffn)
    d_mid_norm, d_norm_ffn = pull_ffn(d_h_ffn)
    d_mid = grad_out + d_mid_norm
    _, pull_post = jax.vjp(rms_scale, attn_out, norm_post)
    d_attn_out, d_norm_post = pull_post(d_mid)
    d_attn = d_attn_out.astype(BF)
    d_o = contract(d_attn, wo_both, 1, 1).astype(BF).reshape(TOK, HEADS, HD).transpose(1, 0, 2)
    inv_rows = inverse[..., :1]
    d_o_f = d_o.astype(F32)
    delta = jnp.sum(d_o_f * o_heads, axis=2) * inverse[..., 0]
    delta = jnp.concatenate([delta, jnp.zeros((4, TOK), F32)], axis=0)
    dq_turned, d_kv = attention_backward(
        kv_all,
        q_all,
        (d_o_f * inv_rows).astype(BF),
        delta,
        key_rows.reshape(4, 8, CHUNK, 1),
        row_token[None, :],
        row_first[None, :],
        8,
    )
    d_q_rot = (dq_turned.transpose(2, 0, 1) * HD**-0.5).astype(BF).astype(F32)
    d_kv = d_kv.astype(BF)
    _, pull_key = jax.vjp(key_piece, k_pre, norm_key)
    d_k_pre, d_norm_key = pull_key(d_kv[:, :HD].astype(F32))
    d_k_pre = d_k_pre.astype(BF)
    d_value = d_kv[:, HD:]
    _, pull_query = jax.vjp(query_piece, q_pre, norm_query)
    d_q_pre, d_norm_query = pull_query(d_q_rot)
    d_q_pre = d_q_pre.reshape(TOK, HEADS * HD).astype(BF)
    d_h_attn = (
        contract(d_q_pre, wq_both, 1, 1)
        + contract(d_k_pre, w_key, 1, 1)
        + contract(d_value, w_value, 1, 1)
    )
    _, pull_attn = jax.vjp(rms_scale, input_f, norm_attn)
    d_input_norm, d_norm_attn = pull_attn(d_h_attn)
    d_input = (d_mid + d_input_norm).astype(BF)

    def in_order(both):
        return jnp.where(tp == 0, both, jnp.roll(both, 2 * HD, axis=1))

    small = jnp.concatenate(
        [
            contract(in_order(d_q_pre), h_attn, 0, 0),
            contract(d_k_pre, h_attn, 0, 0),
            contract(in_order(o_cat), d_attn, 0, 0),
            contract(d_value, h_attn, 0, 0),
        ],
        axis=0,
    ).astype(BF)
    gains = jnp.stack(
        [
            d_norm_attn,
            d_norm_post,
            d_norm_ffn,
            d_norm_out,
            jnp.concatenate([d_norm_query, d_norm_key, jnp.zeros((D - 2 * HD,), F32)]),
            *([jnp.zeros((D,), F32)] * 3),
        ]
    )
    small, gains = small_grads(small.reshape(2, 1280, D), gains, 9)

    def cut(matrix):
        return lax.dynamic_slice(matrix, (tp * 512, sp * 18), (512, 18)).astype(F32)

    return (
        layer_output,
        d_input,
        cut(small[0, :1024]).T,
        small[0, 1024:].astype(F32).T,
        small[1, 1024:].astype(F32).T,
        cut(small[1, :1024]),
        home(0),
        home(1),
        home(2).T,
        gains[0],
        gains[4, :HD],
        gains[4, HD : 2 * HD],
        gains[1],
        gains[2],
        gains[3],
    )


def solution(mesh):
    rows = P(("sp", "tp"), None)
    in_specs = (
        rows,
        P(),
        P(),
        P(None, "tp"),
        P(),
        P(),
        P("tp", None),
        P(None, "tp"),
        P(None, "tp"),
        P("tp", None),
        P(),
        P(),
        P(),
        P(),
        P(),
        P(),
        rows,
    )
    out_specs = (
        rows,
        rows,
        P("sp", "tp"),
        P(),
        P(),
        P("tp", "sp"),
        P("sp", "tp"),
        P("sp", "tp"),
        P("tp", "sp"),
        P(),
        P(),
        P(),
        P(),
        P(),
        P(),
    )
    return jax.shard_map(shards, mesh=mesh, in_specs=in_specs, out_specs=out_specs, check_vma=False)
```

time: 2550 us -> 543 us (0.21)
  the two profiles are of different devices: /device:TPU:1 before, /device:TPU:97 now
where the time goes in v1:
time: 543 us; the launch traced here: 536 us
  Pallas kernels  369 us (68%)
  local copies, waits for them, and re-layouts  77.2 us (14%)
  matrix products  45.9 us (8%)
  other arithmetic  41.2 us (8%)
    pallas_call x1, Pallas kernels, attention_backward(): pl.pallas_call(backward_kernel, out_shape=(shape((HEADS, HD, TOK), F32),...  91.4 us
    pallas_call x1, Pallas kernels, ffn_grads(): pl.pallas_call(ffn_grads_kernel, out_shape=jax.ShapeDtypeStruct((8, 32, H...  81.1 us
    pallas_call x1, Pallas kernels, small_grads(): pl.pallas_call(small_grads_kernel, out_shape=(shape(terms.shape, BF), sha...  69 us
    pallas_call x1, Pallas kernels, attention_forward(): pl.pallas_call(forward_kernel, out_shape=(shape((4, 2048, 2 * HD), BF), s...  57 us
    reshape x2, local copies, waits for them, and re-layouts, shards(): terms = wide.reshape(4, 2, 144, 2, 2, HALF).transpose(3, 0, 1, 4, 2, 5)  30.8 us
    pallas_call x2, Pallas kernels, x_gather(): pl.pallas_call(x_gather_kernel, out_shape=jax.ShapeDtypeStruct((4, TOK, D...  29.9 us
    dot_general x14, matrix products, contract(): lax.dot_general(left, right, (((left_dim,), (right_dim,)), ((), ())), pre...  28.8 us
    pallas_call x2, Pallas kernels, x_scatter(): pl.pallas_call(x_scatter_kernel, out_shape=jax.ShapeDtypeStruct((TOK, D),...  26.3 us

profile of v1, /device:TPU:97, one launch (start us, length us, event | category | flops | bytes accessed | tf_op | source)
XLA Modules:
  0.0 536.0 jit_solution(1766868811671093878)
XLA Ops:
  8.6 14.6 %shard_map.289 = bf16[1152,512]{1,0:T(8,128)(2,1)} custom-call(bf16[1152,512]{1,0:T(8,128)(2,1)} %w_ref.2), custom_call_target="tpu_custom_call" | custom-call | tf_op jit(solution)/shard_map/pallas_call | solution.py:233
  34.1 57.0 %shard_map.290 = (bf16[4,2048,512]{2,1,0:T(8,128)(2,1)}, bf16[4,256,256]{2,1,0:T(8,128)(2,1)}, bf16[512,1152]{1,0:T(8,128)(2,1)}, f32[4,128,256]{2,1,0:T(8,128)}, f32[4,128,128]{2,1,0:T(8,128)}) custom-call(bf16[128,512]{1,0:T(8,128)(2,1)} %pad_maximum_fusion.4.kv_ref, bf16[4,128,256]{2,1,0:T(8,128)(2,1)} %copy.131.q_ref, bf16[512,1152]{1,0:T(8,128)(2,1)} %w_ref.3, ...), custom_call_target="tpu_custom_call" | custom-call | tf_op jit(solution)/shard_map/pallas_call | solution.py:417
  98.7 16.3 %shard_map.291 = bf16[4,128,1152]{2,1,0:T(8,128)(2,1)} custom-call(bf16[128,1152]{1,0:T(8,128)(2,1)} %multiply_convert_fusion.2.rows_ref), custom_call_target="tpu_custom_call" | custom-call | tf_op jit(solution)/shard_map/pallas_call | solution.py:604
  115.0 8.1 %constant_dynamic-slice_fusion.1 = (bf16[1152,1728]{1,0:T(8,128)(2,1)S(1)}, bf16[1152,1728]{1,0:T(8,128)(2,1)S(1)}) fusion(bf16[1152,3456]{1,0:T(8,128)(2,1)} %param.26, s32[]{:T(128)S(6)} %select_n.118, bf16[1152,3456]{1,0:T(8,128)(2,1)} %param.25), kind=kLoop, calls=%fused_computation.169 | loop fusion | bytes 15925252 | tf_op jit(solution)/shard_map/dynamic_slice | solution.py:1044
  123.2 2.5 fusion.17
  127.3 4.7 multiply_convert_fusion.1
  133.4 4.0 fusion.25
  137.3 13.9 %shard_map.292 = f32[128,1152]{1,0:T(8,128)} custom-call(bf16[4,128,1152]{2,1,0:T(8,128)(2,1)} %bitcast.144), custom_call_target="tpu_custom_call" | custom-call | tf_op jit(solution)/shard_map/pallas_call | solution.py:636
  156.5 13.6 %shard_map.293 = bf16[4,128,1152]{2,1,0:T(8,128)(2,1)} custom-call(bf16[128,1152]{1,0:T(8,128)(2,1)} %get-tuple-element.140.rows_ref), custom_call_target="tpu_custom_call" | custom-call | tf_op jit(solution)/shard_map/pallas_call | solution.py:604
  170.2 8.0 %fusion.10 = (bf16[512,1792]{1,0:T(8,128)(2,1)S(1)}, bf16[512,1792]{1,0:T(8,128)(2,1)S(1)}) fusion(f32[512,1792]{1,0:T(8,128)} %copy-done.74, f32[512,1792]{1,0:T(8,128)} %get-tuple-element.175, bf16[512,1152]{1,0:T(8,128)(2,1)} %bitcast.141, bf16[1728,1152]{1,0:T(8,128)(2,1)} %copy-done.17), kind=kOutput, calls=%fused_computation.23 | convolution fusion | flops 2135949312 | bytes 16171008 | tf_op jit(solution)/shard_map/dot_general | solution.py:311
  178.2 2.6 fusion.11
  181.7 3.6 fusion.22
  185.3 12.4 %shard_map.294 = f32[128,1152]{1,0:T(8,128)} custom-call(bf16[4,128,1152]{2,1,0:T(8,128)(2,1)} %bitcast.143), custom_call_target="tpu_custom_call" | custom-call | tf_op jit(solution)/shard_map/pallas_call | solution.py:636
  208.3 2.7 copy.136.key_ref
  211.0 3.0 compare_select_fusion.3
  214.0 91.4 %shard_map.295 = (f32[4,256,128]{2,1,0:T(8,128)}, f32[128,512]{1,0:T(8,128)}) custom-call(bf16[4,2048,512]{2,1,0:T(8,128)(2,1)} %get-tuple-element.26.buf, bf16[4,256,256]{2,1,0:T(8,128)(2,1)} %get-tuple-element.27.q_all, bf16[4,128,256]{2,1,0:T(8,128)(2,1)} %get-tuple-element.143.do_ref, f32[8,128]{1,0:T(8,128)} %concatenate.131.delta_ref, ...), custom_call_target="tpu_custom_call" | custom-call | tf_op jit(solution)/shard_map/pallas_call | solution.py:567
  313.2 3.3 pad_maximum_fusion
  317.3 69.0 %shard_map.296 = (bf16[2,1280,1152]{2,1,0:T(8,128)(2,1)}, f32[8,1152]{1,0:T(8,128)}) custom-call(bf16[2,1280,1152]{2,1,0:T(8,128)(2,1)} %bitcast.118, f32[8,1152]{1,0:T(8,128)} %stack.15.gains_ref), custom_call_target="tpu_custom_call" | custom-call | tf_op jit(solution)/shard_map/pallas_call | solution.py:935
  386.3 4.2 fusion.99
  397.4 4.2 convolution_convert_fusion
  410.1 5.9 %maximum_maximum_fusion = bf16[1152,2,2816]{2,0,1:T(8,128)(2,1)} fusion(bf16[1152,2,896]{2,0,1:T(8,128)(2,1)S(1)} %bitcast.119, bf16[1152,2,896]{2,0,1:T(8,128)(2,1)S(1)} %bitcast.120, bf16[1152,2,896]{2,0,1:T(8,128)(2,1)S(1)} %bitcast.121, bf16[2816]{0:T(1024)(128)(2,1)S(1)} %pad.34.clone), kind=kLoop, calls=%fused_computation | loop fusion | flops 51904512 | bytes 25368064 | tf_op jit(solution)/shard_map/concatenate | solution.py:1071
  416.0 18.3 %reshape.581 = bf16[4,2,144,2,2,1408]{5,4,2,1,0,3:T(2,128)(2,1)} reshape(bf16[1152,2,2816]{2,0,1:T(8,128)(2,1)} %maximum_maximum_fusion) | data formatting | bytes 25952256 | tf_op jit(solution)/shard_map/reshape | solution.py:1080
  434.3 12.5 %copy.162 = bf16[4,2,144,2,2,1408]{5,2,4,1,0,3:T(8,128)(2,1)} copy(bf16[4,2,144,2,2,1408]{5,4,2,1,0,3:T(2,128)(2,1)} %reshape.581) | data formatting | bytes 25952256 | tf_op jit(solution)/shard_map/reshape | solution.py:1080
  446.8 81.1 %shard_map.297 = bf16[8,32,1408]{2,1,0:T(8,128)(2,1)} custom-call(bf16[2,4,2,2,144,1408]{5,4,3,2,1,0:T(8,128)(2,1)} %bitcast.117), custom_call_target="tpu_custom_call" | custom-call | tf_op jit(solution)/shard_map/pallas_call | solution.py:789
  (284 shorter events, 76.6 us)
Async XLA Ops:
  0.7 22.5 %copy-start.2 = (bf16[128,1152]{1,0:T(8,128)(2,1)S(1)}, bf16[128,1152]{1,0:T(8,128)(2,1)}, u32[]{:S(2)}) copy-start(bf16[128,1152]{1,0:T(8,128)(2,1)} %param.18) | copy-start | bytes 884740
  0.7 22.5 %copy-start.33 = (f32[1152]{0:T(1024)S(1)}, f32[1152]{0:T(1024)}, u32[]{:S(2)}) copy-start(f32[1152]{0:T(1024)} %param.28) | copy-start | bytes 13828
  0.7 22.5 %copy-start.19 = (bf16[1152,512]{1,0:T(8,128)(2,1)S(1)}, bf16[1152,512]{1,0:T(8,128)(2,1)}, u32[]{:S(2)}) copy-start(bf16[1152,512]{1,0:T(8,128)(2,1)} %w_ref.2) | copy-start | bytes 3538948
  2.0 23.6 %copy-start.46 = (f32[128]{0:T(128)}, f32[128]{0:T(128)S(1)}, u32[]{:S(2)}) copy-start(f32[128]{0:T(128)S(1)} %fusion.76) | copy-start | bytes 1540
  3.3 22.4 %copy-start.60 = (f32[128]{0:T(128)}, f32[128]{0:T(128)S(1)}, u32[]{:S(2)}) copy-start(f32[128]{0:T(128)S(1)} %multiply_power_fusion) | copy-start | bytes 1540
  4.0 21.6 %copy-start.62 = (f32[128]{0:T(128)}, f32[128]{0:T(128)S(1)}, u32[]{:S(2)}) copy-start(f32[128]{0:T(128)S(1)} %dynamic-slice_convert_fusion) | copy-start | bytes 1540
  8.6 17.9 %copy-start.50 = (f32[256]{0:T(256)S(1)}, f32[256]{0:T(256)}, u32[]{:S(2)}) copy-start(f32[256]{0:T(256)} %param.29) | copy-start | bytes 3076
  25.6 66.7 %copy-start.52 = (f32[128,4]{0,1:T(4,128)}, f32[128,4]{0,1:T(4,128)S(1)}, u32[]{:S(2)}) copy-start(f32[128,4]{0,1:T(4,128)S(1)} %get-tuple-element.170) | copy-start | bytes 6148
  26.7 65.7 %copy-start.26 = (f32[128,128]{0,1:T(8,128)}, f32[128,128]{0,1:T(8,128)S(1)}, u32[]{:S(2)}) copy-start(f32[128,128]{0,1:T(8,128)S(1)} %copy.126) | copy-start | bytes 196612
  26.8 65.6 %copy-start.28 = (f32[128,128]{0,1:T(8,128)}, f32[128,128]{0,1:T(8,128)S(1)}, u32[]{:S(2)}) copy-start(f32[128,128]{0,1:T(8,128)S(1)} %copy.125) | copy-start | bytes 196612
  123.1 8.9 %slice-start = ((s8[7962624]{0:T(1024)(128)(4,1)}), s8[4194304]{0:T(1024)(128)(4,1)S(1)}, s32[]{:S(2)}) async-start(s8[7962624]{0:T(1024)(128)(4,1)} %bitcast.135), calls=%async_computation | async-start | bytes 8388608
  133.4 19.1 %copy-start.18 = (bf16[128,1152]{1,0:T(8,128)(2,1)S(1)}, bf16[128,1152]{1,0:T(8,128)(2,1)}, u32[]{:S(2)}) copy-start(bf16[128,1152]{1,0:T(8,128)(2,1)} %param.34) | copy-start | bytes 884740
  133.4 19.1 %copy-start.39 = (f32[1152]{0:T(1024)S(1)}, f32[1152]{0:T(1024)}, u32[]{:S(2)}) copy-start(f32[1152]{0:T(1024)} %param.33) | copy-start | bytes 13828
  181.7 16.0 %copy-start.59 = (f32[128]{0:T(128)S(1)}, f32[128]{0:T(128)}, u32[]{:S(2)}) copy-start(f32[128]{0:T(128)} %copy-done.58) | copy-start | bytes 1540
  181.7 17.8 %copy-start.67 = (f32[128]{0:T(128)S(1)}, f32[128]{0:T(128)}, u32[]{:S(2)}) copy-start(f32[128]{0:T(128)} %copy-done.66) | copy-start | bytes 1540
  181.7 17.8 %copy-start.6 = (f32[128,1152]{1,0:T(8,128)S(1)}, f32[128,1152]{1,0:T(8,128)}, u32[]{:S(2)}) copy-start(f32[128,1152]{1,0:T(8,128)} %copy-done.5) | copy-start | bytes 1769476
  181.7 17.8 %copy-start.37 = (f32[1152]{0:T(1024)S(1)}, f32[1152]{0:T(1024)}, u32[]{:S(2)}) copy-start(f32[1152]{0:T(1024)} %param.31) | copy-start | bytes 13828
  181.7 17.8 %copy-start.55 = (f32[128]{0:T(128)S(1)}, f32[128]{0:T(128)}, u32[]{:S(2)}) copy-start(f32[128]{0:T(128)} %copy-done.54) | copy-start | bytes 1540
  185.3 16.3 %copy-start.71 = (f32[128]{0:T(128)S(1)}, f32[128]{0:T(128)}, u32[]{:S(2)}) copy-start(f32[128]{0:T(128)} %copy-done.70) | copy-start | bytes 1540
  214.0 92.7 %copy-start.27 = (f32[128,128]{0,1:T(8,128)S(1)}, f32[128,128]{0,1:T(8,128)}, u32[]{:S(2)}) copy-start(f32[128,128]{0,1:T(8,128)} %copy-done.26) | copy-start | bytes 196612
  214.0 92.7 %copy-start.29 = (f32[128,128]{0,1:T(8,128)S(1)}, f32[128,128]{0,1:T(8,128)}, u32[]{:S(2)}) copy-start(f32[128,128]{0,1:T(8,128)} %copy-done.28) | copy-start | bytes 196612
  214.0 92.8 %copy-start.8 = (f32[128,1024]{0,1:T(8,128)S(1)}, f32[128,1024]{0,1:T(8,128)}, u32[]{:S(2)}) copy-start(f32[128,1024]{0,1:T(8,128)} %copy-done.7) | copy-start | bytes 1572868
  214.0 92.8 %copy-start.41 = (f32[128,4]{0,1:T(4,128)S(1)}, f32[128,4]{0,1:T(4,128)}, u32[]{:S(2)}) copy-start(f32[128,4]{0,1:T(4,128)} %copy-done.40) | copy-start | bytes 6148
  214.0 92.8 %copy-start.51 = (f32[256]{0:T(256)S(1)}, f32[256]{0:T(256)}, u32[]{:S(2)}) copy-start(f32[256]{0:T(256)} %param.29) | copy-start | bytes 3076
  (58 other events, 160.8 us)

commit v2 on v1

--- a/solution.py
+++ b/solution.py
@@ -110,9 +110,9 @@
         self.on_left.wait_recv()
 
 
-def by_rows(ref, act, most=16):
+def by_rows(ref, act):
     *lead, rows, _ = ref.shape
-    block = most
+    block = next(size for size in (64, 48, 32, 16) if rows % size == 0)
     for spot in np.ndindex(*lead):
 
         def one(i, carry, spot=spot):
@@ -265,6 +265,10 @@
     return (lambda j: view(j).at[:, pl.ds(0, HD)]), (lambda j: view(j).at[:, pl.ds(HD, HD)])
 
 
+def chunk_rows(n):
+    return [256 * n + 64 * i if n < 6 else 1536 + 128 * i + 64 * (n - 6) for i in range(4)]
+
+
 def key_tokens():
     out = np.zeros((4, 2048), np.int32)
     for skip, rows, base, axes in PARTS:
@@ -277,7 +281,7 @@
     order = np.zeros((8, CHUNK), np.int64)
     for c in range(8):
         for i in range(4):
-            start = 256 * c + 64 * i if c < 6 else 1536 + 128 * i + 64 * (c - 6)
+            start = chunk_rows(c)[i]
             order[c, 64 * i : 64 * i + 64] = np.arange(start, start + 64)
     return out[:, order]
 
@@ -285,25 +289,18 @@
 KEY_TOKENS = key_tokens()
 
 
-def chunk_at(place, n, by):
-    lead = jnp.where(
-        n < 3, place.step("z", by), jnp.where(n < 6, place.step("y", by), place.step("x", by))
-    )
-    first_y = jnp.where(n < 3, n, jnp.where(n < 6, lead, (n - 6) * 2))
-    last_y = jnp.where(n < 3, n + 1, jnp.where(n < 6, lead, (n - 6) * 2 + 1))
-    start = jnp.where(n < 6, n * 256, 1536 + 64 * (n - 6))
-    stride = jnp.where(n < 6, 64, 128)
-    starts = [pl.multiple_of(start + stride * i, 16) for i in range(4)]
-    skip = first_y > place.y
-    holds_first = (lead == 0) & ((n == 0) | (n == 3) | (n == 6))
-    final = (place.x == 3) & (place.y == 3) & (place.z == 3)
-    plain = (last_y < place.y) & jnp.logical_not(holds_first) & jnp.logical_not(final)
-    return lead, starts, skip, plain
-
-
-def read_chunk(buf, lead, starts, column):
-    return jnp.concatenate(
-        [buf[lead, pl.ds(start, 64), pl.ds(column, HD)] for start in starts], axis=0
+def read_sets(place, buf, key_ref, chunks, by):
+    keys, values, tokens = [], [], []
+    for n in chunks:
+        lead = place.step("zyx"[n // 3], by)
+        rows = chunk_rows(n)
+        keys += [buf[lead, start : start + 64, :HD] for start in rows]
+        values += [buf[lead, start : start + 64, HD:] for start in rows]
+        tokens.append(key_ref[lead, n : n + 1])
+    return (
+        jnp.concatenate(keys, axis=0),
+        jnp.concatenate(values, axis=0),
+        jnp.concatenate(tokens, axis=1),
     )
 
 
@@ -363,41 +360,23 @@
     finish_w = swap_weight(place, net, w_ref, w_other, w_ref.shape[0] // 4)
     swap_q.wait_recv()
 
-    def attend(n, by):
-        lead, starts, skip, plain = chunk_at(place, n, by)
-
-        def run(masked):
-            keys = read_chunk(buf, lead, starts, 0)
-            values = read_chunk(buf, lead, starts, HD)
-            if masked:
-                token = key_ref[lead, pl.ds(n, 1)]
-                allowed = (token <= last_ref[...]) & (token >= first_ref[...])
-            for h in range(HEADS):
-                weights = jnp.exp(contract(q_all[h], keys, 1, 1))
-                if masked:
-                    weights = jnp.where(allowed, weights, 0.0)
-                l_sum[h] += weights[:, :128] + weights[:, 128:]
-                o_sum[h] += jnp.dot(weights.astype(BF), values, preferred_element_type=F32)
-
-        @pl.when(plain)
-        def _():
-            run(False)
-
-        @pl.when(jnp.logical_not(plain) & jnp.logical_not(skip))
-        def _():
-            run(True)
-
-    def visit(by):
-        lax.fori_loop(0, 8, lambda n, c: (attend(n, by), c)[1], 0)
-
-    visit(0)
+    def attend(by):
+        keys, values, token = read_sets(place, buf, key_ref, range(8), by)
+        allowed = (token <= last_ref[...]) & (token >= first_ref[...])
+        for h in range(HEADS):
+            weights = jnp.exp(contract(q_all[h], keys, 1, 1))
+            weights = jnp.where(allowed, weights, 0.0)
+            l_sum[h] += sum(weights[:, 128 * i : 128 * i + 128] for i in range(16))
+            o_sum[h] += jnp.dot(weights.astype(BF), values, preferred_element_type=F32)
+
+    attend(0)
     for rings in stages:
         rings[2].forward()
     finish_w()
-    lax.fori_loop(0, 16, lambda n, c: (attend(lax.rem(n, 8), 1 + 2 * lax.div(n, 8)), c)[1], 0)
+    lax.fori_loop(0, 2, lambda i, c: (attend(1 + 2 * i), c)[1], 0)
     for rings in stages:
         rings[2].finish()
-    visit(2)
+    attend(2)
     swap_o = net.copy(o_sum.at[:, theirs], o_got, partner)
     swap_l = net.copy(l_sum.at[:, theirs], l_got, partner)
     net.go(swap_l)
@@ -444,8 +423,10 @@
     key_ref,
     last_ref,
     first_ref,
+    sums_ref,
     dq_out,
     dkv_out,
+    home_out,
     do_all,
     delta_all,
     grads,
@@ -453,10 +434,12 @@
     dq_got,
     *rest,
 ):
-    *rooms, send, recv = rest
+    rooms, rest = rest[:54], rest[54:]
+    *weight_refs, send, recv, send2, recv2, here = rest
     place, net = Place(), Net(send, recv)
     core, partner = place.core, place.partner()
-    greet(ring(place, "x") + ring(place, "y") + ring(place, "z") + [partner])
+    weights = WeightSums(place, net, sums_ref, home_out, weight_refs, (send2, recv2, here))
+    greet(weights.friends + ring(place, "x") + ring(place, "y"))
     mine = pl.ds(pl.multiple_of(core * TOK, TOK), TOK)
     theirs = pl.ds(pl.multiple_of((1 - core) * TOK, TOK), TOK)
     do_all[:, mine] = do_ref[...]
@@ -478,64 +461,56 @@
     swap_do.wait_recv()
     swap_delta.wait_recv()
 
-    def differ(n, by):
-        lead, starts, skip, plain = chunk_at(place, n, by)
-
-        def store(column, value):
-            value = value.astype(BF)
-            for i, start in enumerate(starts):
-                grads[lead, pl.ds(start, 64), pl.ds(column, HD)] = value[64 * i : 64 * i + 64]
-
-        def run(masked):
-            keys = read_chunk(buf, lead, starts, 0)
-            values = read_chunk(buf, lead, starts, HD)
-            if masked:
-                token = key_ref[lead, n]
-                allowed = (token <= last_ref[...]) & (token >= first_ref[...])
-            d_keys = d_values = None
-            for h in range(HEADS):
-                probs = jnp.exp(contract(keys, q_all[h], 1, 1))
-                if masked:
-                    probs = jnp.where(allowed, probs, 0.0)
-                delta = jnp.concatenate(
-                    [delta_all[0, pl.ds(h, 1)], delta_all[1, pl.ds(h, 1)]], axis=1
-                )
-                d_scores = (probs * (contract(values, do_all[h], 1, 1) - delta)).astype(BF)
-                value_term = jnp.dot(probs.astype(BF), do_all[h], preferred_element_type=F32)
-                key_term = jnp.dot(d_scores, q_all[h], preferred_element_type=F32)
-                d_values = value_term if h == 0 else d_values + value_term
-                d_keys = key_term if h == 0 else d_keys + key_term
-                dq_sum[h] += contract(keys, d_scores, 0, 0)
-            store(0, d_keys)
-            store(HD, d_values)
-
-        @pl.when(plain)
-        def _():
-            run(False)
-
-        @pl.when(jnp.logical_not(plain) & jnp.logical_not(skip))
-        def _():
-            run(True)
-
-        @pl.when(skip)
-        def _():
-            for start in starts:
-                grads[lead, pl.ds(start, 64)] = jnp.zeros((64, 2 * HD), BF)
+    def differ(first, by):
+        chunks = range(first, first + 4)
+        keys, values, token = read_sets(place, buf, key_ref, chunks, by)
+        token = jnp.concatenate(
+            [
+                jnp.transpose(jnp.broadcast_to(token[:, 128 * i : 128 * i + 128], (128, 128)))
+                for i in range(8)
+            ],
+            axis=0,
+        )
+        token = jnp.concatenate([token, token], axis=1)
+        allowed = (token <= last_ref[...]) & (token >= first_ref[...])
+        d_keys = d_values = None
+        for h in range(HEADS):
+            probs = jnp.exp(contract(keys, q_all[h], 1, 1))
+            probs = jnp.where(allowed, probs, 0.0)
+            delta = jnp.concatenate([delta_all[0, h : h + 1], delta_all[1, h : h + 1]], axis=1)
+            d_scores = (probs * (contract(values, do_all[h], 1, 1) - delta)).astype(BF)
+            value_term = jnp.dot(probs.astype(BF), do_all[h], preferred_element_type=F32)
+            key_term = jnp.dot(d_scores, q_all[h], preferred_element_type=F32)
+            d_values = value_term if h == 0 else d_values + value_term
+            d_keys = key_term if h == 0 else d_keys + key_term
+            dq_sum[h] += contract(keys, d_scores, 0, 0)
+        d_keys, d_values = d_keys.astype(BF), d_values.astype(BF)
+        for m, n in enumerate(chunks):
+            lead = place.step("zyx"[n // 3], by)
+            for i, start in enumerate(chunk_rows(n)):
+                at = 256 * m + 64 * i
+                grads[lead, start : start + 64, :HD] = d_keys[at : at + 64]
+                grads[lead, start : start + 64, HD:] = d_values[at : at + 64]
 
     def visit(by):
-        lax.fori_loop(0, 8, lambda n, c: (differ(n, by), c)[1], 0)
-
+        differ(0, by)
+        differ(4, by)
+
+    weights.begin()
     visit(2)
     for rings, _ in stages:
         rings[2].start_far()
-    lax.fori_loop(0, 16, lambda n, c: (differ(lax.rem(n, 8), 1 + 2 * lax.div(n, 8)), c)[1], 0)
+    weights.turn()
+    lax.fori_loop(0, 2, lambda i, c: (visit(1 + 2 * i), c)[1], 0)
     for rings, _ in stages:
         rings[2].start_near()
     for rings, _ in stages:
         rings[2].middle()
+    weights.next()
     visit(0)
     swap_dq = net.copy(dq_sum.at[:, :, theirs], dq_got, partner)
     net.go(swap_dq)
+    weights.turn_again()
     for level in (2, 1, 0):
         for (rings, views), part in zip(stages, PARTS):
             axis, view = views[level]
@@ -549,16 +524,19 @@
             else:
                 out = dkv_out.at[pl.ds(skip, rows)]
                 rings[level].finish(out.at[:, pl.ds(0, HD)], out.at[:, pl.ds(HD, HD)])
+        if level == 2:
+            weights.send_home()
         if level:
             for rings, _ in stages:
                 rings[level - 1].middle()
+    weights.arrive()
     swap_dq.wait_recv()
     for h in range(HEADS):
         dq_out[h] = dq_sum[h, :, mine] + dq_got[h]
     net.drain()
 
 
-def attention_backward(kv_all, q_all, d_heads, delta, key_columns, last, first, call_id):
+def attention_backward(kv_all, q_all, d_heads, delta, key_rows, last, first, sums, call_id):
     shape = jax.ShapeDtypeStruct
     rooms = []
     for _, rows, _, _ in PARTS:
@@ -566,9 +544,13 @@
             rooms += RingScatter.room_shapes((blocks * rows, HD), (blocks * rows, HD))
     return pl.pallas_call(
         backward_kernel,
-        out_shape=(shape((HEADS, HD, TOK), F32), shape((TOK, 2 * HD), F32)),
-        in_specs=[IN_VMEM] * 7,
-        out_specs=[IN_VMEM] * 2,
+        out_shape=(
+            shape((HEADS, HD, TOK), F32),
+            shape((TOK, 2 * HD), F32),
+            shape((8, 32, HALF), BF),
+        ),
+        in_specs=[IN_VMEM] * 8,
+        out_specs=[IN_VMEM] * 3,
         scratch_shapes=[
             pltpu.VMEM((HEADS, ROWS, HD), BF),
             pltpu.VMEM((2, 8, TOK), F32),
@@ -576,10 +558,13 @@
             pltpu.VMEM((HEADS, HD, ROWS), F32),
             pltpu.VMEM((HEADS, HD, TOK), F32),
             *rooms,
-            *sems(64),
+            *WeightSums.scratch(),
+            *sems(96),
+            *sems(8),
+            pltpu.SemaphoreType.DMA((1,)),
         ],
         compiler_params=params(call_id),
-    )(kv_all, q_all, d_heads, delta, key_columns, last, first)
+    )(kv_all, q_all, d_heads, delta, key_rows, last, first, sums)
 
 
 def x_gather_kernel(rows_ref, out_ref, send, recv):
@@ -643,165 +628,226 @@
     )(terms)
 
 
-def ffn_grads_kernel(terms_ref, out_ref, got, snd, rcv, *rest):
-    *rooms, send, recv, send2, recv2, here = rest
+def ffn_terms_kernel(
+    terms_ref, h_ref, f_ref, gate_ref, up_ref, act_ref, dh_out, sums_out, snd, got, *rest
+):
+    *room, send, recv = rest
     place, net = Place(), Net(send, recv)
     core, partner = place.core, place.partner()
-    x_hi, x_lo = lax.div(place.x, 2), lax.rem(place.x, 2)
-    r, c = lax.div(place.z, 2), lax.rem(place.z, 2)
-    friends = []
-    for k in range(1, 16):
-        spot = lax.rem(x_hi * 8 + place.z * 2 + core + k, 16)
-        friends.append(
-            place.device(
-                x=lax.div(spot, 8) * 2 + x_lo, z=lax.rem(lax.div(spot, 2), 4), core=lax.rem(spot, 2)
-            )
-        )
-    greet(friends + ring(place, "y"))
-    swaps = [net.copy(terms_ref.at[1 - core, y], got.at[y], partner) for y in range(4)]
+    greet(ring(place, "x") + [partner])
+    half = TOK // 2
+    line = RingScatter(
+        net,
+        place,
+        "x",
+        lambda j: terms_ref.at[j, pl.ds(0, half)],
+        lambda j: terms_ref.at[j, pl.ds(half, half)],
+        room,
+    )
+    line.start_far()
+    line.start_near()
+
+    def fill(target, which):
+        columns = pl.ds(pl.multiple_of(which * 896, 128), 896)
+
+        def some_rows(i, carry):
+            rows = pl.ds(pl.multiple_of(i * 576, 64), 576)
+            pairs = ((h_ref, gate_ref), (h_ref, up_ref), (f_ref, act_ref))
+            for m, (left, right) in enumerate(pairs):
+                term = jnp.dot(left[rows], right[:, columns], preferred_element_type=F32).astype(BF)
+                for k in range(4):
+                    piece = term[144 * k : 144 * k + 144]
+                    for c in range(2):
+                        low = max(896 * m, HALF * c)
+                        high = min(896 * m + 896, HALF * c + HALF)
+                        if low < high:
+                            target[2 * i + k // 2, k % 2, c, :, low - HALF * c : high - HALF * c] = (
+                                piece[:, low - 896 * m : high - 896 * m]
+                            )
+            return carry
+
+        lax.fori_loop(0, 2, some_rows, 0)
+        for y in range(4):
+            target[y, :, 1, :, 1280:] = jnp.zeros((2, 144, 128), BF)
+
+    fill(snd, 1 - core)
+    swaps = [net.copy(snd.at[y], got.at[y], partner) for y in range(4)]
     for swap in swaps:
         net.go(swap)
-
-    def left(lead):
-        return lead.at[..., pl.ds(0, CUT)]
-
-    def right(lead):
-        return lead.at[..., pl.ds(CUT, HALF - CUT)]
-
-    y_first = RingScatter(
-        net, place, "y", lambda j: left(got.at[j, 0]), lambda j: left(got.at[j, 1]), rooms[0:6]
-    )
-
-    def z_spot(j):
-        return got.at[:, lax.div(j, 2), lax.rem(j, 2)]
-
-    z_first = RingScatter(
-        net,
-        place,
-        "z",
-        lambda j: right(z_spot(j).at[pl.ds(0, 2)]),
-        lambda j: right(z_spot(j).at[pl.ds(2, 2)]),
-        rooms[6:12],
-    )
-
-    def then_z(j):
-        return got.at[place.y, lax.div(j, 2), lax.rem(j, 2)]
-
-    z_second = RingScatter(
-        net,
-        place,
-        "z",
-        lambda j: then_z(j).at[:, pl.ds(0, 384)],
-        lambda j: then_z(j).at[:, pl.ds(384, 384)],
-        rooms[12:18],
-    )
-
-    def then_y(j):
-        return got.at[j, r, c]
-
-    y_second = RingScatter(
-        net,
-        place,
-        "y",
-        lambda j: then_y(j).at[:, pl.ds(768, 384)],
-        lambda j: then_y(j).at[:, pl.ds(1152, 256)],
-        rooms[18:24],
-    )
+    line.middle()
+    fill(sums_out, core)
+    line.finish(dh_out.at[pl.ds(0, half)], dh_out.at[pl.ds(half, half)])
     for y, swap in enumerate(swaps):
         swap.wait_recv()
-        add_to(got.at[y], terms_ref.at[core, y])
-    first, second = (y_first, z_first), (z_second, y_second)
-    for line in first:
-        line.start_far()
-        line.start_near()
-    for line in first:
-        line.middle()
-    me = place.y
-    y_first.finish(left(got.at[me, 0]), left(got.at[me, 1]))
-    z_second.start_far()
-    z_second.start_near()
-    own = z_spot(place.z)
-    z_first.finish(right(own.at[pl.ds(0, 2)]), right(own.at[pl.ds(2, 2)]))
-    y_second.start_far()
-    y_second.start_near()
-    for line in second:
-        line.middle()
-    done = got.at[place.y, r, c]
-    z_second.finish(done.at[:, pl.ds(0, 384)], done.at[:, pl.ds(384, 384)])
-    y_second.finish(done.at[:, pl.ds(768, 384)], done.at[:, pl.ds(1152, 256)])
-    total = done[...].astype(F32)
-    rest_rows = jnp.zeros((14, HALF), F32)
-    for k in range(8):
-        snd[k] = jnp.concatenate([total[18 * k : 18 * k + 18], rest_rows], axis=0).astype(BF)
-    slot = x_hi * 4 + core * 2 + c
-    own_spot = place.z * 2 + core
-    stays = r == x_hi
-    for k in range(8):
-        copy = pltpu.make_async_remote_copy(
-            src_ref=snd.at[k],
-            dst_ref=rcv.at[slot],
-            send_sem=send2.at[k],
-            recv_sem=recv2.at[slot],
-            device_id=place.device(x=r * 2 + x_lo, z=k // 2, core=k % 2),
-            device_id_type=MESH,
+        add_to(sums_out.at[y], got.at[y])
+    net.drain()
+
+
+def ffn_terms(terms, h_turned, f_turned, d_gate, d_up, act, call_id):
+    half = (TOK // 2, D)
+    shape = jax.ShapeDtypeStruct
+    every = (4, 2, 2, 144, HALF)
+    return pl.pallas_call(
+        ffn_terms_kernel,
+        out_shape=(shape((TOK, D), F32), shape(every, BF)),
+        in_specs=[IN_VMEM] * 6,
+        out_specs=[IN_VMEM] * 2,
+        scratch_shapes=[
+            pltpu.VMEM(every, BF),
+            pltpu.VMEM(every, BF),
+            *RingScatter.room_shapes(half, half),
+            *sems(10),
+        ],
+        compiler_params=params(call_id),
+    )(terms, h_turned, f_turned, d_gate, d_up, act)
+
+
+class WeightSums:
+    def __init__(self, place, net, sums, home, refs, marks):
+        y1, z1, z2, y2, snd, rcv, *rooms = refs
+        self.place, self.home, self.snd, self.rcv, self.marks = place, home, snd, rcv, marks
+        self.y1, self.z1, self.y2, self.z2 = y1, z1, y2, z2
+        self.x_hi, self.x_lo = lax.div(place.x, 2), lax.rem(place.x, 2)
+        self.friends = []
+        for k in range(1, 16):
+            spot = lax.rem(self.x_hi * 8 + place.z * 2 + place.core + k, 16)
+            x, z = lax.div(spot, 8) * 2 + self.x_lo, lax.rem(lax.div(spot, 2), 4)
+            self.friends.append(place.device(x=x, z=z, core=lax.rem(spot, 2)))
+
+        left, right = pl.ds(0, CUT), pl.ds(CUT, HALF - CUT)
+
+        def z_spot(j):
+            return sums.at[:, lax.div(j, 2), lax.rem(j, 2), :, right]
+
+        def then_z(j):
+            return y1.at[lax.div(j, 2), lax.rem(j, 2)]
+
+        self.y_first = RingScatter(
+            net,
+            place,
+            "y",
+            lambda j: sums.at[j, 0, :, :, left],
+            lambda j: sums.at[j, 1, :, :, left],
+            rooms[0:6],
         )
-        is_here = stays & (own_spot == k)
-
-        @pl.when(jnp.logical_not(is_here))
-        def _(copy=copy):
-            copy.start()
-
-        @pl.when(is_here)
-        def _(k=k):
-            keep = pltpu.make_async_copy(snd.at[k], rcv.at[slot], here.at[0])
-            keep.start()
-            keep.wait()
-
-    for m in range(8):
-        arrival = pltpu.make_async_remote_copy(
-            src_ref=snd.at[m],
-            dst_ref=rcv.at[m],
-            send_sem=send2.at[m],
-            recv_sem=recv2.at[m],
-            device_id=partner,
-            device_id_type=MESH,
+        self.z_first = RingScatter(
+            net,
+            place,
+            "z",
+            lambda j: z_spot(j).at[pl.ds(0, 2)],
+            lambda j: z_spot(j).at[pl.ds(2, 2)],
+            rooms[6:12],
         )
-
-        @pl.when(jnp.logical_not(stays & (slot == m)))
-        def _(arrival=arrival):
-            arrival.wait_recv()
-
-        @pl.when(jnp.logical_not(stays & (own_spot == m)))
-        def _(arrival=arrival):
-            arrival.wait_send()
-
-    out_ref[...] = rcv[...]
-    net.drain()
-
-
-def ffn_grads(terms, call_id):
-    rooms = [
-        *RingScatter.room_shapes((2, 144, CUT), (2, 144, CUT)),
-        *RingScatter.room_shapes((2, 144, HALF - CUT), (2, 144, HALF - CUT)),
-        *RingScatter.room_shapes((144, 384), (144, 384)),
-        *RingScatter.room_shapes((144, 384), (144, 256)),
-    ]
-    return pl.pallas_call(
-        ffn_grads_kernel,
-        out_shape=jax.ShapeDtypeStruct((8, 32, HALF), BF),
-        in_specs=[IN_VMEM],
-        out_specs=IN_VMEM,
-        scratch_shapes=[
-            pltpu.VMEM((4, 2, 2, 144, HALF), BF),
+        self.z_second = RingScatter(
+            net,
+            place,
+            "z",
+            lambda j: then_z(j).at[:, pl.ds(0, 384)],
+            lambda j: then_z(j).at[:, pl.ds(384, 384)],
+            rooms[12:18],
+        )
+        self.y_second = RingScatter(
+            net,
+            place,
+            "y",
+            lambda j: z1.at[j, :, pl.ds(0, 384)],
+            lambda j: z1.at[j, :, pl.ds(384, 256)],
+            rooms[18:24],
+        )
+
+    @staticmethod
+    def scratch():
+        rest = HALF - CUT
+        return [
+            pltpu.VMEM((2, 2, 144, CUT), BF),
+            pltpu.VMEM((4, 144, rest), BF),
+            pltpu.VMEM((144, CUT), F32),
+            pltpu.VMEM((144, rest), F32),
             pltpu.VMEM((8, 32, HALF), BF),
             pltpu.VMEM((8, 32, HALF), BF),
-            *rooms,
-            *sems(32),
-            *sems(8),
-            pltpu.SemaphoreType.DMA((1,)),
-        ],
-        compiler_params=params(call_id),
-    )(terms)
+            *RingScatter.room_shapes((2, 144, CUT), (2, 144, CUT)),
+            *RingScatter.room_shapes((2, 144, rest), (2, 144, rest)),
+            *RingScatter.room_shapes((144, 384), (144, 384)),
+            *RingScatter.room_shapes((144, 384), (144, 256)),
+        ]
+
+    def begin(self):
+        for line in (self.y_first, self.z_first):
+            line.start_far()
+            line.start_near()
+
+    def turn(self):
+        self.y_first.middle()
+        self.z_first.middle()
+
+    def next(self):
+        self.y_first.finish(self.y1.at[0], self.y1.at[1])
+        self.z_second.start_far()
+        self.z_second.start_near()
+        self.z_first.finish(self.z1.at[pl.ds(0, 2)], self.z1.at[pl.ds(2, 2)])
+        self.y_second.start_far()
+        self.y_second.start_near()
+
+    def turn_again(self):
+        self.z_second.middle()
+        self.y_second.middle()
+
+    def send_home(self):
+        z2, y2, snd = self.z2, self.y2, self.snd
+        self.z_second.finish(z2.at[:, pl.ds(0, 384)], z2.at[:, pl.ds(384, 384)])
+        self.y_second.finish(y2.at[:, pl.ds(0, 384)], y2.at[:, pl.ds(384, 256)])
+        total = jnp.concatenate([z2[...], y2[...]], axis=1)
+        blank = jnp.zeros((14, HALF), F32)
+        for k in range(8):
+            snd[k] = jnp.concatenate([total[18 * k : 18 * k + 18], blank], axis=0).astype(BF)
+        place = self.place
+        send, recv, here = self.marks
+        row_half = lax.div(place.z, 2)
+        self.slot = self.x_hi * 4 + place.core * 2 + lax.rem(place.z, 2)
+        self.own = place.z * 2 + place.core
+        self.stays = row_half == self.x_hi
+        for k in range(8):
+            copy = pltpu.make_async_remote_copy(
+                src_ref=snd.at[k],
+                dst_ref=self.rcv.at[self.slot],
+                send_sem=send.at[k],
+                recv_sem=recv.at[self.slot],
+                device_id=place.device(x=row_half * 2 + self.x_lo, z=k // 2, core=k % 2),
+                device_id_type=MESH,
+            )
+            is_here = self.stays & (self.own == k)
+
+            @pl.when(jnp.logical_not(is_here))
+            def _(copy=copy):
+                copy.start()
+
+            @pl.when(is_here)
+            def _(k=k):
+                keep = pltpu.make_async_copy(snd.at[k], self.rcv.at[self.slot], here.at[0])
+                keep.start()
+                keep.wait()
+
+    def arrive(self):
+        send, recv, _ = self.marks
+        for m in range(8):
+            arrival = pltpu.make_async_remote_copy(
+                src_ref=self.snd.at[m],
+                dst_ref=self.rcv.at[m],
+                send_sem=send.at[m],
+                recv_sem=recv.at[m],
+                device_id=self.place.partner(),
+                device_id_type=MESH,
+            )
+
+            @pl.when(jnp.logical_not(self.stays & (self.slot == m)))
+            def _(arrival=arrival):
+                arrival.wait_recv()
+
+            @pl.when(jnp.logical_not(self.stays & (self.own == m)))
+            def _(arrival=arrival):
+                arrival.wait_send()
+
+        self.home[...] = self.rcv[...]
 
 
 LANES = 384
@@ -1064,31 +1110,9 @@
     d_gate = d_gate.astype(BF)
     d_upper = d_upper.astype(BF)
     d_h_term = (contract(d_gate, gate_w, 1, 1) + contract(d_upper, up_w, 1, 1)).astype(BF)
-    d_h_ffn = x_scatter(d_h_term.reshape(4, TOK, D), 6)
-    d_w_gate = contract(h_line, d_gate, 0, 0).astype(BF)
-    d_w_up = contract(h_line, d_upper, 0, 0).astype(BF)
-    d_w_down = contract(d_ffn_line, act, 0, 0).astype(BF)
-    wide = jnp.concatenate(
-        [
-            d_w_gate.reshape(D, 2, 896),
-            d_w_up.reshape(D, 2, 896),
-            d_w_down.reshape(D, 2, 896),
-            jnp.zeros((D, 2, 128), BF),
-        ],
-        axis=2,
-    )
-    terms = wide.reshape(4, 2, 144, 2, 2, HALF).transpose(3, 0, 1, 4, 2, 5)
-    ffn_done = ffn_grads(terms, 7)
-    ffn_done = (
-        ffn_done.reshape(2, 2, 2, 32, HALF)[:, :, :, :18]
-        .transpose(3, 0, 1, 2, 4)
-        .reshape(18, 2, 2, 2 * HALF)
-        .astype(F32)
-    )
-
-    def home(which):
-        part = ffn_done[..., 896 * which : 896 * (which + 1)].reshape(18, 2, HID_PAD)
-        return part[:, :, :HID].reshape(18, 2 * HID)
+    d_h_ffn, sums = ffn_terms(
+        d_h_term.reshape(4, TOK, D), h_line.T, d_ffn_line.T, d_gate, d_upper, act, 6
+    )
 
     _, pull_ffn = jax.vjp(rms_scale, mid, norm_ffn)
     d_mid_norm, d_norm_ffn = pull_ffn(d_h_ffn)
@@ -1101,16 +1125,28 @@
     d_o_f = d_o.astype(F32)
     delta = jnp.sum(d_o_f * o_heads, axis=2) * inverse[..., 0]
     delta = jnp.concatenate([delta, jnp.zeros((4, TOK), F32)], axis=0)
-    dq_turned, d_kv = attention_backward(
+    dq_turned, d_kv, ffn_done = attention_backward(
         kv_all,
         q_all,
         (d_o_f * inv_rows).astype(BF),
         delta,
-        key_rows.reshape(4, 8, CHUNK, 1),
+        key_rows,
         row_token[None, :],
         row_first[None, :],
+        sums,
         8,
     )
+    ffn_done = (
+        ffn_done.reshape(2, 2, 2, 32, HALF)[:, :, :, :18]
+        .transpose(3, 0, 1, 2, 4)
+        .reshape(18, 2, 2, 2 * HALF)
+        .astype(F32)
+    )
+
+    def home(which):
+        part = ffn_done[..., 896 * which : 896 * (which + 1)].reshape(18, 2, HID_PAD)
+        return part[:, :, :HID].reshape(18, 2 * HID)
+
     d_q_rot = (dq_turned.transpose(2, 0, 1) * HD**-0.5).astype(BF).astype(F32)
     d_kv = d_kv.astype(BF)
     _, pull_key = jax.vjp(key_piece, k_pre, norm_key)

time: 543 us -> 446 us (0.82)
  the two profiles are of different devices: /device:TPU:97 before, /device:TPU:1 now
where the time goes in v2:
time: 446 us; the launch traced here: 438 us
  Pallas kernels  319 us (72%)
  local copies, waits for them, and re-layouts  44.8 us (10%)
  matrix products  36.7 us (8%)
  other arithmetic  35.1 us (8%)
    pallas_call x1, Pallas kernels, attention_backward(): pl.pallas_call(backward_kernel, out_shape=(shape((HEADS, HD, TOK), F32),...  100 us
    pallas_call x1, Pallas kernels, small_grads(): pl.pallas_call(small_grads_kernel, out_shape=(shape(terms.shape, BF), sha...  70.6 us
    pallas_call x1, Pallas kernels, attention_forward(): pl.pallas_call(forward_kernel, out_shape=(shape((4, 2048, 2 * HD), BF), s...  61.8 us
    pallas_call x1, Pallas kernels, ffn_terms(): pl.pallas_call(ffn_terms_kernel, out_shape=(shape((TOK, D), F32), shape(e...  29.4 us
    pallas_call x2, Pallas kernels, x_gather(): pl.pallas_call(x_gather_kernel, out_shape=jax.ShapeDtypeStruct((4, TOK, D...  28 us
    dot_general x11, matrix products, contract(): lax.dot_general(left, right, (((left_dim,), (right_dim,)), ((), ())), pre...  19.9 us
    pallas_call x1, Pallas kernels, fetch_weight(): pl.pallas_call(weight_kernel, out_shape=jax.ShapeDtypeStruct(w.shape, w.d...  15.4 us
    unnamed x162, local copies, waits for them, and re-layouts  14 us

profile of v2, /device:TPU:1, one launch (start us, length us, event | category | flops | bytes accessed | tf_op | source)
XLA Modules:
  0.0 438.2 jit_solution(17024180973620826648)
XLA Ops:
  8.6 15.4 %shard_map.289 = bf16[1152,512]{1,0:T(8,128)(2,1)} custom-call(bf16[1152,512]{1,0:T(8,128)(2,1)} %w_ref.2), custom_call_target="tpu_custom_call" | custom-call | tf_op jit(solution)/shard_map/pallas_call | solution.py:233
  24.0 2.4 multiply_reduce_fusion.9
  34.9 61.8 %shard_map.290 = (bf16[4,2048,512]{2,1,0:T(8,128)(2,1)}, bf16[4,256,256]{2,1,0:T(8,128)(2,1)}, bf16[512,1152]{1,0:T(8,128)(2,1)}, f32[4,128,256]{2,1,0:T(8,128)}, f32[4,128,128]{2,1,0:T(8,128)}) custom-call(bf16[128,512]{1,0:T(8,128)(2,1)} %pad_maximum_fusion.4.kv_ref, bf16[4,128,256]{2,1,0:T(8,128)(2,1)} %copy.124.q_ref, bf16[512,1152]{1,0:T(8,128)(2,1)} %w_ref.3, ...), custom_call_target="tpu_custom_call" | custom-call | tf_op jit(solution)/shard_map/pallas_call | solution.py:396
  104.3 15.1 %shard_map.291 = bf16[4,128,1152]{2,1,0:T(8,128)(2,1)} custom-call(bf16[128,1152]{1,0:T(8,128)(2,1)} %multiply_convert_fusion.2.rows_ref), custom_call_target="tpu_custom_call" | custom-call | tf_op jit(solution)/shard_map/pallas_call | solution.py:589
  119.4 8.1 %constant_dynamic-slice_fusion.1 = (bf16[1152,1728]{1,0:T(8,128)(2,1)S(1)}, bf16[1152,1728]{1,0:T(8,128)(2,1)S(1)}) fusion(bf16[1152,3456]{1,0:T(8,128)(2,1)} %param.26, s32[]{:T(128)S(6)} %select_n.118, bf16[1152,3456]{1,0:T(8,128)(2,1)} %param.25), kind=kLoop, calls=%fused_computation.160 | loop fusion | bytes 15925252 | tf_op jit(solution)/shard_map/dynamic_slice | solution.py:1090
  127.6 2.5 fusion.17
  131.8 4.9 %multiply_convert_fusion.1 = (bf16[512,1792]{1,0:T(8,128)(2,1)S(1)}, f32[512,1792]{1,0:T(8,128)}) fusion(f32[512,1792]{1,0:T(8,128)S(1)} %fusion.17, bf16[512,1152]{1,0:T(8,128)(2,1)S(1)} %bitcast.100, bf16[1152,1728]{1,0:T(8,128)(2,1)S(1)} %get-tuple-element.185), kind=kOutput, calls=%fused_computation.17 | convolution fusion | flops 2123104256 | bytes 14336000 | tf_op jit(solution)/shard_map/dot_general | solution.py:1098
  138.0 3.6 fusion.25
  141.6 13.9 %shard_map.292 = f32[128,1152]{1,0:T(8,128)} custom-call(bf16[4,128,1152]{2,1,0:T(8,128)(2,1)} %bitcast.114), custom_call_target="tpu_custom_call" | custom-call | tf_op jit(solution)/shard_map/pallas_call | solution.py:621
  158.6 2.2 fusion.39
  160.7 12.9 %shard_map.293 = bf16[4,128,1152]{2,1,0:T(8,128)(2,1)} custom-call(bf16[128,1152]{1,0:T(8,128)(2,1)} %get-tuple-element.146.rows_ref), custom_call_target="tpu_custom_call" | custom-call | tf_op jit(solution)/shard_map/pallas_call | solution.py:589
  173.6 8.0 %fusion.10 = (bf16[512,1792]{1,0:T(8,128)(2,1)S(1)}, bf16[512,1792]{1,0:T(8,128)(2,1)S(1)}) fusion(f32[512,1792]{1,0:T(8,128)} %copy-done.75, f32[512,1792]{1,0:T(8,128)} %get-tuple-element.179, bf16[512,1152]{1,0:T(8,128)(2,1)} %bitcast.101, bf16[1728,1152]{1,0:T(8,128)(2,1)} %copy-done.17), kind=kOutput, calls=%fused_computation.15 | convolution fusion | flops 2135949312 | bytes 16171008 | tf_op jit(solution)/shard_map/dot_general | solution.py:308
  181.7 2.6 fusion.11
  185.2 3.6 fusion.22
  188.8 2.4 copy.137
  191.2 2.4 copy.138
  193.6 29.4 %shard_map.294 = (f32[128,1152]{1,0:T(8,128)}, bf16[4,2,2,144,1408]{4,3,2,1,0:T(8,128)(2,1)}) custom-call(bf16[4,128,1152]{2,1,0:T(8,128)(2,1)} %bitcast.113, bf16[1152,512]{1,0:T(8,128)(2,1)} %bitcast.96, bf16[1152,512]{1,0:T(8,128)(2,1)} %bitcast.97, bf16[512,1792]{1,0:T(8,128)(2,1)} %copy-done.21, bf16[512,1792]{1,0:T(8,128)(2,1)} %copy-done.22, ...), custom_call_target="tpu_custom_call" | custom-call | tf_op jit(solution)/shard_map/pallas_call | solution.py:690
  224.8 2.1 multiply_reduce_fusion.1
  231.0 1.9 fusion.47
  233.5 3.0 compare_select_fusion.3
  236.6 100.3 %shard_map.295 = (f32[4,256,128]{2,1,0:T(8,128)}, f32[128,512]{1,0:T(8,128)}, bf16[8,32,1408]{2,1,0:T(8,128)(2,1)}) custom-call(bf16[4,2048,512]{2,1,0:T(8,128)(2,1)} %get-tuple-element.30.buf, bf16[4,256,256]{2,1,0:T(8,128)(2,1)} %get-tuple-element.31.q_all, bf16[4,128,256]{2,1,0:T(8,128)(2,1)} %get-tuple-element.149.do_ref, ...), custom_call_target="tpu_custom_call" | custom-call | tf_op jit(solution)/shard_map/pallas_call | solution.py:545
  344.7 3.1 pad_maximum_fusion
  348.6 70.6 %shard_map.296 = (bf16[2,1280,1152]{2,1,0:T(8,128)(2,1)}, f32[8,1152]{1,0:T(8,128)}) custom-call(bf16[2,1280,1152]{2,1,0:T(8,128)(2,1)} %bitcast.94, f32[8,1152]{1,0:T(8,128)} %stack.15.gains_ref), custom_call_target="tpu_custom_call" | custom-call | tf_op jit(solution)/shard_map/pallas_call | solution.py:981
  419.2 4.2 fusion.98
  (265 shorter events, 59.7 us)
Async XLA Ops:
  0.7 23.3 %copy-start.1 = (bf16[128,1152]{1,0:T(8,128)(2,1)S(1)}, bf16[128,1152]{1,0:T(8,128)(2,1)}, u32[]{:S(2)}) copy-start(bf16[128,1152]{1,0:T(8,128)(2,1)} %param.18) | copy-start | bytes 884740
  0.7 23.3 %copy-start.35 = (f32[1152]{0:T(1024)S(1)}, f32[1152]{0:T(1024)}, u32[]{:S(2)}) copy-start(f32[1152]{0:T(1024)} %param.28) | copy-start | bytes 13828
  0.7 23.3 %copy-start.23 = (bf16[1152,512]{1,0:T(8,128)(2,1)S(1)}, bf16[1152,512]{1,0:T(8,128)(2,1)}, u32[]{:S(2)}) copy-start(bf16[1152,512]{1,0:T(8,128)(2,1)} %w_ref.2) | copy-start | bytes 3538948
  2.0 24.4 %copy-start.47 = (f32[128]{0:T(128)}, f32[128]{0:T(128)S(1)}, u32[]{:S(2)}) copy-start(f32[128]{0:T(128)S(1)} %fusion.75) | copy-start | bytes 1540
  3.3 23.1 %copy-start.61 = (f32[128]{0:T(128)}, f32[128]{0:T(128)S(1)}, u32[]{:S(2)}) copy-start(f32[128]{0:T(128)S(1)} %multiply_power_fusion) | copy-start | bytes 1540
  4.0 22.4 %copy-start.63 = (f32[128]{0:T(128)}, f32[128]{0:T(128)S(1)}, u32[]{:S(2)}) copy-start(f32[128]{0:T(128)S(1)} %dynamic-slice_convert_fusion) | copy-start | bytes 1540
  8.6 18.6 %copy-start.51 = (f32[256]{0:T(256)S(1)}, f32[256]{0:T(256)}, u32[]{:S(2)}) copy-start(f32[256]{0:T(256)} %param.29) | copy-start | bytes 3076
  26.4 71.6 %copy-start.53 = (f32[128,4]{0,1:T(4,128)}, f32[128,4]{0,1:T(4,128)S(1)}, u32[]{:S(2)}) copy-start(f32[128,4]{0,1:T(4,128)S(1)} %get-tuple-element.174) | copy-start | bytes 6148
  27.4 70.6 %copy-start.28 = (f32[128,128]{0,1:T(8,128)}, f32[128,128]{0,1:T(8,128)S(1)}, u32[]{:S(2)}) copy-start(f32[128,128]{0,1:T(8,128)S(1)} %copy.119) | copy-start | bytes 196612
  27.5 70.5 %copy-start.30 = (f32[128,128]{0,1:T(8,128)}, f32[128,128]{0,1:T(8,128)S(1)}, u32[]{:S(2)}) copy-start(f32[128,128]{0,1:T(8,128)S(1)} %copy.118) | copy-start | bytes 196612
  127.6 9.0 %slice-start = ((s8[7962624]{0:T(1024)(128)(4,1)}), s8[4194304]{0:T(1024)(128)(4,1)S(1)}, s32[]{:S(2)}) async-start(s8[7962624]{0:T(1024)(128)(4,1)} %bitcast.111), calls=%async_computation | async-start | bytes 8388608
  138.0 18.7 %copy-start.18 = (bf16[128,1152]{1,0:T(8,128)(2,1)S(1)}, bf16[128,1152]{1,0:T(8,128)(2,1)}, u32[]{:S(2)}) copy-start(bf16[128,1152]{1,0:T(8,128)(2,1)} %param.34) | copy-start | bytes 884740
  138.0 18.7 %copy-start.40 = (f32[1152]{0:T(1024)S(1)}, f32[1152]{0:T(1024)}, u32[]{:S(2)}) copy-start(f32[1152]{0:T(1024)} %param.33) | copy-start | bytes 13828
  193.6 29.4 %copy-start.60 = (f32[128]{0:T(128)S(1)}, f32[128]{0:T(128)}, u32[]{:S(2)}) copy-start(f32[128]{0:T(128)} %copy-done.59) | copy-start | bytes 1540
  193.6 31.2 %copy-start.68 = (f32[128]{0:T(128)S(1)}, f32[128]{0:T(128)}, u32[]{:S(2)}) copy-start(f32[128]{0:T(128)} %copy-done.67) | copy-start | bytes 1540
  193.6 31.2 %copy-start.5 = (f32[128,1152]{1,0:T(8,128)S(1)}, f32[128,1152]{1,0:T(8,128)}, u32[]{:S(2)}) copy-start(f32[128,1152]{1,0:T(8,128)} %copy-done.4) | copy-start | bytes 1769476
  193.6 31.3 %copy-start.19 = (bf16[128,1152]{1,0:T(8,128)(2,1)S(1)}, bf16[128,1152]{1,0:T(8,128)(2,1)}, u32[]{:S(2)}) copy-start(bf16[128,1152]{1,0:T(8,128)(2,1)} %param.34) | copy-start | bytes 884740
  193.6 31.3 %copy-start.38 = (f32[1152]{0:T(1024)S(1)}, f32[1152]{0:T(1024)}, u32[]{:S(2)}) copy-start(f32[1152]{0:T(1024)} %param.31) | copy-start | bytes 13828
  193.6 31.3 %copy-start.56 = (f32[128]{0:T(128)S(1)}, f32[128]{0:T(128)}, u32[]{:S(2)}) copy-start(f32[128]{0:T(128)} %copy-done.55) | copy-start | bytes 1540
  236.5 101.6 %copy-start.29 = (f32[128,128]{0,1:T(8,128)S(1)}, f32[128,128]{0,1:T(8,128)}, u32[]{:S(2)}) copy-start(f32[128,128]{0,1:T(8,128)} %copy-done.28) | copy-start | bytes 196612
  236.5 101.6 %copy-start.31 = (f32[128,128]{0,1:T(8,128)S(1)}, f32[128,128]{0,1:T(8,128)}, u32[]{:S(2)}) copy-start(f32[128,128]{0,1:T(8,128)} %copy-done.30) | copy-start | bytes 196612
  236.5 101.7 %copy-start.7 = (f32[128,1024]{0,1:T(8,128)S(1)}, f32[128,1024]{0,1:T(8,128)}, u32[]{:S(2)}) copy-start(f32[128,1024]{0,1:T(8,128)} %copy-done.6) | copy-start | bytes 1572868
  236.5 101.7 %copy-start.42 = (f32[128,4]{0,1:T(4,128)S(1)}, f32[128,4]{0,1:T(4,128)}, u32[]{:S(2)}) copy-start(f32[128,4]{0,1:T(4,128)} %copy-done.41) | copy-start | bytes 6148
  236.5 101.7 %copy-start.52 = (f32[256]{0:T(256)S(1)}, f32[256]{0:T(256)}, u32[]{:S(2)}) copy-start(f32[256]{0:T(256)} %param.29) | copy-start | bytes 3076
  (54 other events, 147.5 us)

commit v3 on v2

--- a/solution.py
+++ b/solution.py
@@ -567,139 +567,270 @@
     )(kv_all, q_all, d_heads, delta, key_rows, last, first, sums)
 
 
-def x_gather_kernel(rows_ref, out_ref, send, recv):
-    place, net = Place(), Net(send, recv)
-    greet(ring(place, "x"))
-    out_ref[place.x] = rows_ref[...]
-    line = RingGather(
-        net,
-        place,
-        "x",
-        lambda j: out_ref.at[j],
-        lambda j: out_ref.at[j, pl.ds(0, TOK // 2)],
-        lambda j: out_ref.at[j, pl.ds(TOK // 2, TOK // 2)],
-    )
-    line.start()
-    line.forward()
-    line.finish()
-    net.drain()
-
-
-def x_gather(rows, call_id):
-    return pl.pallas_call(
-        x_gather_kernel,
-        out_shape=jax.ShapeDtypeStruct((4, TOK, D), BF),
-        in_specs=[IN_VMEM],
-        out_specs=IN_VMEM,
-        scratch_shapes=sems(4),
-        compiler_params=params(call_id),
-    )(rows)
-
-
-def x_scatter_kernel(terms_ref, out_ref, *rest):
-    *room, send, recv = rest
-    place, net = Place(), Net(send, recv)
-    greet(ring(place, "x"))
-    half = TOK // 2
-    line = RingScatter(
-        net,
-        place,
-        "x",
-        lambda j: terms_ref.at[j, pl.ds(0, half)],
-        lambda j: terms_ref.at[j, pl.ds(half, half)],
-        room,
-    )
-    line.start_far()
-    line.start_near()
-    line.middle()
-    line.finish(out_ref.at[pl.ds(0, half)], out_ref.at[pl.ds(half, half)])
-    net.drain()
-
-
-def x_scatter(terms, call_id):
-    half = (TOK // 2, D)
-    return pl.pallas_call(
-        x_scatter_kernel,
-        out_shape=jax.ShapeDtypeStruct((TOK, D), F32),
-        in_specs=[IN_VMEM],
-        out_specs=IN_VMEM,
-        scratch_shapes=[*RingScatter.room_shapes(half, half), *sems(6)],
-        compiler_params=params(call_id),
-    )(terms)
-
-
-def ffn_terms_kernel(
-    terms_ref, h_ref, f_ref, gate_ref, up_ref, act_ref, dh_out, sums_out, snd, got, *rest
+def norm_scale(v):
+    return lax.rsqrt(jnp.mean(v * v, axis=-1, keepdims=True) + EPS)
+
+
+def norm_back(v, r, gain, e):
+    eg = e * gain
+    dv = r * eg - v * (r * r * r) * jnp.mean(eg * v, axis=-1, keepdims=True)
+    return dv, jnp.sum(e * v * r, axis=0, keepdims=True)
+
+
+def feed_kernel(
+    x_ref,
+    o_ref,
+    inv_ref,
+    wo_ref,
+    wo2_ref,
+    gains_ref,
+    cot_ref,
+    wg_hbm,
+    wu_hbm,
+    wd_hbm,
+    out_ref,
+    dmid_out,
+    dattn_out,
+    do_out,
+    delta_out,
+    dgains_out,
+    sums_hbm,
+    wg,
+    wu,
+    wd,
+    h_line,
+    f_line,
+    h_turned,
+    f_turned,
+    gelu_kept,
+    slope_kept,
+    act,
+    d_gate,
+    d_up,
+    f_terms,
+    h_terms,
+    snd,
+    got,
+    attn,
+    mid,
+    ffn,
+    *rest,
 ):
-    *room, send, recv = rest
+    *room, send, recv, local = rest
     place, net = Place(), Net(send, recv)
     core, partner = place.core, place.partner()
+    x_hi = lax.div(place.x, 2)
+    first_unit = pl.multiple_of(x_hi * (2 * HID - HID_PAD), 128)
+    window = pl.ds(first_unit, HID_PAD)
+    loads = [
+        pltpu.make_async_copy(source, target, local.at[i])
+        for i, (source, target) in enumerate(
+            ((wg_hbm.at[:, window], wg), (wu_hbm.at[:, window], wu), (wd_hbm.at[window], wd))
+        )
+    ]
+    for load in loads:
+        load.start()
     greet(ring(place, "x") + [partner])
     half = TOK // 2
-    line = RingScatter(
-        net,
-        place,
-        "x",
-        lambda j: terms_ref.at[j, pl.ds(0, half)],
-        lambda j: terms_ref.at[j, pl.ds(half, half)],
-        room,
-    )
-    line.start_far()
-    line.start_near()
-
-    def fill(target, which):
-        columns = pl.ds(pl.multiple_of(which * 896, 128), 896)
-
-        def some_rows(i, carry):
-            rows = pl.ds(pl.multiple_of(i * 576, 64), 576)
-            pairs = ((h_ref, gate_ref), (h_ref, up_ref), (f_ref, act_ref))
-            for m, (left, right) in enumerate(pairs):
-                term = jnp.dot(left[rows], right[:, columns], preferred_element_type=F32).astype(BF)
-                for k in range(4):
-                    piece = term[144 * k : 144 * k + 144]
-                    for c in range(2):
-                        low = max(896 * m, HALF * c)
-                        high = min(896 * m + 896, HALF * c + HALF)
-                        if low < high:
-                            target[2 * i + k // 2, k % 2, c, :, low - HALF * c : high - HALF * c] = (
-                                piece[:, low - 896 * m : high - 896 * m]
-                            )
-            return carry
-
-        lax.fori_loop(0, 2, some_rows, 0)
-        for y in range(4):
-            target[y, :, 1, :, 1280:] = jnp.zeros((2, 144, 128), BF)
-
-    fill(snd, 1 - core)
+    top, bottom = pl.ds(0, half), pl.ds(half, half)
+    g_post, g_ffn, g_out = (gains_ref[i : i + 1] for i in range(3))
+
+    def gather(lines):
+        line = RingGather(
+            net,
+            place,
+            "x",
+            lambda j: lines.at[j],
+            lambda j: lines.at[j, top],
+            lambda j: lines.at[j, bottom],
+        )
+        line.start()
+        line.forward()
+        line.finish()
+
+    def scatter(terms, room):
+        line = RingScatter(
+            net, place, "x", lambda j: terms.at[j, top], lambda j: terms.at[j, bottom], room
+        )
+        line.start_far()
+        line.start_near()
+        return line
+
+    o_cat = [o_ref[h].astype(BF) for h in range(HEADS)]
+    a = jnp.dot(jnp.concatenate(o_cat[:2], axis=1), wo_ref[...], preferred_element_type=F32)
+    a += jnp.dot(jnp.concatenate(o_cat[2:], axis=1), wo2_ref[...], preferred_element_type=F32)
+    attn[...] = a
+    mid[...] = x_ref[...].astype(F32) + a * norm_scale(a) * g_post
+    m = mid[...]
+    h_line[place.x] = (m * norm_scale(m) * g_ffn).astype(BF)
+    gather(h_line)
+
+    for load in loads:
+        load.wait()
+    lines = 4 * TOK
+    low_unit, high_unit = jnp.where(x_hi == 0, 0, 64), jnp.where(x_hi == 0, HID, HID_PAD)
+
+    def units(n):
+        return pl.ds(pl.multiple_of(n * 256, 256), 256)
+
+    def forward(n, carry):
+        h = h_line[...].reshape(lines, D)
+        gate = jnp.dot(h, wg[:, units(n)], preferred_element_type=F32)
+        up = jnp.dot(h, wu[:, units(n)], preferred_element_type=F32)
+        unit = n * 256 + lax.broadcasted_iota(jnp.int32, (1, 256), 1)
+        own = jnp.where((unit >= low_unit) & (unit < high_unit), 1.0, 0.0)
+        scale, cube = 0.7978845608028654, 0.044715
+        square = gate * gate
+        bent = jnp.tanh(scale * gate * (1.0 + cube * square))
+        lifted = 0.5 * (1.0 + bent)
+        gelu = gate * lifted * own
+        slope = lifted + 0.5 * gate * (1.0 - bent * bent) * scale * (1.0 + 3.0 * cube * square)
+        act[:, units(n)] = (gelu * up).astype(BF)
+        gelu_kept[:, units(n)] = gelu.astype(BF)
+        slope_kept[:, units(n)] = (slope * up * own).astype(BF)
+        return carry
+
+    lax.fori_loop(0, HID_PAD // 256, forward, 0)
+
+    def columns(n):
+        return pl.ds(pl.multiple_of(n * 384, 128), 384)
+
+    def project(n, carry):
+        term = jnp.dot(act[...], wd[:, columns(n)], preferred_element_type=F32)
+        f_terms[:, :, columns(n)] = term.astype(BF).reshape(4, TOK, 384)
+        return carry
+
+    lax.fori_loop(0, 3, project, 0)
+    line = scatter(f_terms, room[:6])
+    h_turned[...] = jnp.transpose(h_line[...].reshape(lines, D))
+    line.middle()
+    line.finish(ffn.at[top], ffn.at[bottom])
+    f = ffn[...]
+    r_out = norm_scale(f)
+    out_ref[...] = (mid[...] + f * r_out * g_out).astype(BF)
+    df, d_out = norm_back(f, r_out, g_out, cot_ref[...].astype(F32))
+    f_line[place.x] = df.astype(BF)
+    gather(f_line)
+
+    def backward(n, carry):
+        d_act = contract(f_line[...].reshape(lines, D), wd[units(n)], 1, 1)
+        d_gate[:, units(n)] = (d_act * slope_kept[:, units(n)].astype(F32)).astype(BF)
+        d_up[:, units(n)] = (d_act * gelu_kept[:, units(n)].astype(F32)).astype(BF)
+        return carry
+
+    lax.fori_loop(0, HID_PAD // 256, backward, 0)
+
+    def back_project(n, carry):
+        term = contract(d_gate[...], wg[columns(n)], 1, 1) + contract(d_up[...], wu[columns(n)], 1, 1)
+        h_terms[:, :, columns(n)] = term.astype(BF).reshape(4, TOK, 384)
+        return carry
+
+    lax.fori_loop(0, 3, back_project, 0)
+    line = scatter(h_terms, room[6:])
+    f_turned[...] = jnp.transpose(f_line[...].reshape(lines, D))
+
+    def fill(i, which, put):
+        some = pl.ds(pl.multiple_of(which * 896, 128), 896)
+        rows = pl.ds(576 * i, 576)
+        pairs = ((h_turned, d_gate), (h_turned, d_up), (f_turned, act))
+        for m, (left, right) in enumerate(pairs):
+            term = jnp.dot(left[rows], right[:, some], preferred_element_type=F32)
+            for k in range(4):
+                piece = term[144 * k : 144 * k + 144]
+                for c in range(2):
+                    low = max(896 * m, HALF * c)
+                    high = min(896 * m + 896, HALF * c + HALF)
+                    if low < high:
+                        at = (2 * i + k // 2, k % 2, c, slice(None), slice(low - HALF * c, high - HALF * c))
+                        put(at, piece[:, low - 896 * m : high - 896 * m])
+
+    def put_snd(at, value):
+        snd[at] = value.astype(BF)
+
+    def put_got(at, value):
+        got[at] = (got[at].astype(F32) + value).astype(BF)
+
     swaps = [net.copy(snd.at[y], got.at[y], partner) for y in range(4)]
-    for swap in swaps:
-        net.go(swap)
+    for y in range(4):
+        snd[y, :, 1, :, 1280:] = jnp.zeros((2, 144, 128), BF)
+    for i in range(2):
+        fill(i, 1 - core, put_snd)
+        net.go(swaps[2 * i])
+        net.go(swaps[2 * i + 1])
     line.middle()
-    fill(sums_out, core)
-    line.finish(dh_out.at[pl.ds(0, half)], dh_out.at[pl.ds(half, half)])
-    for y, swap in enumerate(swaps):
-        swap.wait_recv()
-        add_to(sums_out.at[y], got.at[y])
+    stores = [pltpu.make_async_copy(got.at[y], sums_hbm.at[y], local.at[3 + y]) for y in range(4)]
+    for i in range(2):
+        swaps[2 * i].wait_recv()
+        swaps[2 * i + 1].wait_recv()
+        fill(i, core, put_got)
+        stores[2 * i].start()
+        stores[2 * i + 1].start()
+    line.finish(ffn.at[top], ffn.at[bottom])
+
+    m, a = mid[...], attn[...]
+    dm, d_ffn = norm_back(m, norm_scale(m), g_ffn, ffn[...])
+    d_mid = cot_ref[...].astype(F32) + dm
+    dmid_out[...] = d_mid
+    da, d_post = norm_back(a, norm_scale(a), g_post, d_mid)
+    da = da.astype(BF)
+    dattn_out[...] = da
+    dgains_out[...] = jnp.concatenate([d_post, d_ffn, d_out, jnp.zeros((5, D), F32)], axis=0)
+    delta_out[...] = jnp.zeros((8, TOK), F32)
+    for h in range(HEADS):
+        weight = (wo_ref, wo2_ref)[h // 2]
+        d_o = contract(da, weight[256 * (h % 2) : 256 * (h % 2) + 256], 1, 1).astype(BF).astype(F32)
+        inverse = inv_ref[h]
+        do_out[h] = (d_o * jnp.concatenate([inverse, inverse], axis=1)).astype(BF)
+        delta = jnp.sum(d_o * o_ref[h], axis=1, keepdims=True) * inverse
+        delta_out[h : h + 1] = jnp.transpose(delta)[:1]
+    for store in stores:
+        store.wait()
     net.drain()
 
 
-def ffn_terms(terms, h_turned, f_turned, d_gate, d_up, act, call_id):
+def feed_forward(x, o_heads, inverse, wo, wo2, gains, cotangent, w_gate, w_up, w_down, call_id):
     half = (TOK // 2, D)
     shape = jax.ShapeDtypeStruct
     every = (4, 2, 2, 144, HALF)
+    lines = 4 * TOK
+    anywhere = pl.BlockSpec(memory_space=pl.ANY)
+    unit_rows = [pltpu.VMEM((lines, HID_PAD), BF)] * 5
     return pl.pallas_call(
-        ffn_terms_kernel,
-        out_shape=(shape((TOK, D), F32), shape(every, BF)),
-        in_specs=[IN_VMEM] * 6,
-        out_specs=[IN_VMEM] * 2,
+        feed_kernel,
+        out_shape=(
+            shape((TOK, D), BF),
+            shape((TOK, D), F32),
+            shape((TOK, D), BF),
+            shape((HEADS, TOK, HD), BF),
+            shape((8, TOK), F32),
+            shape((8, D), F32),
+            shape(every, BF),
+        ),
+        in_specs=[IN_VMEM] * 7 + [anywhere] * 3,
+        out_specs=[IN_VMEM] * 6 + [anywhere],
         scratch_shapes=[
+            pltpu.VMEM((D, HID_PAD), BF),
+            pltpu.VMEM((D, HID_PAD), BF),
+            pltpu.VMEM((HID_PAD, D), BF),
+            pltpu.VMEM((4, TOK, D), BF),
+            pltpu.VMEM((4, TOK, D), BF),
+            pltpu.VMEM((D, lines), BF),
+            pltpu.VMEM((D, lines), BF),
+            *unit_rows,
+            pltpu.VMEM((4, TOK, D), BF),
+            pltpu.VMEM((4, TOK, D), BF),
             pltpu.VMEM(every, BF),
             pltpu.VMEM(every, BF),
+            pltpu.VMEM((TOK, D), F32),
+            pltpu.VMEM((TOK, D), F32),
+            pltpu.VMEM((TOK, D), F32),
             *RingScatter.room_shapes(half, half),
-            *sems(10),
+            *RingScatter.room_shapes(half, half),
+            *sems(32),
+            pltpu.SemaphoreType.DMA((7,)),
         ],
         compiler_params=params(call_id),
-    )(terms, h_turned, f_turned, d_gate, d_up, act)
+    )(x, o_heads, inverse, wo, wo2, gains, cotangent, w_gate, w_up, w_down)
 
 
 class WeightSums:
@@ -1014,10 +1145,6 @@
     )
 
 
-def glu_piece(gate_in, up_in):
-    return jax.nn.gelu(gate_in, approximate=True) * up_in
-
-
 def shards(
     layer_input,
     segment_ids,
@@ -1038,7 +1165,7 @@
     cotangent,
 ):
     sp, tp = lax.axis_index("sp"), lax.axis_index("tp")
-    core, x_hi = lax.rem(sp, 2), lax.rem(lax.div(sp, 8), 2)
+    core = lax.rem(sp, 2)
     own_start = (sp * 2 + tp) * TOK
     chip_start = lax.div(sp, 2) * 512 + tp * TOK
 
@@ -1080,55 +1207,24 @@
     kv_all, q_all, wo_other, o_heads, inverse = attention_forward(
         kv_own, q_scaled, w_out, key_rows, row_token[:, None], row_first[:, None], 2
     )
-    wo_both = jnp.concatenate([w_out, wo_other], axis=0)
     o_cat = o_heads.transpose(1, 0, 2).astype(BF).reshape(TOK, HEADS * HD)
-    attn_out = jnp.dot(o_cat, wo_both, preferred_element_type=F32)
-    mid = input_f + rms_scale(attn_out, norm_post)
-    h_ffn = rms_scale(mid, norm_ffn).astype(BF)
-
-    def units(weight, dim):
-        part = lax.dynamic_slice_in_dim(weight, x_hi * HID, HID, axis=dim)
-        pads = [(0, 0), (0, 0)]
-        pads[dim] = (0, HID_PAD - HID)
-        return jnp.pad(part, pads)
-
-    gate_w, up_w, down_w = units(w_gate, 1), units(w_up, 1), units(w_down, 0)
-    h_line = x_gather(h_ffn, 3).reshape(4 * TOK, D)
-    gate = jnp.dot(h_line, gate_w, preferred_element_type=F32)
-    upper = jnp.dot(h_line, up_w, preferred_element_type=F32)
-    act = glu_piece(gate, upper).astype(BF)
-    ffn_term = jnp.dot(act, down_w, preferred_element_type=F32).astype(BF)
-    ffn_out = x_scatter(ffn_term.reshape(4, TOK, D), 4)
-    layer_output = (mid + rms_scale(ffn_out, norm_out)).astype(BF)
-    grad_out = cotangent.astype(F32)
-    _, pull_out = jax.vjp(rms_scale, ffn_out, norm_out)
-    d_ffn_out, d_norm_out = pull_out(grad_out)
-    d_ffn_line = x_gather(d_ffn_out.astype(BF), 5).reshape(4 * TOK, D)
-    d_act = contract(d_ffn_line, down_w, 1, 1)
-    _, pull_glu = jax.vjp(glu_piece, gate, upper)
-    d_gate, d_upper = pull_glu(d_act)
-    d_gate = d_gate.astype(BF)
-    d_upper = d_upper.astype(BF)
-    d_h_term = (contract(d_gate, gate_w, 1, 1) + contract(d_upper, up_w, 1, 1)).astype(BF)
-    d_h_ffn, sums = ffn_terms(
-        d_h_term.reshape(4, TOK, D), h_line.T, d_ffn_line.T, d_gate, d_upper, act, 6
-    )
-
-    _, pull_ffn = jax.vjp(rms_scale, mid, norm_ffn)
-    d_mid_norm, d_norm_ffn = pull_ffn(d_h_ffn)
-    d_mid = grad_out + d_mid_norm
-    _, pull_post = jax.vjp(rms_scale, attn_out, norm_post)
-    d_attn_out, d_norm_post = pull_post(d_mid)
-    d_attn = d_attn_out.astype(BF)
-    d_o = contract(d_attn, wo_both, 1, 1).astype(BF).reshape(TOK, HEADS, HD).transpose(1, 0, 2)
-    inv_rows = inverse[..., :1]
-    d_o_f = d_o.astype(F32)
-    delta = jnp.sum(d_o_f * o_heads, axis=2) * inverse[..., 0]
-    delta = jnp.concatenate([delta, jnp.zeros((4, TOK), F32)], axis=0)
+    layer_output, d_mid, d_attn, d_heads, delta, d_gains, sums = feed_forward(
+        layer_input,
+        o_heads,
+        inverse,
+        w_out,
+        wo_other,
+        jnp.stack([norm_post, norm_ffn, norm_out]),
+        cotangent,
+        w_gate,
+        w_up,
+        w_down,
+        6,
+    )
     dq_turned, d_kv, ffn_done = attention_backward(
         kv_all,
         q_all,
-        (d_o_f * inv_rows).astype(BF),
+        d_heads,
         delta,
         key_rows,
         row_token[None, :],
@@ -1145,7 +1241,7 @@
 
     def home(which):
         part = ffn_done[..., 896 * which : 896 * (which + 1)].reshape(18, 2, HID_PAD)
-        return part[:, :, :HID].reshape(18, 2 * HID)
+        return jnp.concatenate([part[:, 0, :HID], part[:, 1, HID_PAD - HID :]], axis=1)
 
     d_q_rot = (dq_turned.transpose(2, 0, 1) * HD**-0.5).astype(BF).astype(F32)
     d_kv = d_kv.astype(BF)
@@ -1180,9 +1276,9 @@
     gains = jnp.stack(
         [
             d_norm_attn,
-            d_norm_post,
-            d_norm_ffn,
-            d_norm_out,
+            d_gains[0],
+            d_gains[1],
+            d_gains[2],
             jnp.concatenate([d_norm_query, d_norm_key, jnp.zeros((D - 2 * HD,), F32)]),
             *([jnp.zeros((D,), F32)] * 3),
         ]

time: 446 us -> 399 us (0.89)
  matrix products: 36.7 us -> 11.1 us
  local copies, waits for them, and re-layouts: 44.8 us -> 24.7 us
  Pallas kernels: 319 us -> 330 us
  other arithmetic: 35.1 us -> 26.5 us
    dot_general x11 -> x7, matrix products: 19.9 us -> 6.89 us  [contract(): lax.dot_general(left, right, (((left_dim,), (right_dim,)), ((), ())), pre...]
    dot_general x4 -> x0, matrix products: 11.6 us -> none  [the longest x1 4.88 us: shards(): upper = jnp.dot(h_line, up_w, preferred_element_type=F32)]
    dynamic_slice x2 -> x0, local copies, waits for them, and re-layouts: 8.46 us -> none  [units(): part = lax.dynamic_slice_in_dim(weight, x_hi * HID, HID, axis=dim)]
    reshape x5 -> x0, local copies, waits for them, and re-layouts: 7.71 us -> none  [the longest x3 2.94 us: home(): return part[:, :, :HID].reshape(18, 2 * HID)]
    pallas_call x4 -> x1, Pallas kernels: 71.2 us -> 78.9 us  [feed_forward(): pl.pallas_call(feed_kernel, out_shape=(shape((TOK, D), BF), shape((TOK, D...]
    reduce_sum x5 -> x2, other arithmetic: 6.05 us -> 0.32 us  [rms_scale(): tensor * lax.rsqrt(jnp.mean(tensor * tensor, axis=-1, keepdims=True) + EPS)]
    unnamed x162 -> x86, local copies, waits for them, and re-layouts: 14 us -> 10 us
where the time goes in v3:
time: 399 us; the launch traced here: 394 us
  Pallas kernels  330 us (83%)
  other arithmetic  26.5 us (7%)
  local copies, waits for them, and re-layouts  24.7 us (6%)
  matrix products  11.1 us (3%)
    pallas_call x1, Pallas kernels, attention_backward(): pl.pallas_call(backward_kernel, out_shape=(shape((HEADS, HD, TOK), F32),...  103 us
    pallas_call x1, Pallas kernels, feed_forward(): pl.pallas_call(feed_kernel, out_shape=(shape((TOK, D), BF), shape((TOK, D...  78.9 us
    pallas_call x1, Pallas kernels, small_grads(): pl.pallas_call(small_grads_kernel, out_shape=(shape(terms.shape, BF), sha...  71 us
    pallas_call x1, Pallas kernels, attention_forward(): pl.pallas_call(forward_kernel, out_shape=(shape((4, 2048, 2 * HD), BF), s...  61.4 us
    pallas_call x1, Pallas kernels, fetch_weight(): pl.pallas_call(weight_kernel, out_shape=jax.ShapeDtypeStruct(w.shape, w.d...  15.5 us
    unnamed x86, local copies, waits for them, and re-layouts  10 us

profile of v3, /device:TPU:1, one launch (start us, length us, event | category | flops | bytes accessed | tf_op | source)
XLA Modules:
  0.0 393.7 jit_solution(17847670666453393926)
XLA Ops:
  2.7 1.5 multiply_reduce_fusion.5
  6.1 15.5 %shard_map.289 = bf16[1152,512]{1,0:T(8,128)(2,1)} custom-call(bf16[1152,512]{1,0:T(8,128)(2,1)} %w_ref.2), custom_call_target="tpu_custom_call" | custom-call | tf_op jit(solution)/shard_map/pallas_call | solution.py:233
  21.6 2.3 multiply_reduce_fusion.2
  26.1 1.9 compare_select_fusion.6
  28.6 1.4 broadcast_add_fusion
  31.5 61.4 %shard_map.290 = (bf16[4,2048,512]{2,1,0:T(8,128)(2,1)}, bf16[4,256,256]{2,1,0:T(8,128)(2,1)}, bf16[512,1152]{1,0:T(8,128)(2,1)}, f32[4,128,256]{2,1,0:T(8,128)}, f32[4,128,128]{2,1,0:T(8,128)}) custom-call(bf16[128,512]{1,0:T(8,128)(2,1)} %pad_maximum_fusion.6.kv_ref, bf16[4,128,256]{2,1,0:T(8,128)(2,1)} %copy.115.q_ref, bf16[512,1152]{1,0:T(8,128)(2,1)} %wo_ref.1, ...), custom_call_target="tpu_custom_call" | custom-call | tf_op jit(solution)/shard_map/pallas_call | solution.py:396
  93.7 78.9 %shard_map.291 = (bf16[128,1152]{1,0:T(8,128)(2,1)}, f32[128,1152]{1,0:T(8,128)}, bf16[128,1152]{1,0:T(8,128)(2,1)}, bf16[4,128,256]{2,1,0:T(8,128)(2,1)}, f32[8...) custom-call(bf16[128,1152]{1,0:T(8,128)(2,1)} %x_ref.1, ...), custom_call_target="tpu_custom_call" | custom-call | tf_op jit(solution)/shard_map/pallas_call | solution.py:798
  172.6 3.2 compare_select_fusion.3
  175.7 102.9 %shard_map.292 = (f32[4,256,128]{2,1,0:T(8,128)}, f32[128,512]{1,0:T(8,128)}, bf16[8,32,1408]{2,1,0:T(8,128)(2,1)}) custom-call(bf16[4,2048,512]{2,1,0:T(8,128)(2,1)} %get-tuple-element.37.buf, bf16[4,256,256]{2,1,0:T(8,128)(2,1)} %get-tuple-element.38.q_all, bf16[4,128,256]{2,1,0:T(8,128)(2,1)} %get-tuple-element.39.do_ref, ...), custom_call_target="tpu_custom_call" | custom-call | tf_op jit(solution)/shard_map/pallas_call | solution.py:545
  289.5 1.2 fusion.5
  292.1 1.8 convolution_convert_fusion.1
  293.9 1.8 convert_bitcast_fusion.4
  295.7 1.8 copy.116
  298.5 1.8 convolution_convert_fusion
  301.2 3.1 pad_maximum_fusion
  304.3 71.0 %shard_map.293 = (bf16[2,1280,1152]{2,1,0:T(8,128)(2,1)}, f32[8,1152]{1,0:T(8,128)}) custom-call(bf16[2,1280,1152]{2,1,0:T(8,128)(2,1)} %bitcast.82, f32[8,1152]{1,0:T(8,128)} %stack.28.gains_ref), custom_call_target="tpu_custom_call" | custom-call | tf_op jit(solution)/shard_map/pallas_call | solution.py:1112
  375.2 4.2 %fusion.51 = (bf16[1,1024,1152]{2,1,0:T(8,128)(2,1)}, bf16[1,1024,1152]{2,1,0:T(8,128)(2,1)S(1)}) fusion(bf16[2,1280,1152]{2,1,0:T(8,128)(2,1)} %get-tuple-element.46), kind=kLoop, calls=%fused_computation.135 | loop fusion | bytes 9437184 | tf_op jit(solution)/shard_map/slice | solution.py:1297
  379.4 1.8 bitcast_convert_fusion
  381.2 1.7 copy.124
  383.7 1.7 copy.121
  385.4 1.4 convert_bitcast_fusion
  386.8 1.4 copy.122
  388.2 1.4 copy.123
  391.8 1.7 copy.154
  (156 shorter events, 25.2 us)
Async XLA Ops:
  0.6 29.3 %copy-start = (bf16[1152,256]{1,0:T(8,128)(2,1)S(1)}, bf16[1152,256]{1,0:T(8,128)(2,1)}, u32[]{:S(2)}) copy-start(bf16[1152,256]{1,0:T(8,128)(2,1)} %param.23) | copy-start | bytes 1769476
  0.7 20.9 %copy-start.1 = (bf16[128,1152]{1,0:T(8,128)(2,1)S(1)}, bf16[128,1152]{1,0:T(8,128)(2,1)}, u32[]{:S(2)}) copy-start(bf16[128,1152]{1,0:T(8,128)(2,1)} %x_ref.1) | copy-start | bytes 884740
  0.7 20.9 %copy-start.14 = (f32[1152]{0:T(1024)S(1)}, f32[1152]{0:T(1024)}, u32[]{:S(2)}) copy-start(f32[1152]{0:T(1024)} %param.28) | copy-start | bytes 13828
  0.7 20.9 %copy-start.5 = (bf16[1152,512]{1,0:T(8,128)(2,1)S(1)}, bf16[1152,512]{1,0:T(8,128)(2,1)}, u32[]{:S(2)}) copy-start(bf16[1152,512]{1,0:T(8,128)(2,1)} %w_ref.2) | copy-start | bytes 3538948
  1.6 22.4 %copy-start.29 = (f32[128]{0:T(128)}, f32[128]{0:T(128)S(1)}, u32[]{:S(2)}) copy-start(f32[128]{0:T(128)S(1)} %dynamic-slice_convert_fusion) | copy-start | bytes 1540
  2.7 3.4 copy-start.33
  4.8 281.5 %copy-start.27 = (f32[128]{0:T(128)}, f32[128]{0:T(128)S(1)}, u32[]{:S(2)}) copy-start(f32[128]{0:T(128)S(1)} %fusion.39) | copy-start | bytes 1540
  5.6 18.4 %copy-start.31 = (f32[128]{0:T(128)}, f32[128]{0:T(128)S(1)}, u32[]{:S(2)}) copy-start(f32[128]{0:T(128)S(1)} %multiply_power_fusion) | copy-start | bytes 1540
  24.0 6.3 %copy-start.22 = (f32[128,4]{0,1:T(4,128)}, f32[128,4]{0,1:T(4,128)S(1)}, u32[]{:S(2)}) copy-start(f32[128,4]{0,1:T(4,128)S(1)} %get-tuple-element.175) | copy-start | bytes 6148
  24.1 6.8 %copy-start.16 = (s32[4,8,256]{2,1,0:T(8,128)S(1)}, s32[4,8,256]{2,1,0:T(8,128)}, u32[]{:S(2)}) copy-start(s32[4,8,256]{2,1,0:T(8,128)} %constant.76.clone) | copy-start | bytes 98308
  24.3 68.7 %copy-start.24 = (f32[1152]{0:T(1024)S(1)}, f32[1152]{0:T(1024)}, u32[]{:S(2)}) copy-start(f32[1152]{0:T(1024)} %param.31) | copy-start | bytes 13828
  24.3 68.7 %copy-start.25 = (f32[1152]{0:T(1024)S(1)}, f32[1152]{0:T(1024)}, u32[]{:S(2)}) copy-start(f32[1152]{0:T(1024)} %param.32) | copy-start | bytes 13828
  24.3 68.7 %copy-start.26 = (f32[1152]{0:T(1024)S(1)}, f32[1152]{0:T(1024)}, u32[]{:S(2)}) copy-start(f32[1152]{0:T(1024)} %param.33) | copy-start | bytes 13828
  282.8 3.1 copy-start.13
  283.1 2.9 copy-start.30
  283.1 2.9 copy-start.32
  283.5 2.9 copy-start.18
  283.5 3.0 copy-start.12
  285.9 3.6 copy-start.8
  287.5 4.6 %copy-start.4 = (bf16[128,4,256]{0,2,1:T(8,128)(2,1)}, bf16[128,4,256]{0,2,1:T(8,128)(2,1)S(1)}, u32[]{:S(2)}) copy-start(bf16[128,4,256]{0,2,1:T(8,128)(2,1)S(1)} %fusion.10) | copy-start | bytes 786436
  297.5 3.2 copy-start.9
  386.8 2.8 copy-start.17
  386.8 4.0 %copy-start.34 = (f32[128]{0:T(128)S(1)}, f32[128]{0:T(128)}, u32[]{:S(2)}) copy-start(f32[128]{0:T(128)} %copy-done.33) | copy-start | bytes 1540
  388.2 2.6 copy-start.11
  (13 other events, 18.3 us)

commit v4 on v3

--- a/solution.py
+++ b/solution.py
@@ -68,6 +68,10 @@
         copy.start()
         self.started.append(copy)
 
+    def settle(self, copy):
+        copy.wait_send()
+        self.started = [other for other in self.started if other is not copy]
+
     def drain(self):
         for copy in self.started:
             copy.wait_send()
@@ -110,6 +114,25 @@
         self.on_left.wait_recv()
 
 
+class Direct:
+    def __init__(self, net, place, axis, source, landing):
+        self.net = net
+        self.copies = [
+            net.copy(
+                source(place.step(axis, by)), landing(getattr(place, axis)), place.toward(axis, by)
+            )
+            for by in (2, 1, 3)
+        ]
+
+    def start(self):
+        for copy in self.copies:
+            self.net.go(copy)
+
+    def wait(self):
+        for copy in self.copies:
+            copy.wait_recv()
+
+
 def by_rows(ref, act):
     *lead, rows, _ = ref.shape
     block = next(size for size in (64, 48, 32, 16) if rows % size == 0)
@@ -141,16 +164,19 @@
     by_rows(target, act)
 
 
+def stepped(place, axis, view):
+    return lambda by: view(place.step(axis, by))
+
+
 class RingScatter:
-    def __init__(self, net, place, axis, lo, hi, room):
-        self.net, self.lo, self.hi = net, lo, hi
-        self.me, self.nxt, self.opp, self.prev = (place.step(axis, by) for by in range(4))
+    def __init__(self, net, place, axis, lo, hi, room, lo_here=None, hi_here=None):
+        self.net, self.lo, self.hi = net, lo_here or lo, hi_here or hi
         right, left = ring(place, axis)
         self.lo1, self.lo_l, self.lo_r, self.hi1, self.hi_l, self.hi_r = room
-        self.a = net.copy(lo(self.opp), self.lo1, right)
-        self.b = net.copy(hi(self.opp), self.hi1, left)
-        self.c_hi = net.copy(hi(self.nxt), self.hi_l, right)
-        self.d_lo = net.copy(lo(self.prev), self.lo_r, left)
+        self.a = net.copy(lo(2), self.lo1, right)
+        self.b = net.copy(hi(2), self.hi1, left)
+        self.c_hi = net.copy(hi(1), self.hi_l, right)
+        self.d_lo = net.copy(lo(3), self.lo_r, left)
         self.c_lo = net.copy(self.lo1, self.lo_l, right)
         self.d_hi = net.copy(self.hi1, self.hi_r, left)
 
@@ -164,19 +190,19 @@
 
     def middle(self):
         self.a.wait_recv()
-        add_to(self.lo1, self.lo(self.nxt))
+        add_to(self.lo1, self.lo(1))
         self.net.go(self.c_lo)
         self.b.wait_recv()
-        add_to(self.hi1, self.hi(self.prev))
+        add_to(self.hi1, self.hi(3))
         self.net.go(self.d_hi)
 
     def finish(self, lo_out, hi_out):
         self.c_hi.wait_recv()
         self.d_hi.wait_recv()
-        sum_to(hi_out, [self.hi(self.me), self.hi_l, self.hi_r])
+        sum_to(hi_out, [self.hi(0), self.hi_l, self.hi_r])
         self.d_lo.wait_recv()
         self.c_lo.wait_recv()
-        sum_to(lo_out, [self.lo(self.me), self.lo_l, self.lo_r])
+        sum_to(lo_out, [self.lo(0), self.lo_l, self.lo_r])
 
     @staticmethod
     def room_shapes(lo_shape, hi_shape):
@@ -289,14 +315,17 @@
 KEY_TOKENS = key_tokens()
 
 
-def read_sets(place, buf, key_ref, chunks, by):
+def set_lead(place, n, by):
+    return place.step("zyx"[n // 3], by)
+
+
+def read_sets(buf, key_ref, chunks, leads, key_leads):
     keys, values, tokens = [], [], []
-    for n in chunks:
-        lead = place.step("zyx"[n // 3], by)
+    for n, lead, key_lead in zip(chunks, leads, key_leads):
         rows = chunk_rows(n)
         keys += [buf[lead, start : start + 64, :HD] for start in rows]
         values += [buf[lead, start : start + 64, HD:] for start in rows]
-        tokens.append(key_ref[lead, n : n + 1])
+        tokens.append(key_ref[key_lead, n : n + 1])
     return (
         jnp.concatenate(keys, axis=0),
         jnp.concatenate(values, axis=0),
@@ -308,6 +337,16 @@
     return lax.dot_general(
         left, right, (((left_dim,), (right_dim,)), ((), ())), preferred_element_type=F32
     )
+
+
+def norm_scale(v):
+    return lax.rsqrt(jnp.mean(v * v, axis=-1, keepdims=True) + EPS)
+
+
+def norm_back(v, r, gain, e):
+    eg = e * gain
+    dv = r * eg - v * (r * r * r) * jnp.mean(eg * v, axis=-1, keepdims=True)
+    return dv, jnp.sum(e * v * r, axis=0, keepdims=True)
 
 
 def forward_kernel(
@@ -361,7 +400,8 @@
     swap_q.wait_recv()
 
     def attend(by):
-        keys, values, token = read_sets(place, buf, key_ref, range(8), by)
+        leads = [set_lead(place, n, by) for n in range(8)]
+        keys, values, token = read_sets(buf, key_ref, range(8), leads, leads)
         allowed = (token <= last_ref[...]) & (token >= first_ref[...])
         for h in range(HEADS):
             weights = jnp.exp(contract(q_all[h], keys, 1, 1))
@@ -415,30 +455,113 @@
     )(kv, q, w_out, key_rows, last, first)
 
 
+GRAD_SLOT = {2: 0, 0: 0, 1: 1, 3: 2}
+
+
+def turn_back(e, cosine, sine):
+    half = HD // 2
+    low, high = e[:, :half], e[:, half:]
+    return jnp.concatenate([low * cosine + high * sine, high * cosine - low * sine], axis=1)
+
+
 def backward_kernel(
-    buf,
+    kv_hbm,
+    sums_hbm,
+    wq_hbm,
+    wq2_hbm,
+    wk_hbm,
+    wv_hbm,
     q_all,
     do_ref,
     delta_ref,
     key_ref,
     last_ref,
     first_ref,
-    sums_ref,
-    dq_out,
-    dkv_out,
-    home_out,
+    q_pre,
+    k_pre,
+    cos_ref,
+    sin_ref,
+    h_ref,
+    da_ref,
+    o_ref,
+    x_ref,
+    dmid_ref,
+    g_attn,
+    g_query,
+    g_key,
+    gains_ref,
+    dx_out,
+    dwq_out,
+    dwk_out,
+    dwv_out,
+    dwo_out,
+    dwg_out,
+    dwu_out,
+    dwd_out,
+    gains_out,
+    buf,
+    wk,
+    wv,
     do_all,
     delta_all,
     grads,
     dq_sum,
     dq_got,
+    dkv,
+    h_line,
+    da_line,
+    o_line,
+    dq_line,
+    dq_own,
+    o_own,
+    late_all,
+    late_got,
+    late_y,
+    late_z,
+    gain_got,
+    kv_own,
+    kv_line,
+    w_all,
+    w_got,
+    w_y,
+    w_z,
+    w_line,
+    w_both,
+    dh,
     *rest,
 ):
-    rooms, rest = rest[:54], rest[54:]
+    rooms, late_rooms, rest = rest[:54], rest[54:66], rest[66:]
     *weight_refs, send, recv, send2, recv2, here = rest
     place, net = Place(), Net(send, recv)
     core, partner = place.core, place.partner()
-    weights = WeightSums(place, net, sums_ref, home_out, weight_refs, (send2, recv2, here))
+    w_loads = [
+        pltpu.make_async_copy(source, target, here.at[1 + i])
+        for i, (source, target) in enumerate(
+            (
+                (wq_hbm, buf.at[0, pl.ds(0, D)]),
+                (wq2_hbm, buf.at[1, pl.ds(0, D)]),
+                (wk_hbm, wk),
+                (wv_hbm, wv),
+            )
+        )
+    ]
+    w_loads[2].start()
+    w_loads[3].start()
+
+    def set_loads(by, slot):
+        copies = []
+        for i, (_, rows, base, axes) in enumerate(PARTS):
+            span = pl.ds(base, 16 * rows)
+            source = kv_hbm.at[place.step(axes[2], by), span]
+            copies.append(
+                pltpu.make_async_copy(source, buf.at[slot, span], here.at[16 + 3 * slot + i])
+            )
+        return copies
+
+    sets = [set_loads(by, slot) for by, slot in ((2, 0), (1, 1), (3, 0), (0, 1))]
+    for copy in sets[0] + sets[1]:
+        copy.start()
+    weights = WeightSums(place, net, sums_hbm, late_z, weight_refs, (send2, recv2, here))
     greet(weights.friends + ring(place, "x") + ring(place, "y"))
     mine = pl.ds(pl.multiple_of(core * TOK, TOK), TOK)
     theirs = pl.ds(pl.multiple_of((1 - core) * TOK, TOK), TOK)
@@ -448,26 +571,101 @@
     swap_delta = net.copy(delta_all.at[core], delta_all.at[core], partner)
     net.go(swap_do)
     net.go(swap_delta)
+
+    x_lo = lax.rem(place.x, 2)
+    half = TOK // 2
+
+    def line_of(rows):
+        return RingGather(
+            net,
+            place,
+            "x",
+            lambda j: rows.at[j],
+            lambda j: rows.at[j, pl.ds(0, half)],
+            lambda j: rows.at[j, pl.ds(half, half)],
+        )
+
+    def head_of(j):
+        return jnp.where(lax.rem(j, 2) == x_lo, 0, 2) + lax.div(j, 2)
+
+    h_line[place.x] = h_ref[...]
+    da_line[place.x] = da_ref[...]
+    for h in range(HEADS):
+        o_own[h] = o_ref[h].astype(BF)
+    o_line[place.x] = o_own[head_of(place.x)]
+    line_h, line_da = line_of(h_line), line_of(da_line)
+    o_swap = Direct(net, place, "x", lambda j: o_own.at[head_of(j)], lambda j: o_line.at[j])
+    dq_swap = Direct(net, place, "x", lambda j: dq_own.at[head_of(j)], lambda j: dq_line.at[j])
+    o_swap.start()
+    line_h.start()
+    line_da.start()
     for h in range(HEADS):
         dq_sum[h] = jnp.zeros((HD, ROWS), F32)
     stages = []
     for i, part in enumerate(PARTS):
-        views = part_views(place, grads, part)
+        _, rows, base, (first, second, third) = part
+        at1, at2 = getattr(place, first), getattr(place, second)
+
+        def block(slot, start, size, base=base):
+            return grads.at[slot, pl.ds(pl.multiple_of(base + start, 16), size)]
+
+        views = (
+            lambda by, block=block, first=first, at2=at2, rows=rows: block(
+                0, (at2 * 4 + place.step(first, by)) * rows, rows
+            ),
+            lambda by, block=block, second=second, rows=rows: block(
+                0, place.step(second, by) * 4 * rows, 4 * rows
+            ),
+            lambda by, block=block, rows=rows: block(GRAD_SLOT[by], 0, 16 * rows),
+        )
         rings = []
-        for level, (axis, view) in enumerate(views):
-            at = 6 * (3 * i + level)
-            rings.append(RingScatter(net, place, axis, *halves(view), rooms[at : at + 6]))
+        for level, axis in enumerate((first, second, third)):
+            spot = 6 * (3 * i + level)
+            rings.append(
+                RingScatter(net, place, axis, *halves(views[level]), rooms[spot : spot + 6])
+            )
         stages.append((rings, views))
+    late_first = RingScatter(
+        net,
+        place,
+        "y",
+        stepped(place, "y", lambda j: late_got.at[j, 0]),
+        stepped(place, "y", lambda j: late_got.at[j, 1]),
+        late_rooms[:6],
+    )
+
+    def late_spot(j):
+        return late_y.at[lax.div(j, 2), lax.rem(j, 2)]
+
+    late_second = RingScatter(
+        net,
+        place,
+        "z",
+        stepped(place, "z", lambda j: late_spot(j).at[pl.ds(0, 80)]),
+        stepped(place, "z", lambda j: late_spot(j).at[pl.ds(80, 64)]),
+        late_rooms[6:],
+    )
+
+    def late_term(c, rows, columns):
+        term = contract(rows[...].reshape(4 * TOK, D), columns[...].reshape(4 * TOK, HD), 0, 0)
+        term = term.astype(BF)
+        for k in range(8):
+            for which in range(2):
+                late_all[which, k // 2, k % 2, c] = term[
+                    144 * k : 144 * k + 144, 128 * which : 128 * which + 128
+                ]
+
+    weights.begin()
     swap_do.wait_recv()
     swap_delta.wait_recv()
 
-    def differ(first, by):
-        chunks = range(first, first + 4)
-        keys, values, token = read_sets(place, buf, key_ref, chunks, by)
+    def differ(chunks, by, slot):
+        key_leads = [set_lead(place, n, by) for n in chunks]
+        keys, values, token = read_sets(buf, key_ref, chunks, [slot] * len(chunks), key_leads)
         token = jnp.concatenate(
             [
                 jnp.transpose(jnp.broadcast_to(token[:, 128 * i : 128 * i + 128], (128, 128)))
-                for i in range(8)
+                for i in range(2 * len(chunks))
             ],
             axis=0,
         )
@@ -486,95 +684,246 @@
             dq_sum[h] += contract(keys, d_scores, 0, 0)
         d_keys, d_values = d_keys.astype(BF), d_values.astype(BF)
         for m, n in enumerate(chunks):
-            lead = place.step("zyx"[n // 3], by)
             for i, start in enumerate(chunk_rows(n)):
-                at = 256 * m + 64 * i
-                grads[lead, start : start + 64, :HD] = d_keys[at : at + 64]
-                grads[lead, start : start + 64, HD:] = d_values[at : at + 64]
-
-    def visit(by):
-        differ(0, by)
-        differ(4, by)
-
-    weights.begin()
-    visit(2)
+                spot = 256 * m + 64 * i
+                grads[GRAD_SLOT[by], start : start + 64, :HD] = d_keys[spot : spot + 64]
+                grads[GRAD_SLOT[by], start : start + 64, HD:] = d_values[spot : spot + 64]
+
+    def visit(step, after):
+        by, slot = ((2, 0), (1, 1), (3, 0), (0, 1))[step]
+        for copy in sets[step]:
+            copy.wait()
+        for chunks in ((0, 1, 2), (3, 4, 5), (6, 7)):
+            differ(chunks, by, slot)
+        for copy in after:
+            copy.start()
+
+    visit(0, sets[2])
     for rings, _ in stages:
         rings[2].start_far()
+    line_h.forward()
+    line_da.forward()
     weights.turn()
-    lax.fori_loop(0, 2, lambda i, c: (visit(1 + 2 * i), c)[1], 0)
+    visit(1, sets[3])
+    visit(2, w_loads[0:1])
     for rings, _ in stages:
         rings[2].start_near()
     for rings, _ in stages:
         rings[2].middle()
     weights.next()
-    visit(0)
+    for rings, _ in stages:
+        net.settle(rings[2].a)
+        net.settle(rings[2].b)
+    visit(3, w_loads[1:2])
     swap_dq = net.copy(dq_sum.at[:, :, theirs], dq_got, partner)
     net.go(swap_dq)
+    line_h.finish()
+    line_da.finish()
+    o_swap.wait()
+    late_term(0, da_line, o_line)
     weights.turn_again()
+    for load in w_loads:
+        load.wait()
+
+    swap_dq.wait_recv()
+    d_query = jnp.zeros((1, HD), F32)
+    for h in range(HEADS):
+        e = jnp.transpose(dq_sum[h, :, mine] + dq_got[h]) * HD**-0.5
+        e = turn_back(e.astype(BF).astype(F32), cos_ref[...], sin_ref[...])
+        u = q_pre[h]
+        du, gain = norm_back(u, norm_scale(u), g_query[...], e)
+        d_query = d_query + gain
+        dq_own[h] = du.astype(BF)
+    dq_line[place.x] = dq_own[head_of(place.x)]
+    dq_swap.start()
     for level in (2, 1, 0):
         for (rings, views), part in zip(stages, PARTS):
-            axis, view = views[level]
-            lo, hi = halves(view)
-            me = getattr(place, axis)
+            lo, hi = halves(views[level])
             skip, rows, _, _ = part
             if level:
-                rings[level].finish(lo(me), hi(me))
+                rings[level].finish(lo(0), hi(0))
                 rings[level - 1].start_far()
                 rings[level - 1].start_near()
             else:
-                out = dkv_out.at[pl.ds(skip, rows)]
+                out = dkv.at[pl.ds(skip, rows)]
                 rings[level].finish(out.at[:, pl.ds(0, HD)], out.at[:, pl.ds(HD, HD)])
         if level == 2:
-            weights.send_home()
+            d_h = sum(
+                contract(dq_own[h], buf[h // 2, :D, 256 * (h % 2) : 256 * (h % 2) + 256], 1, 1)
+                for h in range(HEADS)
+            )
+            dh[...] = d_h
+            dq_swap.wait()
+            late_term(1, h_line, dq_line)
+            late_swap = net.copy(late_all.at[1 - core], late_got, partner)
+            net.go(late_swap)
         if level:
             for rings, _ in stages:
                 rings[level - 1].middle()
-    weights.arrive()
-    swap_dq.wait_recv()
-    for h in range(HEADS):
-        dq_out[h] = dq_sum[h, :, mine] + dq_got[h]
+        if level == 2:
+            late_swap.wait_recv()
+            for y in range(4):
+                add_to(late_got.at[y], late_all.at[core, y])
+            late_first.start_far()
+            late_first.start_near()
+            weights.last()
+        if level == 1:
+            late_first.middle()
+    late_first.finish(late_y.at[0], late_y.at[1])
+    late_second.start_far()
+    late_second.start_near()
+
+    e = turn_back(dkv[:, :HD].astype(BF).astype(F32), cos_ref[...], sin_ref[...])
+    u = k_pre[...]
+    dk, d_key = norm_back(u, norm_scale(u), g_key[...], e)
+    dk, dv = dk.astype(BF), dkv[:, HD:].astype(BF)
+    for i in range(2):
+        kv_own[i] = dk[:, 128 * i : 128 * i + 128]
+        kv_own[2 + i] = dv[:, 128 * i : 128 * i + 128]
+    kv_line[place.x] = kv_own[place.x]
+    kv_swap = Direct(net, place, "x", lambda j: kv_own.at[j], lambda j: kv_line.at[j])
+    kv_swap.start()
+    d_h = dh[...] + contract(dk, wk[...], 1, 1) + contract(dv, wv[...], 1, 1)
+    xf = x_ref[...].astype(F32)
+    dx, d_attn = norm_back(xf, norm_scale(xf), g_attn[...], d_h)
+    dx_out[...] = (dmid_ref[...] + dx).astype(BF)
+    late_second.middle()
+
+    def gain_swap(level, axis):
+        return Direct(
+            net, place, axis, lambda j: gain_got.at[level, at(axis)], lambda j: gain_got.at[level, j]
+        )
+
+    def at(axis):
+        return getattr(place, axis)
+
+    def gain_sum(level):
+        return (gain_got[level, 0] + gain_got[level, 1]) + (gain_got[level, 2] + gain_got[level, 3])
+
+    swaps = [gain_swap(0, "x"), gain_swap(1, "y"), gain_swap(2, "z")]
+    norms = jnp.concatenate([d_query, d_key, jnp.zeros((1, D - 2 * HD), F32)], axis=1)
+    gain_got[0, place.x] = jnp.concatenate(
+        [d_attn, gains_ref[0:3], norms, jnp.zeros((3, D), F32)], axis=0
+    )
+    swaps[0].start()
+    kv_swap.wait()
+    term = contract(h_line[...].reshape(4 * TOK, D), kv_line[...].reshape(4 * TOK, 128), 0, 0)
+    term = term.astype(BF)
+    for k in range(8):
+        w_all[k // 4, k % 4] = term[144 * k : 144 * k + 144]
+    w_swap = net.copy(w_all.at[1 - core], w_got, partner)
+    net.go(w_swap)
+    late_second.finish(late_z.at[pl.ds(0, 80)], late_z.at[pl.ds(80, 64)])
+    weights.send_home()
+    swaps[0].wait()
+    gain_got[1, place.y] = gain_sum(0)
+    swaps[1].start()
+    w_swap.wait_recv()
+    add_to(w_got, w_all.at[core])
+    w_scatter = Direct(net, place, "y", lambda j: w_got.at[j], lambda j: w_y.at[j])
+    w_scatter.start()
+    w_y[place.y] = w_got[place.y]
+    swaps[1].wait()
+    gain_got[2, place.z] = gain_sum(1)
+    swaps[2].start()
+    w_scatter.wait()
+    sum_to(w_z.at[place.z], [w_y.at[j] for j in range(4)])
+    w_sums = Direct(net, place, "z", lambda j: w_z.at[place.z], lambda j: w_z.at[j])
+    w_sums.start()
+    swaps[2].wait()
+    gain_got[3, core] = gain_sum(2)
+    gain_last = net.copy(gain_got.at[3, core], gain_got.at[3, core], partner)
+    net.go(gain_last)
+    w_sums.wait()
+    sum_to(w_line.at[place.x, place.y], [w_z.at[j] for j in range(4)])
+    y_back = Direct(
+        net, place, "y", lambda j: w_line.at[place.x, place.y], lambda j: w_line.at[place.x, j]
+    )
+    y_back.start()
+    weights.arrive(dwq_out, dwo_out, dwg_out, dwu_out, dwd_out)
+    y_back.wait()
+    x_back = Direct(net, place, "x", lambda j: w_line.at[place.x], lambda j: w_line.at[j])
+    x_back.start()
+    gain_last.wait_recv()
+    gains_out[...] = gain_got[3, 0] + gain_got[3, 1]
+    x_back.wait()
+    w_both[core] = w_line[...]
+    w_last = net.copy(w_line, w_both.at[core], partner)
+    net.go(w_last)
+    w_last.wait_recv()
+    for which in range(2):
+        for j in range(4):
+            out = (dwk_out, dwv_out)[j // 2]
+            for y in range(4):
+                rows = pl.ds(576 * which + 144 * y, 144)
+                out[rows, 128 * (j % 2) : 128 * (j % 2) + 128] = w_both[which, j, y].astype(F32)
     net.drain()
 
 
-def attention_backward(kv_all, q_all, d_heads, delta, key_rows, last, first, sums, call_id):
+def attention_backward(hbm, small, call_id):
     shape = jax.ShapeDtypeStruct
     rooms = []
     for _, rows, _, _ in PARTS:
         for blocks in (1, 4, 16):
             rooms += RingScatter.room_shapes((blocks * rows, HD), (blocks * rows, HD))
+    late_rooms = [
+        *RingScatter.room_shapes((2, 144, 128), (2, 144, 128)),
+        *RingScatter.room_shapes((80, 128), (64, 128)),
+    ]
     return pl.pallas_call(
         backward_kernel,
         out_shape=(
-            shape((HEADS, HD, TOK), F32),
-            shape((TOK, 2 * HD), F32),
-            shape((8, 32, HALF), BF),
+            shape((TOK, D), BF),
+            shape((18, 2 * HD), F32),
+            shape((D, HD), F32),
+            shape((D, HD), F32),
+            shape((2 * HD, 18), F32),
+            shape((18, 2 * HID), F32),
+            shape((18, 2 * HID), F32),
+            shape((2 * HID, 18), F32),
+            shape((8, D), F32),
         ),
-        in_specs=[IN_VMEM] * 8,
-        out_specs=[IN_VMEM] * 3,
+        in_specs=[pl.BlockSpec(memory_space=pl.ANY)] * 6 + [IN_VMEM] * len(small),
+        out_specs=[IN_VMEM] * 9,
         scratch_shapes=[
+            pltpu.VMEM((2, 2048, 2 * HD), BF),
+            pltpu.VMEM((D, HD), BF),
+            pltpu.VMEM((D, HD), BF),
             pltpu.VMEM((HEADS, ROWS, HD), BF),
             pltpu.VMEM((2, 8, TOK), F32),
-            pltpu.VMEM((4, 2048, 2 * HD), BF),
+            pltpu.VMEM((3, 2048, 2 * HD), BF),
             pltpu.VMEM((HEADS, HD, ROWS), F32),
             pltpu.VMEM((HEADS, HD, TOK), F32),
+            pltpu.VMEM((TOK, 2 * HD), F32),
+            pltpu.VMEM((4, TOK, D), BF),
+            pltpu.VMEM((4, TOK, D), BF),
+            pltpu.VMEM((4, TOK, HD), BF),
+            pltpu.VMEM((4, TOK, HD), BF),
+            pltpu.VMEM((4, TOK, HD), BF),
+            pltpu.VMEM((4, TOK, HD), BF),
+            pltpu.VMEM((2, 4, 2, 2, 144, 128), BF),
+            pltpu.VMEM((4, 2, 2, 144, 128), BF),
+            pltpu.VMEM((2, 2, 144, 128), BF),
+            pltpu.VMEM((144, 128), F32),
+            pltpu.VMEM((4, 4, 8, D), F32),
+            pltpu.VMEM((4, TOK, 128), BF),
+            pltpu.VMEM((4, TOK, 128), BF),
+            pltpu.VMEM((2, 4, 144, 128), BF),
+            pltpu.VMEM((4, 144, 128), BF),
+            pltpu.VMEM((4, 144, 128), BF),
+            pltpu.VMEM((4, 144, 128), BF),
+            pltpu.VMEM((4, 4, 144, 128), BF),
+            pltpu.VMEM((2, 4, 4, 144, 128), BF),
+            pltpu.VMEM((TOK, D), F32),
             *rooms,
+            *late_rooms,
             *WeightSums.scratch(),
-            *sems(96),
+            *sems(160),
             *sems(8),
-            pltpu.SemaphoreType.DMA((1,)),
+            pltpu.SemaphoreType.DMA((24,)),
         ],
         compiler_params=params(call_id),
-    )(kv_all, q_all, d_heads, delta, key_rows, last, first, sums)
-
-
-def norm_scale(v):
-    return lax.rsqrt(jnp.mean(v * v, axis=-1, keepdims=True) + EPS)
-
-
-def norm_back(v, r, gain, e):
-    eg = e * gain
-    dv = r * eg - v * (r * r * r) * jnp.mean(eg * v, axis=-1, keepdims=True)
-    return dv, jnp.sum(e * v * r, axis=0, keepdims=True)
+    )(*hbm, *small)
 
 
 def feed_kernel(
@@ -650,7 +999,12 @@
 
     def scatter(terms, room):
         line = RingScatter(
-            net, place, "x", lambda j: terms.at[j, top], lambda j: terms.at[j, bottom], room
+            net,
+            place,
+            "x",
+            stepped(place, "x", lambda j: terms.at[j, top]),
+            stepped(place, "x", lambda j: terms.at[j, bottom]),
+            room,
         )
         line.start_far()
         line.start_near()
@@ -834,9 +1188,9 @@
 
 
 class WeightSums:
-    def __init__(self, place, net, sums, home, refs, marks):
-        y1, z1, z2, y2, snd, rcv, *rooms = refs
-        self.place, self.home, self.snd, self.rcv, self.marks = place, home, snd, rcv, marks
+    def __init__(self, place, net, sums, late, refs, marks):
+        y_here, z_here, y1, z1, z2, y2, snd, rcv, *rooms = refs
+        self.place, self.late, self.snd, self.rcv, self.marks = place, late, snd, rcv, marks
         self.y1, self.z1, self.y2, self.z2 = y1, z1, y2, z2
         self.x_hi, self.x_lo = lax.div(place.x, 2), lax.rem(place.x, 2)
         self.friends = []
@@ -847,42 +1201,63 @@
 
         left, right = pl.ds(0, CUT), pl.ds(CUT, HALF - CUT)
 
-        def z_spot(j):
-            return sums.at[:, lax.div(j, 2), lax.rem(j, 2), :, right]
-
-        def then_z(j):
-            return y1.at[lax.div(j, 2), lax.rem(j, 2)]
-
+        def y_spot(half):
+            return stepped(place, "y", lambda j: sums.at[j, half, :, :, left])
+
+        def z_spot(half):
+            return stepped(
+                place,
+                "z",
+                lambda j: sums.at[pl.ds(2 * half, 2), lax.div(j, 2), lax.rem(j, 2), :, right],
+            )
+
+        self.loads = []
+        here = []
+        for i, spot in enumerate((y_spot, z_spot)):
+            for k, (half, by) in enumerate(((0, 1), (1, 3), (0, 0), (1, 0))):
+                target = (y_here, z_here)[i].at[k]
+                here.append(target)
+                self.loads.append(
+                    pltpu.make_async_copy(spot(half)(by), target, marks[2].at[8 + 4 * i + k])
+                )
         self.y_first = RingScatter(
             net,
             place,
             "y",
-            lambda j: sums.at[j, 0, :, :, left],
-            lambda j: sums.at[j, 1, :, :, left],
+            y_spot(0),
+            y_spot(1),
             rooms[0:6],
+            {1: here[0], 0: here[2]}.get,
+            {3: here[1], 0: here[3]}.get,
         )
         self.z_first = RingScatter(
             net,
             place,
             "z",
-            lambda j: z_spot(j).at[pl.ds(0, 2)],
-            lambda j: z_spot(j).at[pl.ds(2, 2)],
+            z_spot(0),
+            z_spot(1),
             rooms[6:12],
+            {1: here[4], 0: here[6]}.get,
+            {3: here[5], 0: here[7]}.get,
         )
+
+        def then_z(j):
+            return y1.at[lax.div(j, 2), lax.rem(j, 2)]
+
         self.z_second = RingScatter(
             net,
             place,
             "z",
-            lambda j: then_z(j).at[:, pl.ds(0, 384)],
-            lambda j: then_z(j).at[:, pl.ds(384, 384)],
+            stepped(place, "z", lambda j: then_z(j).at[:, pl.ds(0, 384)]),
+            stepped(place, "z", lambda j: then_z(j).at[:, pl.ds(384, 384)]),
             rooms[12:18],
         )
         self.y_second = RingScatter(
             net,
             place,
             "y",
-            lambda j: z1.at[j, :, pl.ds(0, 384)],
-            lambda j: z1.at[j, :, pl.ds(384, 256)],
+            stepped(place, "y", lambda j: z1.at[j, :, pl.ds(0, 384)]),
+            stepped(place, "y", lambda j: z1.at[j, :, pl.ds(384, 256)]),
             rooms[18:24],
         )
 
@@ -890,12 +1265,14 @@
     def scratch():
         rest = HALF - CUT
         return [
+            pltpu.VMEM((4, 2, 144, CUT), BF),
+            pltpu.VMEM((4, 2, 144, rest), BF),
             pltpu.VMEM((2, 2, 144, CUT), BF),
             pltpu.VMEM((4, 144, rest), BF),
             pltpu.VMEM((144, CUT), F32),
             pltpu.VMEM((144, rest), F32),
-            pltpu.VMEM((8, 32, HALF), BF),
-            pltpu.VMEM((8, 32, HALF), BF),
+            pltpu.VMEM((8, 32, HALF + 128), BF),
+            pltpu.VMEM((8, 32, HALF + 128), BF),
             *RingScatter.room_shapes((2, 144, CUT), (2, 144, CUT)),
             *RingScatter.room_shapes((2, 144, rest), (2, 144, rest)),
             *RingScatter.room_shapes((144, 384), (144, 384)),
@@ -903,11 +1280,15 @@
         ]
 
     def begin(self):
+        for load in self.loads:
+            load.start()
         for line in (self.y_first, self.z_first):
             line.start_far()
             line.start_near()
 
     def turn(self):
+        for load in self.loads:
+            load.wait()
         self.y_first.middle()
         self.z_first.middle()
 
@@ -923,12 +1304,15 @@
         self.z_second.middle()
         self.y_second.middle()
 
-    def send_home(self):
-        z2, y2, snd = self.z2, self.y2, self.snd
+    def last(self):
+        z2, y2 = self.z2, self.y2
         self.z_second.finish(z2.at[:, pl.ds(0, 384)], z2.at[:, pl.ds(384, 384)])
         self.y_second.finish(y2.at[:, pl.ds(0, 384)], y2.at[:, pl.ds(384, 256)])
-        total = jnp.concatenate([z2[...], y2[...]], axis=1)
-        blank = jnp.zeros((14, HALF), F32)
+
+    def send_home(self):
+        snd = self.snd
+        total = jnp.concatenate([self.z2[...], self.y2[...], self.late[...]], axis=1)
+        blank = jnp.zeros((14, HALF + 128), F32)
         for k in range(8):
             snd[k] = jnp.concatenate([total[18 * k : 18 * k + 18], blank], axis=0).astype(BF)
         place = self.place
@@ -958,7 +1342,7 @@
                 keep.start()
                 keep.wait()
 
-    def arrive(self):
+    def arrive(self, dwq, dwo, dwg, dwu, dwd):
         send, recv, _ = self.marks
         for m in range(8):
             arrival = pltpu.make_async_remote_copy(
@@ -978,151 +1362,33 @@
             def _(arrival=arrival):
                 arrival.wait_send()
 
-        self.home[...] = self.rcv[...]
-
-
-LANES = 384
-ORDERS = (("x", "y", "z"), ("y", "z", "x"), ("z", "x", "y"))
-
-
-def small_grads_kernel(terms_ref, gains_ref, out_ref, gains_out, got, sums, gain_got, *rest):
-    *rooms, send, recv = rest
-    place, net = Place(), Net(send, recv)
-    core, partner = place.core, place.partner()
-    greet(ring(place, "x") + ring(place, "y") + ring(place, "z") + [partner])
-    swap = net.copy(terms_ref.at[1 - core], got, partner)
-    gain_got[0, core] = gains_ref[...]
-    gain_swap = net.copy(gain_got.at[0, core], gain_got.at[0, core], partner)
-    net.go(gain_swap)
-    net.go(swap)
-
-    def gain_ring(level, axis):
-        return RingGather(
-            net,
-            place,
-            axis,
-            lambda j: gain_got.at[level, j],
-            lambda j: gain_got.at[level, j, :, pl.ds(0, 512)],
-            lambda j: gain_got.at[level, j, :, pl.ds(512, 640)],
-        )
-
-    gain_lines = [gain_ring(1, "x"), gain_ring(2, "y"), gain_ring(3, "z")]
-    gain_swap.wait_recv()
-    gain_got[1, place.x] = gain_got[0, 0] + gain_got[0, 1]
-    gain_lines[0].start()
-
-    rows = out_ref.at[core]
-    scatters, gathers = [], []
-    for p, (first, second, third) in enumerate(ORDERS):
-        lanes = pl.ds(LANES * p, LANES)
-        at1, at2, at3 = (getattr(place, axis) for axis in (first, second, third))
-
-        def views(ref, lanes=lanes, at1=at1):
-            def piece(start, size):
-                return ref.at[pl.ds(pl.multiple_of(start, 16), size), lanes]
-
-            return (
-                lambda j: piece(320 * j, 320),
-                lambda j: piece(320 * j, 160),
-                lambda j: piece(320 * j + 160, 160),
-                lambda j: piece(320 * at1 + 80 * j, 80),
-                lambda j: piece(320 * at1 + 80 * j, 48),
-                lambda j: piece(320 * at1 + 80 * j + 48, 32),
-            )
-
-        _, lo1, hi1, term2, lo2, hi2 = views(got)
-        room = rooms[12 * p : 12 * p + 12]
-        scatters.append(
-            (
-                (RingScatter(net, place, first, lo1, hi1, room[:6]), lo1, hi1, at1),
-                (RingScatter(net, place, second, lo2, hi2, room[6:]), lo2, hi2, at2),
-            )
-        )
-        spot = sums.at[p]
-        last = RingGather(
-            net,
-            place,
-            third,
-            lambda j, spot=spot: spot.at[j],
-            lambda j, spot=spot: spot.at[j, pl.ds(0, 48)],
-            lambda j, spot=spot: spot.at[j, pl.ds(48, 32)],
-        )
-        whole1, whole_lo1, whole_hi1, whole2, whole_lo2, whole_hi2 = views(rows)
-        gathers.append(
-            (
-                last,
-                RingGather(net, place, second, whole2, whole_lo2, whole_hi2),
-                RingGather(net, place, first, whole1, whole_lo1, whole_hi1),
-                term2(at2),
-                whole2(at2),
-                at3,
-            )
-        )
-    swap.wait_recv()
-    add_to(got, terms_ref.at[core])
-    for level in (0, 1):
-        for pair in scatters:
-            pair[level][0].start_far()
-            pair[level][0].start_near()
-        for pair in scatters:
-            pair[level][0].middle()
-        gain_lines[level].forward()
-        for pair in scatters:
-            line, lo, hi, at = pair[level]
-            line.finish(lo(at), hi(at))
-        gain_lines[level].finish()
-        nxt = place.y if level == 0 else place.z
-        gain_got[level + 2, nxt] = (gain_got[level + 1, 0] + gain_got[level + 1, 1]) + (
-            gain_got[level + 1, 2] + gain_got[level + 1, 3]
-        )
-        gain_lines[level + 1].start()
-    for p, (last, _, _, term, _, at3) in enumerate(gathers):
-        sums[p, at3] = term[...]
-        last.start()
-    for last, *_ in gathers:
-        last.forward()
-    gain_lines[2].forward()
-    for p, (last, second, _, _, own, _) in enumerate(gathers):
-        last.finish()
-        sum_to(own, [sums.at[p, j] for j in range(4)])
-        second.start()
-    for _, second, *_ in gathers:
-        second.forward()
-    for _, second, first, *_ in gathers:
-        second.finish()
-        first.start()
-    for _, _, first, *_ in gathers:
-        first.forward()
-    gain_lines[2].finish()
-    gains_out[...] = (gain_got[3, 0] + gain_got[3, 1]) + (gain_got[3, 2] + gain_got[3, 3])
-    for _, _, first, *_ in gathers:
-        first.finish()
-    final = net.copy(rows, rows, partner)
-    net.go(final)
-    final.wait_recv()
-    net.drain()
-
-
-def small_grads(terms, gains, call_id):
-    shape = jax.ShapeDtypeStruct
-    rooms = []
-    for _ in ORDERS:
-        rooms += RingScatter.room_shapes((160, LANES), (160, LANES))
-        rooms += RingScatter.room_shapes((48, LANES), (32, LANES))
-    return pl.pallas_call(
-        small_grads_kernel,
-        out_shape=(shape(terms.shape, BF), shape(gains.shape, F32)),
-        in_specs=[IN_VMEM] * 2,
-        out_specs=[IN_VMEM] * 2,
-        scratch_shapes=[
-            pltpu.VMEM((1280, D), BF),
-            pltpu.VMEM((3, 4, 80, LANES), BF),
-            pltpu.VMEM((4, 4, 8, D), F32),
-            *rooms,
-            *sems(96),
-        ],
-        compiler_params=params(call_id),
-    )(terms, gains)
+        def tile(x_hi, n):
+            core, n = (n % 14) // 7, (n // 14) * 7 + n % 7
+            c, n = n // 11, n % 11
+            return self.rcv[x_hi * 4 + core * 2 + c, :, 128 * n : 128 * n + 128].astype(F32)[:24]
+
+        def turned(value):
+            value = jnp.concatenate([value, jnp.zeros((104, 128), F32)], axis=0)
+            return jnp.transpose(value)[:, :18]
+
+        for which, out in enumerate((dwg, dwu, dwd)):
+            for n in range(27):
+                value = None
+                for x_hi in range(2):
+                    if 0 <= n - 13 * x_hi < 14:
+                        term = tile(x_hi, 14 * which + n - 13 * x_hi)
+                        value = term if value is None else value + term
+                span = slice(128 * n, 128 * n + 128)
+                if which < 2:
+                    out[:, span] = value[:18]
+                else:
+                    out[span] = turned(value)
+        for x_hi in range(2):
+            for core in range(2):
+                at = x_hi * 4 + core * 2
+                span = slice(128 * (at // 2), 128 * (at // 2) + 128)
+                dwo[span] = turned(self.rcv[at, :, HALF:].astype(F32)[:24])
+                dwq[:, span] = self.rcv[at + 1, :, HALF:].astype(F32)[:18]
 
 
 def rms_scale(tensor, scaling):
@@ -1207,7 +1473,6 @@
     kv_all, q_all, wo_other, o_heads, inverse = attention_forward(
         kv_own, q_scaled, w_out, key_rows, row_token[:, None], row_first[:, None], 2
     )
-    o_cat = o_heads.transpose(1, 0, 2).astype(BF).reshape(TOK, HEADS * HD)
     layer_output, d_mid, d_attn, d_heads, delta, d_gains, sums = feed_forward(
         layer_input,
         o_heads,
@@ -1221,83 +1486,41 @@
         w_down,
         6,
     )
-    dq_turned, d_kv, ffn_done = attention_backward(
-        kv_all,
-        q_all,
-        d_heads,
-        delta,
-        key_rows,
-        row_token[None, :],
-        row_first[None, :],
-        sums,
+    d_input, d_wq, d_wk, d_wv, d_wo, d_wg, d_wu, d_wd, gains = attention_backward(
+        (kv_all, sums, w_query, wq_other, w_key, w_value),
+        (
+            q_all,
+            d_heads,
+            delta,
+            key_rows,
+            row_token[None, :],
+            row_first[None, :],
+            q_pre.transpose(1, 0, 2),
+            k_pre,
+            cosine,
+            sine,
+            h_attn,
+            d_attn,
+            o_heads,
+            layer_input,
+            d_mid,
+            norm_attn[None, :],
+            norm_query[None, :],
+            norm_key[None, :],
+            d_gains,
+        ),
         8,
     )
-    ffn_done = (
-        ffn_done.reshape(2, 2, 2, 32, HALF)[:, :, :, :18]
-        .transpose(3, 0, 1, 2, 4)
-        .reshape(18, 2, 2, 2 * HALF)
-        .astype(F32)
-    )
-
-    def home(which):
-        part = ffn_done[..., 896 * which : 896 * (which + 1)].reshape(18, 2, HID_PAD)
-        return jnp.concatenate([part[:, 0, :HID], part[:, 1, HID_PAD - HID :]], axis=1)
-
-    d_q_rot = (dq_turned.transpose(2, 0, 1) * HD**-0.5).astype(BF).astype(F32)
-    d_kv = d_kv.astype(BF)
-    _, pull_key = jax.vjp(key_piece, k_pre, norm_key)
-    d_k_pre, d_norm_key = pull_key(d_kv[:, :HD].astype(F32))
-    d_k_pre = d_k_pre.astype(BF)
-    d_value = d_kv[:, HD:]
-    _, pull_query = jax.vjp(query_piece, q_pre, norm_query)
-    d_q_pre, d_norm_query = pull_query(d_q_rot)
-    d_q_pre = d_q_pre.reshape(TOK, HEADS * HD).astype(BF)
-    d_h_attn = (
-        contract(d_q_pre, wq_both, 1, 1)
-        + contract(d_k_pre, w_key, 1, 1)
-        + contract(d_value, w_value, 1, 1)
-    )
-    _, pull_attn = jax.vjp(rms_scale, input_f, norm_attn)
-    d_input_norm, d_norm_attn = pull_attn(d_h_attn)
-    d_input = (d_mid + d_input_norm).astype(BF)
-
-    def in_order(both):
-        return jnp.where(tp == 0, both, jnp.roll(both, 2 * HD, axis=1))
-
-    small = jnp.concatenate(
-        [
-            contract(in_order(d_q_pre), h_attn, 0, 0),
-            contract(d_k_pre, h_attn, 0, 0),
-            contract(in_order(o_cat), d_attn, 0, 0),
-            contract(d_value, h_attn, 0, 0),
-        ],
-        axis=0,
-    ).astype(BF)
-    gains = jnp.stack(
-        [
-            d_norm_attn,
-            d_gains[0],
-            d_gains[1],
-            d_gains[2],
-            jnp.concatenate([d_norm_query, d_norm_key, jnp.zeros((D - 2 * HD,), F32)]),
-            *([jnp.zeros((D,), F32)] * 3),
-        ]
-    )
-    small, gains = small_grads(small.reshape(2, 1280, D), gains, 9)
-
-    def cut(matrix):
-        return lax.dynamic_slice(matrix, (tp * 512, sp * 18), (512, 18)).astype(F32)
-
     return (
         layer_output,
         d_input,
-        cut(small[0, :1024]).T,
-        small[0, 1024:].astype(F32).T,
-        small[1, 1024:].astype(F32).T,
-        cut(small[1, :1024]),
-        home(0),
-        home(1),
-        home(2).T,
+        d_wq,
+        d_wk,
+        d_wv,
+        d_wo,
+        d_wg,
+        d_wu,
+        d_wd,
         gains[0],
         gains[4, :HD],
         gains[4, HD : 2 * HD],

time: 399 us -> 329 us (0.82)
  Pallas kernels: 330 us -> 292 us
  other arithmetic: 26.5 us -> 13.1 us
  local copies, waits for them, and re-layouts: 24.7 us -> 13.5 us
  matrix products: 11.1 us -> 4.05 us
    pallas_call x2 -> x1, Pallas kernels: 174 us -> 136 us  [attention_backward(): pl.pallas_call(backward_kernel, out_shape=(shape((TOK, D), BF), shape((18...]
    slice x8 -> x0, local copies, waits for them, and re-layouts: 7.02 us -> none  [the longest x1 4.18 us: shards(): small[1, :1024]]
    dot_general x7 -> x0, matrix products: 6.89 us -> none  [contract(): lax.dot_general(left, right, (((left_dim,), (right_dim,)), ((), ())), pre...]
    convert_element_type x9 -> x1, other arithmetic: 5.93 us -> 1.11 us  [shards(): h_attn = rms_scale(input_f, norm_attn).astype(BF)]
    concatenate x4 -> x0, other arithmetic: 4.79 us -> none  [the longest x1 3.1 us: shards(): jnp.concatenate([contract(in_order(d_q_pre), h_attn, 0, 0), contract(d_k_...]
    unnamed x86 -> x55, local copies, waits for them, and re-layouts: 10 us -> 10.4 us
where the time goes in v4:
time: 329 us; the launch traced here: 324 us
  Pallas kernels  292 us (89%)
  local copies, waits for them, and re-layouts  13.5 us (4%)
  other arithmetic  13.1 us (4%)
  matrix products  4.05 us (1%)
    pallas_call x1, Pallas kernels, attention_backward(): pl.pallas_call(backward_kernel, out_shape=(shape((TOK, D), BF), shape((18...  136 us
    pallas_call x1, Pallas kernels, feed_forward(): pl.pallas_call(feed_kernel, out_shape=(shape((TOK, D), BF), shape((TOK, D...  79 us
    pallas_call x1, Pallas kernels, attention_forward(): pl.pallas_call(forward_kernel, out_shape=(shape((4, 2048, 2 * HD), BF), s...  61.4 us
    pallas_call x1, Pallas kernels, fetch_weight(): pl.pallas_call(weight_kernel, out_shape=jax.ShapeDtypeStruct(w.shape, w.d...  15.4 us
    unnamed x55, local copies, waits for them, and re-layouts  10.4 us

profile of v4, /device:TPU:1, one launch (start us, length us, event | category | flops | bytes accessed | tf_op | source)
XLA Modules:
  0.0 323.6 jit_solution(872547183357052499)
XLA Ops:
  0.7 1.2 fusion.4
  1.8 1.1 fusion.6.h_ref
  3.0 1.4 convolution_convert_fusion
  4.4 0.8 dynamic-slice_convert_fusion
  6.0 0.7 pad_maximum_fusion.kv_ref
  6.7 15.4 %shard_map.289.wq2_hbm = bf16[1152,512]{1,0:T(8,128)(2,1)} custom-call(bf16[1152,512]{1,0:T(8,128)(2,1)} %wq_hbm.1), custom_call_target="tpu_custom_call" | custom-call | tf_op jit(solution)/shard_map/pallas_call | solution.py:259
  22.1 2.3 multiply_reduce_fusion
  24.9 0.8 fusion.7.q_ref
  27.6 1.9 compare_select_fusion.6
  29.7 1.4 broadcast_add_fusion
  31.1 61.4 %shard_map.290 = (bf16[4,2048,512]{2,1,0:T(8,128)(2,1)}, bf16[4,256,256]{2,1,0:T(8,128)(2,1)}, bf16[512,1152]{1,0:T(8,128)(2,1)}, f32[4,128,256]{2,1,0:T(8,128)}, f32[4,128,128]{2,1,0:T(8,128)}) custom-call(bf16[128,512]{1,0:T(8,128)(2,1)} %pad_maximum_fusion.kv_ref, bf16[4,128,256]{2,1,0:T(8,128)(2,1)} %fusion.7.q_ref, bf16[512,1152]{1,0:T(8,128)(2,1)} %wo_ref.1, ...), custom_call_target="tpu_custom_call" | custom-call | tf_op jit(solution)/shard_map/pallas_call | solution.py:436
  92.5 0.6 pad_maximum_fusion.1.gains_ref
  93.2 79.0 %shard_map.291 = (bf16[128,1152]{1,0:T(8,128)(2,1)}, f32[128,1152]{1,0:T(8,128)}, bf16[128,1152]{1,0:T(8,128)(2,1)}, bf16[4,128,256]{2,1,0:T(8,128)(2,1)}, f32[8...) custom-call(bf16[128,1152]{1,0:T(8,128)(2,1)} %x_ref.3, ...), custom_call_target="tpu_custom_call" | custom-call | tf_op jit(solution)/shard_map/pallas_call | solution.py:1152
  172.2 3.2 compare_select_fusion.3
  175.9 135.9 %shard_map.292 = (bf16[128,1152]{1,0:T(8,128)(2,1)}, f32[18,512]{1,0:T(8,128)}, f32[1152,256]{1,0:T(8,128)}, f32[1152,256]{1,0:T(8,128)}, f32[512,18]{1,0:T(8,12...) custom-call(bf16[4,2048,512]{2,1,0:T(8,128)(2,1)} %get-tuple-element.40.kv_hbm, ...), custom_call_target="tpu_custom_call" | custom-call | tf_op jit(solution)/shard_map/pallas_call | solution.py:873
  311.9 1.7 copy.85
  313.6 2.8 copy.86
  316.5 0.6 slice_reduce_fusion
  317.7 0.7 copy.100
  318.4 0.7 copy.101
  319.7 1.0 copy.103
  320.8 1.0 copy.104
  321.9 0.7 copy.105
  322.6 0.7 copy.106
  (75 shorter events, 5.3 us)
Async XLA Ops:
  0.6 4.5 %copy-start.3 = (bf16[1152,256]{1,0:T(8,128)(2,1)S(1)}, bf16[1152,256]{1,0:T(8,128)(2,1)}, u32[]{:S(2)}) copy-start(bf16[1152,256]{1,0:T(8,128)(2,1)} %wk_hbm.1) | copy-start | bytes 1769476
  0.7 4.9 %copy-start.21 = (f32[256]{0:T(256)S(1)}, f32[256]{0:T(256)}, u32[]{:S(2)}) copy-start(f32[256]{0:T(256)} %param.30) | copy-start | bytes 3076
  2.9 19.1 %copy-start.2 = (bf16[128,1152]{1,0:T(8,128)(2,1)}, bf16[128,1152]{1,0:T(8,128)(2,1)S(1)}, u32[]{:S(2)}) copy-start(bf16[128,1152]{1,0:T(8,128)(2,1)S(1)} %fusion.6.h_ref) | copy-start | bytes 884740
  5.5 18.9 %copy-start.4 = (f32[128,256]{1,0:T(8,128)}, f32[128,256]{1,0:T(8,128)S(1)}, u32[]{:S(2)}) copy-start(f32[128,256]{1,0:T(8,128)S(1)} %get-tuple-element.155.k_pre) | copy-start | bytes 393220
  5.5 16.6 %copy-start.1 = (bf16[1152,512]{1,0:T(8,128)(2,1)S(1)}, bf16[1152,512]{1,0:T(8,128)(2,1)}, u32[]{:S(2)}) copy-start(bf16[1152,512]{1,0:T(8,128)(2,1)} %wq_hbm.1) | copy-start | bytes 3538948
  6.0 18.8 %copy-start.7 = (f32[128,128]{1,0:T(8,128)}, f32[128,128]{1,0:T(8,128)S(1)}, u32[]{:S(2)}) copy-start(f32[128,128]{1,0:T(8,128)S(1)} %get-tuple-element.146.cos_ref) | copy-start | bytes 196612
  6.0 18.8 %copy-start.8 = (f32[128,128]{1,0:T(8,128)}, f32[128,128]{1,0:T(8,128)S(1)}, u32[]{:S(2)}) copy-start(f32[128,128]{1,0:T(8,128)S(1)} %get-tuple-element.147.sin_ref) | copy-start | bytes 196612
  22.1 2.6 copy-start.22
  24.4 1.3 copy-start.16
  24.4 2.1 copy-start.13
  24.6 6.5 %copy-start = (f32[128,4,256]{2,0,1:T(8,128)}, f32[128,4,256]{2,0,1:T(8,128)S(1)}, u32[]{:S(2)}) copy-start(f32[128,4,256]{2,0,1:T(8,128)S(1)} %copy.79) | copy-start | bytes 1572868
  24.9 67.6 %copy-start.18 = (f32[1152]{0:T(1024)S(1)}, f32[1152]{0:T(1024)}, u32[]{:S(2)}) copy-start(f32[1152]{0:T(1024)} %param.33) | copy-start | bytes 13828
  24.9 67.6 %copy-start.19 = (f32[1152]{0:T(1024)S(1)}, f32[1152]{0:T(1024)}, u32[]{:S(2)}) copy-start(f32[1152]{0:T(1024)} %param.32) | copy-start | bytes 13828
  24.9 67.6 %copy-start.20 = (f32[1152]{0:T(1024)S(1)}, f32[1152]{0:T(1024)}, u32[]{:S(2)}) copy-start(f32[1152]{0:T(1024)} %param.31) | copy-start | bytes 13828
  93.2 82.2 %copy-start.15 = (f32[1152]{0:T(1024)S(1)}, f32[1152]{0:T(1024)}, u32[]{:S(2)}) copy-start(f32[1152]{0:T(1024)} %param.28) | copy-start | bytes 13828
  311.8 4.6 %copy-start.17 = (f32[8,1152]{1,0:T(8,128)S(1)}, f32[8,1152]{1,0:T(8,128)}, u32[]{:S(2)}) copy-start(f32[8,1152]{1,0:T(8,128)} %get-tuple-element.56) | copy-start | bytes 110596
  311.8 5.8 %copy-start.11 = (bf16[128,1152]{1,0:T(8,128)(2,1)S(1)}, bf16[128,1152]{1,0:T(8,128)(2,1)}, u32[]{:S(2)}) copy-start(bf16[128,1152]{1,0:T(8,128)(2,1)} %get-tuple-element.177) | copy-start | bytes 884740
  311.8 6.6 %copy-start.12 = (bf16[128,1152]{1,0:T(8,128)(2,1)S(1)}, bf16[128,1152]{1,0:T(8,128)(2,1)}, u32[]{:S(2)}) copy-start(bf16[128,1152]{1,0:T(8,128)(2,1)} %get-tuple-element.178) | copy-start | bytes 884740
  311.9 7.3 %copy-start.14 = (f32[18,512]{1,0:T(8,128)S(1)}, f32[18,512]{1,0:T(8,128)}, u32[]{:S(2)}) copy-start(f32[18,512]{1,0:T(8,128)} %get-tuple-element.179) | copy-start | bytes 110596
  313.6 6.1 %copy-start.6 = (f32[1152,256]{1,0:T(8,128)S(1)}, f32[1152,256]{1,0:T(8,128)}, u32[]{:S(2)}) copy-start(f32[1152,256]{1,0:T(8,128)} %get-tuple-element.180) | copy-start | bytes 3538948
  317.7 3.1 copy-start.5
  320.7 1.2 copy-start.10
  320.8 1.9 copy-start.9

commit v5 on v4

--- a/solution.py
+++ b/solution.py
@@ -78,10 +78,12 @@
         self.started = []
 
 
-def greet(devices):
+def greet(devices, meanwhile=None):
     barrier = pltpu.get_barrier_semaphore()
     for device in devices:
         pl.semaphore_signal(barrier, inc=1, device_id=device, device_id_type=MESH)
+    if meanwhile is not None:
+        meanwhile()
     pl.semaphore_wait(barrier, len(devices))
 
 
@@ -219,51 +221,36 @@
     return [pltpu.SemaphoreType.DMA((count,)), pltpu.SemaphoreType.DMA((count,))]
 
 
-def weight_kernel(w_ref, other_ref, send, recv):
-    place, net = Place(), Net(send, recv)
-    right, left = ring(place, "x")
-    quarter = w_ref.shape[0] // 4
-    greet([right, left, place.partner()])
-    finish = swap_weight(place, net, w_ref, other_ref, quarter)
-    finish()
-    net.drain()
-
-
-def swap_weight(place, net, w_ref, other_ref, quarter):
-    right, left = ring(place, "x")
-    core = place.core
-
-    def rows(side):
-        return pl.ds(pl.multiple_of((2 * side + core) * quarter, 16), quarter)
-
-    def cores_rows(side):
-        return other_ref.at[rows(side)]
-
-    one = net.copy(w_ref.at[rows(0)], cores_rows(0), left)
-    two = net.copy(w_ref.at[rows(1)], cores_rows(1), right)
-    trades = [net.copy(cores_rows(side), cores_rows(side), place.partner()) for side in (0, 1)]
-    net.go(one)
-    net.go(two)
-
-    def finish():
-        for first, trade in zip((one, two), trades):
-            first.wait_recv()
-            net.go(trade)
-        for trade in trades:
+class WeightSwap:
+    def __init__(self, net, place, w_ref, other_ref):
+        self.net = net
+        quarter = w_ref.shape[0] // 4
+        right, left = ring(place, "x")
+
+        def rows(ref, side):
+            return ref.at[pl.ds(pl.multiple_of((2 * side + place.core) * quarter, 16), quarter)]
+
+        self.first = [
+            net.copy(rows(w_ref, side), rows(other_ref, side), (left, right)[side])
+            for side in (0, 1)
+        ]
+        self.trades = [
+            net.copy(rows(other_ref, side), rows(other_ref, side), place.partner())
+            for side in (0, 1)
+        ]
+
+    def start(self):
+        for copy in self.first:
+            self.net.go(copy)
+
+    def forward(self):
+        for copy, trade in zip(self.first, self.trades):
+            copy.wait_recv()
+            self.net.go(trade)
+
+    def finish(self):
+        for trade in self.trades:
             trade.wait_recv()
-
-    return finish
-
-
-def fetch_weight(w, call_id):
-    return pl.pallas_call(
-        weight_kernel,
-        out_shape=jax.ShapeDtypeStruct(w.shape, w.dtype),
-        in_specs=[IN_VMEM],
-        out_specs=IN_VMEM,
-        scratch_shapes=sems(4),
-        compiler_params=params(call_id),
-    )(w)
 
 
 PARTS = (
@@ -339,6 +326,40 @@
     )
 
 
+def turn(u, cosine, sine):
+    half = HD // 2
+    low, high = u[:, :half], u[:, half:]
+    return jnp.concatenate([low * cosine - high * sine, high * cosine + low * sine], axis=1)
+
+
+def row_bounds(place, segments):
+    at = (place.y * 2 + lax.div(place.x, 2)) * 16 + place.z * 4 + lax.rem(place.x, 2)
+    rows = jnp.concatenate([segments[pl.ds(at, 1)], segments[pl.ds(at + 2, 1)]], axis=1)
+    every = segments[...]
+    first = jnp.zeros((1, ROWS), jnp.int32)
+    for k in range(1, 4):
+        below = jnp.sum((every < k).astype(F32), axis=0, keepdims=True)
+        below = jnp.sum(below, axis=1, keepdims=True).astype(jnp.int32)
+        first = jnp.where(rows == k, below, first)
+    lane = lax.broadcasted_iota(jnp.int32, (1, ROWS), 1)
+    last = at * TOK + lane + jnp.where(lane < TOK, 0, TOK)
+    return first, last
+
+
+def down(row):
+    return jnp.concatenate(
+        [
+            jnp.transpose(jnp.broadcast_to(row[:, 128 * i : 128 * i + 128], (128, 128)))
+            for i in range(row.shape[1] // 128)
+        ],
+        axis=0,
+    )
+
+
+def across(ref):
+    return ref[...].reshape(1, ref.shape[0])
+
+
 def norm_scale(v):
     return lax.rsqrt(jnp.mean(v * v, axis=-1, keepdims=True) + EPS)
 
@@ -350,17 +371,27 @@
 
 
 def forward_kernel(
-    kv_ref,
-    q_ref,
+    x_ref,
+    g_attn,
+    g_query,
+    g_key,
+    wq_ref,
+    wk_ref,
+    wv_ref,
     w_ref,
+    cos_ref,
+    sin_ref,
+    segments,
     key_ref,
-    last_ref,
-    first_ref,
     buf,
     q_all,
+    wq_other,
     w_other,
     o_out,
     inv_out,
+    q_pre,
+    k_pre,
+    h_out,
     o_sum,
     l_sum,
     o_got,
@@ -371,38 +402,81 @@
     place, net = Place(), Net(send, recv)
     core = place.core
     partner = place.partner()
-    greet(ring(place, "x") + ring(place, "y") + ring(place, "z") + [partner])
     mine = pl.ds(pl.multiple_of(core * TOK, TOK), TOK)
     theirs = pl.ds(pl.multiple_of((1 - core) * TOK, TOK), TOK)
-    q_all[:, mine] = q_ref[...]
-    stages = []
-    for part in PARTS:
-        skip, rows, _, _ = part
-        views = part_views(place, buf, part)
-        axis, view = views[0]
-        own = view(getattr(place, axis))
-        own[...] = kv_ref[pl.ds(skip, rows)]
-        stages.append([RingGather(net, place, axis, view, *halves(view)) for axis, view in views])
+    all_views = [part_views(place, buf, part) for part in PARTS]
+
+    def keys_and_values():
+        xf = x_ref[...].astype(F32)
+        h = (xf * norm_scale(xf) * across(g_attn)).astype(BF)
+        h_out[...] = h
+        k = jnp.dot(h, wk_ref[...], preferred_element_type=F32)
+        k_pre[...] = k
+        k = turn(k * norm_scale(k) * across(g_key), cos_ref[...], sin_ref[...]).astype(BF)
+        v = jnp.dot(h, wv_ref[...], preferred_element_type=F32).astype(BF)
+        for (skip, rows, _, _), views in zip(PARTS, all_views):
+            axis, view = views[0]
+            own = view(getattr(place, axis))
+            own[:, :HD] = k[skip : skip + rows]
+            own[:, HD:] = v[skip : skip + rows]
+
+    greet(
+        ring(place, "x") + ring(place, "y") + ring(place, "z") + [partner],
+        keys_and_values,
+    )
+    swap_wq = WeightSwap(net, place, wq_ref, wq_other)
+    swap_w = WeightSwap(net, place, w_ref, w_other)
+    stages = [
+        [RingGather(net, place, axis, view, *halves(view)) for axis, view in views]
+        for views in all_views
+    ]
     for rings in stages:
         rings[0].start()
-    swap_q = net.copy(q_all.at[:, mine], q_all.at[:, mine], partner)
-    net.go(swap_q)
+    swap_wq.start()
+
+    def queries(which, w):
+        q = jnp.dot(h_out[...], w[...], preferred_element_type=F32)
+        for i in range(2):
+            u = q[:, HD * i : HD * i + HD]
+            q_pre[2 * which + i] = u
+            u = turn(u * norm_scale(u) * across(g_query), cos_ref[...], sin_ref[...])
+            q_all[2 * which + i, mine] = (u.astype(BF).astype(F32) * HD**-0.5).astype(BF)
+
+    queries(0, wq_ref)
     for h in range(HEADS):
         o_sum[h] = jnp.zeros((ROWS, HD), F32)
         l_sum[h] = jnp.zeros((ROWS, 128), F32)
-    for level in (0, 1):
-        for rings in stages:
-            rings[level].forward()
-        for rings in stages:
-            rings[level].finish()
-            rings[level + 1].start()
-    finish_w = swap_weight(place, net, w_ref, w_other, w_ref.shape[0] // 4)
+    for rings in stages:
+        rings[0].forward()
+    for rings in stages:
+        rings[0].finish()
+        rings[1].start()
+    swap_wq.forward()
+    first, last = (down(row) for row in row_bounds(place, segments))
+    swap_wq.finish()
+    queries(1, wq_other)
+    swap_q = net.copy(q_all.at[:, mine], q_all.at[:, mine], partner)
+    net.go(swap_q)
+    for rings in stages:
+        rings[1].forward()
+    for rings in stages:
+        rings[1].finish()
+        rings[2].start()
+    swap_w.start()
     swap_q.wait_recv()
 
     def attend(by):
         leads = [set_lead(place, n, by) for n in range(8)]
         keys, values, token = read_sets(buf, key_ref, range(8), leads, leads)
-        allowed = (token <= last_ref[...]) & (token >= first_ref[...])
+        token = token + core * 256
+        allowed = jnp.concatenate(
+            [
+                (token[:, 128 * i : 128 * i + 128] <= last)
+                & (token[:, 128 * i : 128 * i + 128] >= first)
+                for i in range(16)
+            ],
+            axis=1,
+        )
         for h in range(HEADS):
             weights = jnp.exp(contract(q_all[h], keys, 1, 1))
             weights = jnp.where(allowed, weights, 0.0)
@@ -412,11 +486,12 @@
     attend(0)
     for rings in stages:
         rings[2].forward()
-    finish_w()
+    swap_w.forward()
     lax.fori_loop(0, 2, lambda i, c: (attend(1 + 2 * i), c)[1], 0)
     for rings in stages:
         rings[2].finish()
     attend(2)
+    swap_w.finish()
     swap_o = net.copy(o_sum.at[:, theirs], o_got, partner)
     swap_l = net.copy(l_sum.at[:, theirs], l_got, partner)
     net.go(swap_l)
@@ -431,28 +506,32 @@
     net.drain()
 
 
-def attention_forward(kv, q, w_out, key_rows, last, first, call_id):
+def attention_forward(args, call_id):
     shape = jax.ShapeDtypeStruct
     return pl.pallas_call(
         forward_kernel,
         out_shape=(
             shape((4, 2048, 2 * HD), BF),
             shape((HEADS, ROWS, HD), BF),
-            shape(w_out.shape, BF),
+            shape((D, 2 * HD), BF),
+            shape((2 * HD, D), BF),
             shape((HEADS, TOK, HD), F32),
             shape((HEADS, TOK, 128), F32),
+            shape((HEADS, TOK, HD), F32),
+            shape((TOK, HD), F32),
+            shape((TOK, D), BF),
         ),
-        in_specs=[IN_VMEM] * 6,
-        out_specs=[IN_VMEM] * 5,
+        in_specs=[IN_VMEM] * len(args),
+        out_specs=[IN_VMEM] * 9,
         scratch_shapes=[
             pltpu.VMEM((HEADS, ROWS, HD), F32),
             pltpu.VMEM((HEADS, ROWS, 128), F32),
             pltpu.VMEM((HEADS, TOK, HD), F32),
             pltpu.VMEM((HEADS, TOK, 128), F32),
-            *sems(48),
+            *sems(52),
         ],
         compiler_params=params(call_id),
-    )(kv, q, w_out, key_rows, last, first)
+    )(*args)
 
 
 GRAD_SLOT = {2: 0, 0: 0, 1: 1, 3: 2}
@@ -475,8 +554,7 @@
     do_ref,
     delta_ref,
     key_ref,
-    last_ref,
-    first_ref,
+    segments,
     q_pre,
     k_pre,
     cos_ref,
@@ -491,13 +569,8 @@
     g_key,
     gains_ref,
     dx_out,
-    dwq_out,
-    dwk_out,
-    dwv_out,
-    dwo_out,
-    dwg_out,
-    dwu_out,
-    dwd_out,
+    home_out,
+    w_both,
     gains_out,
     buf,
     wk,
@@ -526,7 +599,6 @@
     w_y,
     w_z,
     w_line,
-    w_both,
     dh,
     *rest,
 ):
@@ -659,18 +731,14 @@
     swap_do.wait_recv()
     swap_delta.wait_recv()
 
+    first, last = row_bounds(place, segments)
+
     def differ(chunks, by, slot):
         key_leads = [set_lead(place, n, by) for n in chunks]
         keys, values, token = read_sets(buf, key_ref, chunks, [slot] * len(chunks), key_leads)
-        token = jnp.concatenate(
-            [
-                jnp.transpose(jnp.broadcast_to(token[:, 128 * i : 128 * i + 128], (128, 128)))
-                for i in range(2 * len(chunks))
-            ],
-            axis=0,
-        )
+        token = down(token + core * 256)
         token = jnp.concatenate([token, token], axis=1)
-        allowed = (token <= last_ref[...]) & (token >= first_ref[...])
+        allowed = (token <= last) & (token >= first)
         d_keys = d_values = None
         for h in range(HEADS):
             probs = jnp.exp(contract(keys, q_all[h], 1, 1))
@@ -731,7 +799,7 @@
         e = jnp.transpose(dq_sum[h, :, mine] + dq_got[h]) * HD**-0.5
         e = turn_back(e.astype(BF).astype(F32), cos_ref[...], sin_ref[...])
         u = q_pre[h]
-        du, gain = norm_back(u, norm_scale(u), g_query[...], e)
+        du, gain = norm_back(u, norm_scale(u), across(g_query), e)
         d_query = d_query + gain
         dq_own[h] = du.astype(BF)
     dq_line[place.x] = dq_own[head_of(place.x)]
@@ -775,7 +843,7 @@
 
     e = turn_back(dkv[:, :HD].astype(BF).astype(F32), cos_ref[...], sin_ref[...])
     u = k_pre[...]
-    dk, d_key = norm_back(u, norm_scale(u), g_key[...], e)
+    dk, d_key = norm_back(u, norm_scale(u), across(g_key), e)
     dk, dv = dk.astype(BF), dkv[:, HD:].astype(BF)
     for i in range(2):
         kv_own[i] = dk[:, 128 * i : 128 * i + 128]
@@ -785,7 +853,7 @@
     kv_swap.start()
     d_h = dh[...] + contract(dk, wk[...], 1, 1) + contract(dv, wv[...], 1, 1)
     xf = x_ref[...].astype(F32)
-    dx, d_attn = norm_back(xf, norm_scale(xf), g_attn[...], d_h)
+    dx, d_attn = norm_back(xf, norm_scale(xf), across(g_attn), d_h)
     dx_out[...] = (dmid_ref[...] + dx).astype(BF)
     late_second.middle()
 
@@ -840,7 +908,8 @@
         net, place, "y", lambda j: w_line.at[place.x, place.y], lambda j: w_line.at[place.x, j]
     )
     y_back.start()
-    weights.arrive(dwq_out, dwo_out, dwg_out, dwu_out, dwd_out)
+    weights.arrive()
+    home_out[...] = weights.rcv[...]
     y_back.wait()
     x_back = Direct(net, place, "x", lambda j: w_line.at[place.x], lambda j: w_line.at[j])
     x_back.start()
@@ -851,12 +920,6 @@
     w_last = net.copy(w_line, w_both.at[core], partner)
     net.go(w_last)
     w_last.wait_recv()
-    for which in range(2):
-        for j in range(4):
-            out = (dwk_out, dwv_out)[j // 2]
-            for y in range(4):
-                rows = pl.ds(576 * which + 144 * y, 144)
-                out[rows, 128 * (j % 2) : 128 * (j % 2) + 128] = w_both[which, j, y].astype(F32)
     net.drain()
 
 
@@ -874,17 +937,12 @@
         backward_kernel,
         out_shape=(
             shape((TOK, D), BF),
-            shape((18, 2 * HD), F32),
-            shape((D, HD), F32),
-            shape((D, HD), F32),
-            shape((2 * HD, 18), F32),
-            shape((18, 2 * HID), F32),
-            shape((18, 2 * HID), F32),
-            shape((2 * HID, 18), F32),
+            shape((8, 32, HALF + 128), BF),
+            shape((2, 4, 4, 144, 128), BF),
             shape((8, D), F32),
         ),
         in_specs=[pl.BlockSpec(memory_space=pl.ANY)] * 6 + [IN_VMEM] * len(small),
-        out_specs=[IN_VMEM] * 9,
+        out_specs=[IN_VMEM] * 4,
         scratch_shapes=[
             pltpu.VMEM((2, 2048, 2 * HD), BF),
             pltpu.VMEM((D, HD), BF),
@@ -913,7 +971,6 @@
             pltpu.VMEM((4, 144, 128), BF),
             pltpu.VMEM((4, 144, 128), BF),
             pltpu.VMEM((4, 4, 144, 128), BF),
-            pltpu.VMEM((2, 4, 4, 144, 128), BF),
             pltpu.VMEM((TOK, D), F32),
             *rooms,
             *late_rooms,
@@ -932,7 +989,9 @@
     inv_ref,
     wo_ref,
     wo2_ref,
-    gains_ref,
+    post_ref,
+    ffn_ref,
+    out_gain_ref,
     cot_ref,
     wg_hbm,
     wu_hbm,
@@ -982,7 +1041,7 @@
     greet(ring(place, "x") + [partner])
     half = TOK // 2
     top, bottom = pl.ds(0, half), pl.ds(half, half)
-    g_post, g_ffn, g_out = (gains_ref[i : i + 1] for i in range(3))
+    g_post, g_ffn, g_out = (across(ref) for ref in (post_ref, ffn_ref, out_gain_ref))
 
     def gather(lines):
         line = RingGather(
@@ -1142,7 +1201,7 @@
     net.drain()
 
 
-def feed_forward(x, o_heads, inverse, wo, wo2, gains, cotangent, w_gate, w_up, w_down, call_id):
+def feed_forward(args, call_id):
     half = (TOK // 2, D)
     shape = jax.ShapeDtypeStruct
     every = (4, 2, 2, 144, HALF)
@@ -1160,7 +1219,7 @@
             shape((8, D), F32),
             shape(every, BF),
         ),
-        in_specs=[IN_VMEM] * 7 + [anywhere] * 3,
+        in_specs=[IN_VMEM] * 9 + [anywhere] * 3,
         out_specs=[IN_VMEM] * 6 + [anywhere],
         scratch_shapes=[
             pltpu.VMEM((D, HID_PAD), BF),
@@ -1184,7 +1243,7 @@
             pltpu.SemaphoreType.DMA((7,)),
         ],
         compiler_params=params(call_id),
-    )(x, o_heads, inverse, wo, wo2, gains, cotangent, w_gate, w_up, w_down)
+    )(*args)
 
 
 class WeightSums:
@@ -1342,7 +1401,7 @@
                 keep.start()
                 keep.wait()
 
-    def arrive(self, dwq, dwo, dwg, dwu, dwd):
+    def arrive(self):
         send, recv, _ = self.marks
         for m in range(8):
             arrival = pltpu.make_async_remote_copy(
@@ -1362,37 +1421,76 @@
             def _(arrival=arrival):
                 arrival.wait_send()
 
-        def tile(x_hi, n):
-            core, n = (n % 14) // 7, (n // 14) * 7 + n % 7
-            c, n = n // 11, n % 11
-            return self.rcv[x_hi * 4 + core * 2 + c, :, 128 * n : 128 * n + 128].astype(F32)[:24]
-
-        def turned(value):
-            value = jnp.concatenate([value, jnp.zeros((104, 128), F32)], axis=0)
-            return jnp.transpose(value)[:, :18]
-
-        for which, out in enumerate((dwg, dwu, dwd)):
-            for n in range(27):
-                value = None
-                for x_hi in range(2):
-                    if 0 <= n - 13 * x_hi < 14:
-                        term = tile(x_hi, 14 * which + n - 13 * x_hi)
-                        value = term if value is None else value + term
-                span = slice(128 * n, 128 * n + 128)
-                if which < 2:
-                    out[:, span] = value[:18]
-                else:
-                    out[span] = turned(value)
-        for x_hi in range(2):
-            for core in range(2):
-                at = x_hi * 4 + core * 2
-                span = slice(128 * (at // 2), 128 * (at // 2) + 128)
-                dwo[span] = turned(self.rcv[at, :, HALF:].astype(F32)[:24])
-                dwq[:, span] = self.rcv[at + 1, :, HALF:].astype(F32)[:18]
-
-
-def rms_scale(tensor, scaling):
-    return tensor * lax.rsqrt(jnp.mean(tensor * tensor, axis=-1, keepdims=True) + EPS) * scaling
+
+def last_kernel(
+    home_ref,
+    w_ref,
+    gains_ref,
+    y_ref,
+    dx_ref,
+    y_out,
+    dx_out,
+    dwq_out,
+    dwk_out,
+    dwv_out,
+    dwo_out,
+    dwg_out,
+    dwu_out,
+    dwd_out,
+    *gain_outs,
+):
+    y_out[...] = y_ref[...]
+    dx_out[...] = dx_ref[...]
+
+    def tile(x_hi, n):
+        core, n = (n % 14) // 7, (n // 14) * 7 + n % 7
+        c, n = n // 11, n % 11
+        return home_ref[x_hi * 4 + core * 2 + c, :, 128 * n : 128 * n + 128].astype(F32)[:24]
+
+    for which, out in enumerate((dwg_out, dwu_out, dwd_out)):
+        for n in range(27):
+            value = None
+            for x_hi in range(2):
+                if 0 <= n - 13 * x_hi < 14:
+                    term = tile(x_hi, 14 * which + n - 13 * x_hi)
+                    value = term if value is None else value + term
+            span = slice(128 * n, 128 * n + 128)
+            out[:, span] = value[:18]
+    for k in range(4):
+        span = slice(128 * k, 128 * k + 128)
+        dwo_out[:, span] = home_ref[2 * k, :, HALF:].astype(F32)[:18]
+        dwq_out[:, span] = home_ref[2 * k + 1, :, HALF:].astype(F32)[:18]
+    for which in range(2):
+        for j in range(4):
+            out = (dwk_out, dwv_out)[j // 2]
+            for y in range(4):
+                rows = slice(576 * which + 144 * y, 576 * which + 144 * y + 144)
+                out[rows, 128 * (j % 2) : 128 * (j % 2) + 128] = w_ref[which, j, y].astype(F32)
+    for out, row, start in zip(gain_outs, (0, 4, 4, 1, 2, 3), (0, 0, HD, 0, 0, 0)):
+        size = out.shape[0]
+        out[...] = gains_ref[row : row + 1, start : start + size].reshape(size)
+
+
+def last_layout(*args):
+    shape = jax.ShapeDtypeStruct
+    return pl.pallas_call(
+        last_kernel,
+        out_shape=(
+            shape((TOK, D), BF),
+            shape((TOK, D), BF),
+            shape((18, 2 * HD), F32),
+            shape((D, HD), F32),
+            shape((D, HD), F32),
+            shape((18, 2 * HD), F32),
+            shape((18, 2 * HID), F32),
+            shape((18, 2 * HID), F32),
+            shape((18, 2 * HID), F32),
+            *(shape((size,), F32) for size in (D, HD, HD, D, D, D)),
+        ),
+        in_specs=[IN_VMEM] * 5,
+        out_specs=[IN_VMEM] * 15,
+        compiler_params=pltpu.CompilerParams(vmem_limit_bytes=VMEM_BYTES),
+    )(*args)
 
 
 def angles(token_pos):
@@ -1400,15 +1498,6 @@
     frequency = THETA ** (-2.0 * jnp.arange(middle, dtype=F32) / HD)
     turned = token_pos.astype(F32)[:, None] * frequency[None, :]
     return (jnp.cos(turned), jnp.sin(turned))
-
-
-def rotary(tensor, cosine, sine):
-    middle = tensor.shape[-1] // 2
-    lower_half = tensor[..., :middle]
-    upper_half = tensor[..., middle:]
-    return jnp.concatenate(
-        [lower_half * cosine - upper_half * sine, upper_half * cosine + lower_half * sine], axis=-1
-    )
 
 
 def shards(
@@ -1431,71 +1520,52 @@
     cotangent,
 ):
     sp, tp = lax.axis_index("sp"), lax.axis_index("tp")
-    core = lax.rem(sp, 2)
-    own_start = (sp * 2 + tp) * TOK
-    chip_start = lax.div(sp, 2) * 512 + tp * TOK
-
-    firsts = jnp.sum(
-        (segment_ids[None, :] < jnp.arange(4, dtype=jnp.int32)[:, None]).astype(jnp.int32), axis=1
-    )
-    row_token = chip_start + jnp.concatenate([jnp.arange(TOK), 256 + jnp.arange(TOK)]).astype(
-        jnp.int32
-    )
-    row_segs = jnp.concatenate(
-        [
-            lax.dynamic_slice_in_dim(segment_ids, chip_start, TOK),
-            lax.dynamic_slice_in_dim(segment_ids, chip_start + 256, TOK),
-        ]
-    )
-    row_first = jnp.zeros_like(row_token)
-    for k in range(4):
-        row_first = jnp.where(row_segs == k, firsts[k], row_first)
-    key_rows = jnp.asarray(KEY_TOKENS) + core * 256
-    cosine, sine = angles(lax.dynamic_slice_in_dim(positions, own_start, TOK))
-
-    def query_piece(pre_rot, scaling):
-        return rotary(rms_scale(pre_rot, scaling), cosine[:, None, :], sine[:, None, :])
-
-    def key_piece(pre_rot, scaling):
-        return rotary(rms_scale(pre_rot, scaling), cosine, sine)
-
-    wq_other = fetch_weight(w_query, 1)
-    wq_both = jnp.concatenate([w_query, wq_other], axis=1)
-    input_f = layer_input.astype(F32)
-    h_attn = rms_scale(input_f, norm_attn).astype(BF)
-    q_pre = jnp.dot(h_attn, wq_both, preferred_element_type=F32).reshape(TOK, HEADS, HD)
-    q_rot = query_piece(q_pre, norm_query).astype(BF)
-    q_scaled = (q_rot * BF(HD**-0.5)).transpose(1, 0, 2)
-    k_pre = jnp.dot(h_attn, w_key, preferred_element_type=F32)
-    k_rot = key_piece(k_pre, norm_key).astype(BF)
-    v_own = jnp.dot(h_attn, w_value, preferred_element_type=F32).astype(BF)
-    kv_own = jnp.concatenate([k_rot, v_own], axis=1)
-    kv_all, q_all, wo_other, o_heads, inverse = attention_forward(
-        kv_own, q_scaled, w_out, key_rows, row_token[:, None], row_first[:, None], 2
+    cosine, sine = angles(lax.dynamic_slice_in_dim(positions, (sp * 2 + tp) * TOK, TOK))
+    segments = segment_ids.reshape(128, 128)
+    key_rows = jnp.asarray(KEY_TOKENS)
+    kv_all, q_all, wq_other, wo_other, o_heads, inverse, q_pre, k_pre, h_attn = attention_forward(
+        (
+            layer_input,
+            norm_attn,
+            norm_query,
+            norm_key,
+            w_query,
+            w_key,
+            w_value,
+            w_out,
+            cosine,
+            sine,
+            segments,
+            key_rows,
+        ),
+        2,
     )
     layer_output, d_mid, d_attn, d_heads, delta, d_gains, sums = feed_forward(
-        layer_input,
-        o_heads,
-        inverse,
-        w_out,
-        wo_other,
-        jnp.stack([norm_post, norm_ffn, norm_out]),
-        cotangent,
-        w_gate,
-        w_up,
-        w_down,
+        (
+            layer_input,
+            o_heads,
+            inverse,
+            w_out,
+            wo_other,
+            norm_post,
+            norm_ffn,
+            norm_out,
+            cotangent,
+            w_gate,
+            w_up,
+            w_down,
+        ),
         6,
     )
-    d_input, d_wq, d_wk, d_wv, d_wo, d_wg, d_wu, d_wd, gains = attention_backward(
+    d_input, home, w_both, gains = attention_backward(
         (kv_all, sums, w_query, wq_other, w_key, w_value),
         (
             q_all,
             d_heads,
             delta,
             key_rows,
-            row_token[None, :],
-            row_first[None, :],
-            q_pre.transpose(1, 0, 2),
+            segments,
+            q_pre,
             k_pre,
             cosine,
             sine,
@@ -1504,30 +1574,17 @@
             o_heads,
             layer_input,
             d_mid,
-            norm_attn[None, :],
-            norm_query[None, :],
-            norm_key[None, :],
+            norm_attn,
+            norm_query,
+            norm_key,
             d_gains,
         ),
         8,
     )
-    return (
-        layer_output,
-        d_input,
-        d_wq,
-        d_wk,
-        d_wv,
-        d_wo,
-        d_wg,
-        d_wu,
-        d_wd,
-        gains[0],
-        gains[4, :HD],
-        gains[4, HD : 2 * HD],
-        gains[1],
-        gains[2],
-        gains[3],
+    y, dx, d_wq, d_wk, d_wv, d_wo, d_wg, d_wu, d_wd, *d_norms = last_layout(
+        home, w_both, gains, layer_output, d_input
     )
+    return (y, dx, d_wq, d_wk, d_wv, d_wo.T, d_wg, d_wu, d_wd.T, *d_norms)
 
 
 def solution(mesh):

time: 329 us -> 288 us (0.88)
  local copies, waits for them, and re-layouts: 13.5 us -> 0 us
  other arithmetic: 13.1 us -> 1.74 us
  Pallas kernels: 292 us -> 281 us
  matrix products: 4.05 us -> 0 us
    pallas_call x2, Pallas kernels: 151 us -> 134 us  [the longest x1 130 us: attention_backward(): pl.pallas_call(backward_kernel, out_shape=(shape((TOK, D), BF), shape((8,...]
    unnamed x55 -> x0, local copies, waits for them, and re-layouts: 10.4 us -> none
    select_n x2 -> x0, other arithmetic: 5.1 us -> none  [shards(): row_first = jnp.where(row_segs == k, firsts[k], row_first)]
    pallas_call x1, Pallas kernels: 61.4 us -> 65.8 us  [attention_forward(): pl.pallas_call(forward_kernel, out_shape=(shape((4, 2048, 2 * HD), BF), s...]
    dot_general x3 -> x0, matrix products: 4.05 us -> none  [the longest x1 2.29 us: shards(): jnp.dot(h_attn, wq_both, preferred_element_type=F32).reshape(TOK, HEADS, HD)]
where the time goes in v5:
time: 288 us; the launch traced here: 284 us
  Pallas kernels  281 us (98%)
    pallas_call x1, Pallas kernels, attention_backward(): pl.pallas_call(backward_kernel, out_shape=(shape((TOK, D), BF), shape((8,...  130 us
    pallas_call x1, Pallas kernels, feed_forward(): pl.pallas_call(feed_kernel, out_shape=(shape((TOK, D), BF), shape((TOK, D...  81.8 us
    pallas_call x1, Pallas kernels, attention_forward(): pl.pallas_call(forward_kernel, out_shape=(shape((4, 2048, 2 * HD), BF), s...  65.8 us

profile of v5, /device:TPU:1, one launch (start us, length us, event | category | flops | bytes accessed | tf_op | source)
XLA Modules:
  0.0 284.1 jit_solution(8999892211170557373)
XLA Ops:
  0.7 0.8 dynamic-slice_convert_fusion
  1.4 1.0 multiply_sine_fusion
  2.4 65.8 %shard_map.289 = (bf16[4,2048,512]{2,1,0:T(8,128)(2,1)}, bf16[4,256,256]{2,1,0:T(8,128)(2,1)}, bf16[1152,512]{1,0:T(8,128)(2,1)}, bf16[512,1152]{1,0:T(8,128)(2,...) custom-call(bf16[128,1152]{1,0:T(8,128)(2,1)} %x_ref.5, ...), custom_call_target="tpu_custom_call" | custom-call | tf_op jit(solution)/shard_map/pallas_call | solution.py:511
  68.2 81.8 %shard_map.290 = (bf16[128,1152]{1,0:T(8,128)(2,1)}, f32[128,1152]{1,0:T(8,128)}, bf16[128,1152]{1,0:T(8,128)(2,1)}, bf16[4,128,256]{2,1,0:T(8,128)(2,1)}, f32[8...) custom-call(bf16[128,1152]{1,0:T(8,128)(2,1)} %x_ref.5, ...), custom_call_target="tpu_custom_call" | custom-call | tf_op jit(solution)/shard_map/pallas_call | solution.py:1211
  150.0 130.1 %shard_map.291 = (bf16[128,1152]{1,0:T(8,128)(2,1)}, bf16[8,32,1536]{2,1,0:T(8,128)(2,1)}, bf16[2,4,4,144,128]{4,3,2,1,0:T(8,128)(2,1)}, f32[8,1152]{1,0:T(8,128)}) custom-call(bf16[4,2048,512]{2,1,0:T(8,128)(2,1)} %get-tuple-element.50.kv_hbm, bf16[4,2,2,144,1408]{4,3,2,1,0:T(8,128)(2,1)} %get-tuple-element.54.sums_hbm, bf16[1152,512]{1,0:T(8,128)(2,1)} %wq_hbm.1, ...), custom_call_target="tpu_custom_call" | custom-call | tf_op jit(solution)/shard_map/pallas_call | solution.py:936
  280.1 3.7 %shard_map.292 = (bf16[128,1152]{1,0:T(8,128)(2,1)}, bf16[128,1152]{1,0:T(8,128)(2,1)}, f32[18,512]{1,0:T(8,128)}, f32[1152,256]{1,0:T(8,128)}, f32[1152,256]{1,...) custom-call(bf16[8,32,1536]{2,1,0:T(8,128)(2,1)} %get-tuple-element., ...), custom_call_target="tpu_custom_call" | custom-call | tf_op jit(solution)/shard_map/pallas_call | solution.py:1476
  (1 shorter events, 0.0 us)

commit v6 on v5

--- a/solution.py
+++ b/solution.py
@@ -1,3 +1,5 @@
+import functools
+
 import jax
 import jax.numpy as jnp
 import numpy as np
@@ -21,8 +23,10 @@
 ROWS = 2 * TOK
 HID = 1728
 HID_PAD = 1792
-HALF = 1408
-CUT = 768
+AHEAD, AHEAD_CUT = 512, 256
+LATER, LATER_CUT = 896, 512
+CUT = AHEAD_CUT + LATER_CUT
+HALF = AHEAD + LATER
 CHUNK = 256
 
 
@@ -186,17 +190,30 @@
         self.net.go(self.a)
         self.net.go(self.b)
 
-    def start_near(self):
+    def start_right(self):
         self.net.go(self.c_hi)
+
+    def start_left(self):
         self.net.go(self.d_lo)
 
-    def middle(self):
+    def start(self):
+        self.start_far()
+        self.start_right()
+        self.start_left()
+
+    def middle_right(self):
         self.a.wait_recv()
         add_to(self.lo1, self.lo(1))
         self.net.go(self.c_lo)
+
+    def middle_left(self):
         self.b.wait_recv()
         add_to(self.hi1, self.hi(3))
         self.net.go(self.d_hi)
+
+    def middle(self):
+        self.middle_right()
+        self.middle_left()
 
     def finish(self, lo_out, hi_out):
         self.c_hi.wait_recv()
@@ -537,6 +554,10 @@
 GRAD_SLOT = {2: 0, 0: 0, 1: 1, 3: 2}
 
 
+def kept_head(place, j):
+    return jnp.where(lax.rem(j, 2) == lax.rem(place.x, 2), 0, 2) + lax.div(j, 2)
+
+
 def turn_back(e, cosine, sine):
     half = HD // 2
     low, high = e[:, :half], e[:, half:]
@@ -546,6 +567,8 @@
 def backward_kernel(
     kv_hbm,
     sums_hbm,
+    ahead_y,
+    ahead_z,
     wq_hbm,
     wq2_hbm,
     wk_hbm,
@@ -617,8 +640,8 @@
             )
         )
     ]
-    w_loads[2].start()
-    w_loads[3].start()
+    for load in w_loads[2:]:
+        load.start()
 
     def set_loads(by, slot):
         copies = []
@@ -634,6 +657,13 @@
     for copy in sets[0] + sets[1]:
         copy.start()
     weights = WeightSums(place, net, sums_hbm, late_z, weight_refs, (send2, recv2, here))
+    y1, z1 = weights.y1, weights.z1
+    ahead_loads = [
+        pltpu.make_async_copy(ahead_y, y1.at[:, :, :, pl.ds(0, AHEAD_CUT)], here.at[6]),
+        pltpu.make_async_copy(ahead_z, z1.at[:, :, pl.ds(0, AHEAD - AHEAD_CUT)], here.at[7]),
+    ]
+    for load in ahead_loads:
+        load.start()
     greet(weights.friends + ring(place, "x") + ring(place, "y"))
     mine = pl.ds(pl.multiple_of(core * TOK, TOK), TOK)
     theirs = pl.ds(pl.multiple_of((1 - core) * TOK, TOK), TOK)
@@ -644,7 +674,6 @@
     net.go(swap_do)
     net.go(swap_delta)
 
-    x_lo = lax.rem(place.x, 2)
     half = TOK // 2
 
     def line_of(rows):
@@ -658,7 +687,7 @@
         )
 
     def head_of(j):
-        return jnp.where(lax.rem(j, 2) == x_lo, 0, 2) + lax.div(j, 2)
+        return kept_head(place, j)
 
     h_line[place.x] = h_ref[...]
     da_line[place.x] = da_ref[...]
@@ -668,9 +697,8 @@
     line_h, line_da = line_of(h_line), line_of(da_line)
     o_swap = Direct(net, place, "x", lambda j: o_own.at[head_of(j)], lambda j: o_line.at[j])
     dq_swap = Direct(net, place, "x", lambda j: dq_own.at[head_of(j)], lambda j: dq_line.at[j])
+    line_da.start()
     o_swap.start()
-    line_h.start()
-    line_da.start()
     for h in range(HEADS):
         dq_sum[h] = jnp.zeros((HD, ROWS), F32)
     stages = []
@@ -727,7 +755,8 @@
                     144 * k : 144 * k + 144, 128 * which : 128 * which + 128
                 ]
 
-    weights.begin()
+    weights.first.begin()
+    weights.first.go_on()
     swap_do.wait_recv()
     swap_delta.wait_recv()
 
@@ -769,27 +798,29 @@
     visit(0, sets[2])
     for rings, _ in stages:
         rings[2].start_far()
-    line_h.forward()
+    visit(1, sets[3])
+    for rings, _ in stages:
+        rings[2].start_right()
+    for rings, _ in stages:
+        rings[2].middle_right()
+    weights.first.turn()
     line_da.forward()
-    weights.turn()
-    visit(1, sets[3])
+    line_h.start()
     visit(2, w_loads[0:1])
     for rings, _ in stages:
-        rings[2].start_near()
+        rings[2].start_left()
     for rings, _ in stages:
-        rings[2].middle()
-    weights.next()
+        rings[2].middle_left()
     for rings, _ in stages:
         net.settle(rings[2].a)
         net.settle(rings[2].b)
     visit(3, w_loads[1:2])
     swap_dq = net.copy(dq_sum.at[:, :, theirs], dq_got, partner)
     net.go(swap_dq)
-    line_h.finish()
+    line_h.forward()
     line_da.finish()
     o_swap.wait()
     late_term(0, da_line, o_line)
-    weights.turn_again()
     for load in w_loads:
         load.wait()
 
@@ -804,42 +835,43 @@
         dq_own[h] = du.astype(BF)
     dq_line[place.x] = dq_own[head_of(place.x)]
     dq_swap.start()
-    for level in (2, 1, 0):
-        for (rings, views), part in zip(stages, PARTS):
+    for load in ahead_loads:
+        load.wait()
+    weights.next()
+
+    def finish_keys(level):
+        for (rings, views), (skip, rows, _, _) in zip(stages, PARTS):
             lo, hi = halves(views[level])
-            skip, rows, _, _ = part
             if level:
                 rings[level].finish(lo(0), hi(0))
-                rings[level - 1].start_far()
-                rings[level - 1].start_near()
+                rings[level - 1].start()
             else:
                 out = dkv.at[pl.ds(skip, rows)]
                 rings[level].finish(out.at[:, pl.ds(0, HD)], out.at[:, pl.ds(HD, HD)])
-        if level == 2:
-            d_h = sum(
-                contract(dq_own[h], buf[h // 2, :D, 256 * (h % 2) : 256 * (h % 2) + 256], 1, 1)
-                for h in range(HEADS)
-            )
-            dh[...] = d_h
-            dq_swap.wait()
-            late_term(1, h_line, dq_line)
-            late_swap = net.copy(late_all.at[1 - core], late_got, partner)
-            net.go(late_swap)
-        if level:
-            for rings, _ in stages:
-                rings[level - 1].middle()
-        if level == 2:
-            late_swap.wait_recv()
-            for y in range(4):
-                add_to(late_got.at[y], late_all.at[core, y])
-            late_first.start_far()
-            late_first.start_near()
-            weights.last()
-        if level == 1:
-            late_first.middle()
-    late_first.finish(late_y.at[0], late_y.at[1])
-    late_second.start_far()
-    late_second.start_near()
+
+    finish_keys(2)
+    d_h = sum(
+        contract(dq_own[h], buf[h // 2, :D, 256 * (h % 2) : 256 * (h % 2) + 256], 1, 1)
+        for h in range(HEADS)
+    )
+    dh[...] = d_h
+    line_h.finish()
+    dq_swap.wait()
+    late_term(1, h_line, dq_line)
+    late_swap = net.copy(late_all.at[1 - core], late_got, partner)
+    net.go(late_swap)
+    for rings, _ in stages:
+        rings[1].middle()
+    late_swap.wait_recv()
+    for y in range(4):
+        add_to(late_got.at[y], late_all.at[core, y])
+    late_first.start()
+    finish_keys(1)
+    weights.turn_again()
+    for rings, _ in stages:
+        rings[0].middle()
+    late_first.middle()
+    finish_keys(0)
 
     e = turn_back(dkv[:, :HD].astype(BF).astype(F32), cos_ref[...], sin_ref[...])
     u = k_pre[...]
@@ -855,7 +887,8 @@
     xf = x_ref[...].astype(F32)
     dx, d_attn = norm_back(xf, norm_scale(xf), across(g_attn), d_h)
     dx_out[...] = (dmid_ref[...] + dx).astype(BF)
-    late_second.middle()
+    late_first.finish(late_y.at[0], late_y.at[1])
+    late_second.start()
 
     def gain_swap(level, axis):
         return Direct(
@@ -881,8 +914,7 @@
         w_all[k // 4, k % 4] = term[144 * k : 144 * k + 144]
     w_swap = net.copy(w_all.at[1 - core], w_got, partner)
     net.go(w_swap)
-    late_second.finish(late_z.at[pl.ds(0, 80)], late_z.at[pl.ds(80, 64)])
-    weights.send_home()
+    late_second.middle()
     swaps[0].wait()
     gain_got[1, place.y] = gain_sum(0)
     swaps[1].start()
@@ -891,6 +923,9 @@
     w_scatter = Direct(net, place, "y", lambda j: w_got.at[j], lambda j: w_y.at[j])
     w_scatter.start()
     w_y[place.y] = w_got[place.y]
+    weights.last()
+    late_second.finish(late_z.at[pl.ds(0, 80)], late_z.at[pl.ds(80, 64)])
+    weights.send_home()
     swaps[1].wait()
     gain_got[2, place.z] = gain_sum(1)
     swaps[2].start()
@@ -937,11 +972,11 @@
         backward_kernel,
         out_shape=(
             shape((TOK, D), BF),
-            shape((8, 32, HALF + 128), BF),
+            shape((8, 16, HALF + 384), BF),
             shape((2, 4, 4, 144, 128), BF),
             shape((8, D), F32),
         ),
-        in_specs=[pl.BlockSpec(memory_space=pl.ANY)] * 6 + [IN_VMEM] * len(small),
+        in_specs=[pl.BlockSpec(memory_space=pl.ANY)] * len(hbm) + [IN_VMEM] * len(small),
         out_specs=[IN_VMEM] * 4,
         scratch_shapes=[
             pltpu.VMEM((2, 2048, 2 * HD), BF),
@@ -1002,6 +1037,8 @@
     do_out,
     delta_out,
     dgains_out,
+    ahead_y,
+    ahead_z,
     sums_hbm,
     wg,
     wu,
@@ -1017,6 +1054,8 @@
     d_up,
     f_terms,
     h_terms,
+    ahead_snd,
+    ahead_got,
     snd,
     got,
     attn,
@@ -1038,13 +1077,19 @@
     ]
     for load in loads:
         load.start()
-    greet(ring(place, "x") + [partner])
-    half = TOK // 2
-    top, bottom = pl.ds(0, half), pl.ds(half, half)
+    greet(ring(place, "x") + ring(place, "y") + ring(place, "z") + [partner])
+    half, quarter = TOK // 2, TOK // 4
+    top, bottom = pl.ds(0, quarter), pl.ds(quarter, quarter)
     g_post, g_ffn, g_out = (across(ref) for ref in (post_ref, ffn_ref, out_gain_ref))
 
+    def rows_of(part):
+        return slice(half * part, half * part + half)
+
+    def lines_of(part):
+        return slice(4 * half * part, 4 * half * part + 4 * half)
+
     def gather(lines):
-        line = RingGather(
+        return RingGather(
             net,
             place,
             "x",
@@ -1052,12 +1097,9 @@
             lambda j: lines.at[j, top],
             lambda j: lines.at[j, bottom],
         )
-        line.start()
-        line.forward()
-        line.finish()
 
     def scatter(terms, room):
-        line = RingScatter(
+        return RingScatter(
             net,
             place,
             "x",
@@ -1065,9 +1107,10 @@
             stepped(place, "x", lambda j: terms.at[j, bottom]),
             room,
         )
-        line.start_far()
-        line.start_near()
-        return line
+
+    def summed(line, part):
+        at = half * part
+        line.finish(ffn.at[pl.ds(at, quarter)], ffn.at[pl.ds(at + quarter, quarter)])
 
     o_cat = [o_ref[h].astype(BF) for h in range(HEADS)]
     a = jnp.dot(jnp.concatenate(o_cat[:2], axis=1), wo_ref[...], preferred_element_type=F32)
@@ -1075,19 +1118,26 @@
     attn[...] = a
     mid[...] = x_ref[...].astype(F32) + a * norm_scale(a) * g_post
     m = mid[...]
-    h_line[place.x] = (m * norm_scale(m) * g_ffn).astype(BF)
-    gather(h_line)
+    h = (m * norm_scale(m) * g_ffn).astype(BF)
+    for part in range(2):
+        h_line[part, place.x] = h[rows_of(part)]
+    h_gathers = [gather(h_line.at[part]) for part in range(2)]
+    f_gathers = [gather(f_line.at[part]) for part in range(2)]
+    f_sums = [scatter(f_terms.at[part], room[6 * part : 6 * part + 6]) for part in range(2)]
+    h_sums = [
+        scatter(h_terms.at[part], room[12 + 6 * part : 18 + 6 * part]) for part in range(2)
+    ]
+    h_gathers[0].start()
 
     for load in loads:
         load.wait()
-    lines = 4 * TOK
     low_unit, high_unit = jnp.where(x_hi == 0, 0, 64), jnp.where(x_hi == 0, HID, HID_PAD)
 
     def units(n):
         return pl.ds(pl.multiple_of(n * 256, 256), 256)
 
-    def forward(n, carry):
-        h = h_line[...].reshape(lines, D)
+    def forward(part, n, carry):
+        h = h_line[part].reshape(4 * half, D)
         gate = jnp.dot(h, wg[:, units(n)], preferred_element_type=F32)
         up = jnp.dot(h, wu[:, units(n)], preferred_element_type=F32)
         unit = n * 256 + lax.broadcasted_iota(jnp.int32, (1, 256), 1)
@@ -1098,87 +1148,126 @@
         lifted = 0.5 * (1.0 + bent)
         gelu = gate * lifted * own
         slope = lifted + 0.5 * gate * (1.0 - bent * bent) * scale * (1.0 + 3.0 * cube * square)
-        act[:, units(n)] = (gelu * up).astype(BF)
-        gelu_kept[:, units(n)] = gelu.astype(BF)
-        slope_kept[:, units(n)] = (slope * up * own).astype(BF)
+        act[lines_of(part), units(n)] = (gelu * up).astype(BF)
+        gelu_kept[lines_of(part), units(n)] = gelu.astype(BF)
+        slope_kept[lines_of(part), units(n)] = (slope * up * own).astype(BF)
         return carry
-
-    lax.fori_loop(0, HID_PAD // 256, forward, 0)
 
     def columns(n):
         return pl.ds(pl.multiple_of(n * 384, 128), 384)
 
-    def project(n, carry):
-        term = jnp.dot(act[...], wd[:, columns(n)], preferred_element_type=F32)
-        f_terms[:, :, columns(n)] = term.astype(BF).reshape(4, TOK, 384)
+    def project(part, n, carry):
+        term = jnp.dot(act[lines_of(part)], wd[:, columns(n)], preferred_element_type=F32)
+        f_terms[part, :, :, columns(n)] = term.astype(BF).reshape(4, half, 384)
         return carry
 
-    lax.fori_loop(0, 3, project, 0)
-    line = scatter(f_terms, room[:6])
-    h_turned[...] = jnp.transpose(h_line[...].reshape(lines, D))
-    line.middle()
-    line.finish(ffn.at[top], ffn.at[bottom])
-    f = ffn[...]
-    r_out = norm_scale(f)
-    out_ref[...] = (mid[...] + f * r_out * g_out).astype(BF)
-    df, d_out = norm_back(f, r_out, g_out, cot_ref[...].astype(F32))
-    f_line[place.x] = df.astype(BF)
-    gather(f_line)
-
-    def backward(n, carry):
-        d_act = contract(f_line[...].reshape(lines, D), wd[units(n)], 1, 1)
-        d_gate[:, units(n)] = (d_act * slope_kept[:, units(n)].astype(F32)).astype(BF)
-        d_up[:, units(n)] = (d_act * gelu_kept[:, units(n)].astype(F32)).astype(BF)
+    def backward(part, n, carry):
+        d_act = contract(f_line[part].reshape(4 * half, D), wd[units(n)], 1, 1)
+        rows = lines_of(part)
+        d_gate[rows, units(n)] = (d_act * slope_kept[rows, units(n)].astype(F32)).astype(BF)
+        d_up[rows, units(n)] = (d_act * gelu_kept[rows, units(n)].astype(F32)).astype(BF)
         return carry
 
-    lax.fori_loop(0, HID_PAD // 256, backward, 0)
-
-    def back_project(n, carry):
-        term = contract(d_gate[...], wg[columns(n)], 1, 1) + contract(d_up[...], wu[columns(n)], 1, 1)
-        h_terms[:, :, columns(n)] = term.astype(BF).reshape(4, TOK, 384)
+    def back_project(part, n, carry):
+        rows = lines_of(part)
+        term = contract(d_gate[rows], wg[columns(n)], 1, 1)
+        term += contract(d_up[rows], wu[columns(n)], 1, 1)
+        h_terms[part, :, :, columns(n)] = term.astype(BF).reshape(4, half, 384)
         return carry
 
-    lax.fori_loop(0, 3, back_project, 0)
-    line = scatter(h_terms, room[6:])
-    f_turned[...] = jnp.transpose(f_line[...].reshape(lines, D))
-
-    def fill(i, which, put):
-        some = pl.ds(pl.multiple_of(which * 896, 128), 896)
-        rows = pl.ds(576 * i, 576)
-        pairs = ((h_turned, d_gate), (h_turned, d_up), (f_turned, act))
-        for m, (left, right) in enumerate(pairs):
-            term = jnp.dot(left[rows], right[:, some], preferred_element_type=F32)
-            for k in range(4):
-                piece = term[144 * k : 144 * k + 144]
-                for c in range(2):
-                    low = max(896 * m, HALF * c)
-                    high = min(896 * m + 896, HALF * c + HALF)
-                    if low < high:
-                        at = (2 * i + k // 2, k % 2, c, slice(None), slice(low - HALF * c, high - HALF * c))
-                        put(at, piece[:, low - 896 * m : high - 896 * m])
-
-    def put_snd(at, value):
-        snd[at] = value.astype(BF)
-
-    def put_got(at, value):
-        got[at] = (got[at].astype(F32) + value).astype(BF)
-
+    def each(times, step, part):
+        lax.fori_loop(0, times, functools.partial(step, part), 0)
+
+    blocks = HID_PAD // 256
+
+    def turn_round(part):
+        rows = rows_of(part)
+        summed(f_sums[part], part)
+        f = ffn[rows]
+        r = norm_scale(f)
+        out_ref[rows] = (mid[rows] + f * r * g_out).astype(BF)
+        df, gain = norm_back(f, r, g_out, cot_ref[rows].astype(F32))
+        f_line[part, place.x] = df.astype(BF)
+        f_gathers[part].start()
+        return gain
+
+    h_gathers[0].forward()
+    h_gathers[1].start()
+    h_gathers[0].finish()
+    each(blocks, forward, 0)
+    h_gathers[1].forward()
+    each(3, project, 0)
+    f_sums[0].start()
+    h_gathers[1].finish()
+    each(blocks, forward, 1)
+    f_sums[0].middle()
+    each(3, project, 1)
+    f_sums[1].start()
+    d_out = turn_round(0)
+    f_sums[1].middle()
+    h_turned[...] = jnp.transpose(h_line[...].reshape(8 * half, D))
+    f_gathers[0].forward()
+    d_out = d_out + turn_round(1)
+    f_gathers[0].finish()
+    each(blocks, backward, 0)
+    f_gathers[1].forward()
+    each(3, back_project, 0)
+    h_sums[0].start()
+    f_gathers[1].finish()
+    f_turned[...] = jnp.transpose(f_line[...].reshape(8 * half, D))
+
+    def halves_of(which):
+        return pl.ds(pl.multiple_of(which * 896, 128), 896)
+
+    def fill(target, i, which, left, right, c, add):
+        term = jnp.dot(
+            left[576 * i : 576 * i + 576], right[:, halves_of(which)], preferred_element_type=F32
+        )
+        spans = ((c, 0, 896),) if c is not None else ((0, 0, AHEAD), (1, AHEAD, 896))
+        for k in range(4):
+            for half, low, high in spans:
+                at = (2 * i + k // 2, k % 2, half, slice(None), slice(0, high - low))
+                value = term[144 * k : 144 * k + 144, low:high]
+                if add:
+                    value = value + target[at].astype(F32)
+                target[at] = value.astype(BF)
+
+    def fill_later(target, i, which, add):
+        fill(target, i, which, h_turned, d_gate, 0, add)
+        fill(target, i, which, h_turned, d_up, 1, add)
+
+    for y in range(4):
+        ahead_snd[y, :, 1, :, 896 - AHEAD :] = jnp.zeros((2, 144, 2 * AHEAD - 896), BF)
+    ahead_swap = net.copy(ahead_snd, ahead_got, partner)
     swaps = [net.copy(snd.at[y], got.at[y], partner) for y in range(4)]
-    for y in range(4):
-        snd[y, :, 1, :, 1280:] = jnp.zeros((2, 144, 128), BF)
+    ahead = FirstSums(net, place, ahead_got, AHEAD_CUT, room[24:])
     for i in range(2):
-        fill(i, 1 - core, put_snd)
+        fill(ahead_snd, i, 1 - core, f_turned, act, None, False)
+    net.go(ahead_swap)
+    each(blocks, backward, 1)
+    h_sums[0].middle()
+    each(3, back_project, 1)
+    h_sums[1].start()
+    ahead_swap.wait_recv()
+    for i in range(2):
+        fill(ahead_got, i, core, f_turned, act, None, True)
+    ahead.begin()
+    ahead.go_on()
+    for i in range(2):
+        fill_later(snd, i, 1 - core, False)
         net.go(swaps[2 * i])
         net.go(swaps[2 * i + 1])
-    line.middle()
+    summed(h_sums[0], 0)
+    h_sums[1].middle()
     stores = [pltpu.make_async_copy(got.at[y], sums_hbm.at[y], local.at[3 + y]) for y in range(4)]
     for i in range(2):
         swaps[2 * i].wait_recv()
         swaps[2 * i + 1].wait_recv()
-        fill(i, core, put_got)
+        fill_later(got, i, core, True)
         stores[2 * i].start()
         stores[2 * i + 1].start()
-    line.finish(ffn.at[top], ffn.at[bottom])
+    ahead.turn()
+    summed(h_sums[1], 1)
 
     m, a = mid[...], attn[...]
     dm, d_ffn = norm_back(m, norm_scale(m), g_ffn, ffn[...])
@@ -1196,15 +1285,19 @@
         do_out[h] = (d_o * jnp.concatenate([inverse, inverse], axis=1)).astype(BF)
         delta = jnp.sum(d_o * o_ref[h], axis=1, keepdims=True) * inverse
         delta_out[h : h + 1] = jnp.transpose(delta)[:1]
+    y_line, z_line = ahead.lines
+    y_line.finish(ahead_y.at[0], ahead_y.at[1])
+    z_line.finish(ahead_z.at[pl.ds(0, 2)], ahead_z.at[pl.ds(2, 2)])
     for store in stores:
         store.wait()
     net.drain()
 
 
 def feed_forward(args, call_id):
-    half = (TOK // 2, D)
+    quarter = (TOK // 4, D)
     shape = jax.ShapeDtypeStruct
-    every = (4, 2, 2, 144, HALF)
+    every = (4, 2, 2, 144, LATER)
+    every_ahead = (4, 2, 2, 144, AHEAD)
     lines = 4 * TOK
     anywhere = pl.BlockSpec(memory_space=pl.ANY)
     unit_rows = [pltpu.VMEM((lines, HID_PAD), BF)] * 5
@@ -1217,33 +1310,92 @@
             shape((HEADS, TOK, HD), BF),
             shape((8, TOK), F32),
             shape((8, D), F32),
+            shape((2, 2, 144, AHEAD_CUT), BF),
+            shape((4, 144, AHEAD - AHEAD_CUT), BF),
             shape(every, BF),
         ),
         in_specs=[IN_VMEM] * 9 + [anywhere] * 3,
-        out_specs=[IN_VMEM] * 6 + [anywhere],
+        out_specs=[IN_VMEM] * 8 + [anywhere],
         scratch_shapes=[
             pltpu.VMEM((D, HID_PAD), BF),
             pltpu.VMEM((D, HID_PAD), BF),
             pltpu.VMEM((HID_PAD, D), BF),
-            pltpu.VMEM((4, TOK, D), BF),
-            pltpu.VMEM((4, TOK, D), BF),
+            pltpu.VMEM((2, 4, TOK // 2, D), BF),
+            pltpu.VMEM((2, 4, TOK // 2, D), BF),
             pltpu.VMEM((D, lines), BF),
             pltpu.VMEM((D, lines), BF),
             *unit_rows,
-            pltpu.VMEM((4, TOK, D), BF),
-            pltpu.VMEM((4, TOK, D), BF),
+            pltpu.VMEM((2, 4, TOK // 2, D), BF),
+            pltpu.VMEM((2, 4, TOK // 2, D), BF),
+            pltpu.VMEM(every_ahead, BF),
+            pltpu.VMEM(every_ahead, BF),
             pltpu.VMEM(every, BF),
             pltpu.VMEM(every, BF),
             pltpu.VMEM((TOK, D), F32),
             pltpu.VMEM((TOK, D), F32),
             pltpu.VMEM((TOK, D), F32),
-            *RingScatter.room_shapes(half, half),
-            *RingScatter.room_shapes(half, half),
-            *sems(32),
+            *(RingScatter.room_shapes(quarter, quarter) * 4),
+            *FirstSums.room_shapes(AHEAD_CUT, AHEAD - AHEAD_CUT),
+            *sems(72),
             pltpu.SemaphoreType.DMA((7,)),
         ],
         compiler_params=params(call_id),
     )(*args)
+
+
+class FirstSums:
+    def __init__(self, net, place, sums, cut, rooms, here=None, marks=None):
+        left, right = pl.ds(0, cut), pl.ds(cut, sums.shape[-1] - cut)
+
+        def y_spot(half):
+            return stepped(place, "y", lambda j: sums.at[j, half, :, :, left])
+
+        def z_spot(half):
+            return stepped(
+                place,
+                "z",
+                lambda j: sums.at[pl.ds(2 * half, 2), lax.div(j, 2), lax.rem(j, 2), :, right],
+            )
+
+        self.loads = []
+        self.lines = []
+        for i, (axis, spot) in enumerate((("y", y_spot), ("z", z_spot))):
+            near = (None, None)
+            if here is not None:
+                near = ({}, {})
+                for k, (half, by) in enumerate(((0, 1), (1, 3), (0, 0), (1, 0))):
+                    target = here[i].at[k]
+                    near[half][by] = target
+                    self.loads.append(
+                        pltpu.make_async_copy(spot(half)(by), target, marks.at[8 + 4 * i + k])
+                    )
+                near = (near[0].get, near[1].get)
+            room = rooms[6 * i : 6 * i + 6]
+            self.lines.append(RingScatter(net, place, axis, spot(0), spot(1), room, *near))
+
+    @staticmethod
+    def room_shapes(cut, rest):
+        return [
+            *RingScatter.room_shapes((2, 144, cut), (2, 144, cut)),
+            *RingScatter.room_shapes((2, 144, rest), (2, 144, rest)),
+        ]
+
+    def begin(self):
+        for load in self.loads:
+            load.start()
+        for line in self.lines:
+            line.start_far()
+
+    def go_on(self):
+        for line in self.lines:
+            line.start_right()
+            line.start_left()
+
+    def turn(self):
+        for load in self.loads:
+            load.wait()
+        for line in self.lines:
+            line.middle()
 
 
 class WeightSums:
@@ -1258,47 +1410,7 @@
             x, z = lax.div(spot, 8) * 2 + self.x_lo, lax.rem(lax.div(spot, 2), 4)
             self.friends.append(place.device(x=x, z=z, core=lax.rem(spot, 2)))
 
-        left, right = pl.ds(0, CUT), pl.ds(CUT, HALF - CUT)
-
-        def y_spot(half):
-            return stepped(place, "y", lambda j: sums.at[j, half, :, :, left])
-
-        def z_spot(half):
-            return stepped(
-                place,
-                "z",
-                lambda j: sums.at[pl.ds(2 * half, 2), lax.div(j, 2), lax.rem(j, 2), :, right],
-            )
-
-        self.loads = []
-        here = []
-        for i, spot in enumerate((y_spot, z_spot)):
-            for k, (half, by) in enumerate(((0, 1), (1, 3), (0, 0), (1, 0))):
-                target = (y_here, z_here)[i].at[k]
-                here.append(target)
-                self.loads.append(
-                    pltpu.make_async_copy(spot(half)(by), target, marks[2].at[8 + 4 * i + k])
-                )
-        self.y_first = RingScatter(
-            net,
-            place,
-            "y",
-            y_spot(0),
-            y_spot(1),
-            rooms[0:6],
-            {1: here[0], 0: here[2]}.get,
-            {3: here[1], 0: here[3]}.get,
-        )
-        self.z_first = RingScatter(
-            net,
-            place,
-            "z",
-            z_spot(0),
-            z_spot(1),
-            rooms[6:12],
-            {1: here[4], 0: here[6]}.get,
-            {3: here[5], 0: here[7]}.get,
-        )
+        self.first = FirstSums(net, place, sums, LATER_CUT, rooms[:12], (y_here, z_here), marks[2])
 
         def then_z(j):
             return y1.at[lax.div(j, 2), lax.rem(j, 2)]
@@ -1324,40 +1436,27 @@
     def scratch():
         rest = HALF - CUT
         return [
-            pltpu.VMEM((4, 2, 144, CUT), BF),
-            pltpu.VMEM((4, 2, 144, rest), BF),
+            pltpu.VMEM((4, 2, 144, LATER_CUT), BF),
+            pltpu.VMEM((4, 2, 144, LATER - LATER_CUT), BF),
             pltpu.VMEM((2, 2, 144, CUT), BF),
             pltpu.VMEM((4, 144, rest), BF),
             pltpu.VMEM((144, CUT), F32),
             pltpu.VMEM((144, rest), F32),
-            pltpu.VMEM((8, 32, HALF + 128), BF),
-            pltpu.VMEM((8, 32, HALF + 128), BF),
-            *RingScatter.room_shapes((2, 144, CUT), (2, 144, CUT)),
-            *RingScatter.room_shapes((2, 144, rest), (2, 144, rest)),
+            pltpu.VMEM((8, 16, HALF + 384), BF),
+            pltpu.VMEM((8, 16, HALF + 384), BF),
+            *FirstSums.room_shapes(LATER_CUT, LATER - LATER_CUT),
             *RingScatter.room_shapes((144, 384), (144, 384)),
             *RingScatter.room_shapes((144, 384), (144, 256)),
         ]
 
-    def begin(self):
-        for load in self.loads:
-            load.start()
-        for line in (self.y_first, self.z_first):
-            line.start_far()
-            line.start_near()
-
-    def turn(self):
-        for load in self.loads:
-            load.wait()
-        self.y_first.middle()
-        self.z_first.middle()
-
     def next(self):
-        self.y_first.finish(self.y1.at[0], self.y1.at[1])
-        self.z_second.start_far()
-        self.z_second.start_near()
-        self.z_first.finish(self.z1.at[pl.ds(0, 2)], self.z1.at[pl.ds(2, 2)])
-        self.y_second.start_far()
-        self.y_second.start_near()
+        y_line, z_line = self.first.lines
+        after = pl.ds(AHEAD_CUT, LATER_CUT)
+        y_line.finish(self.y1.at[0, :, :, after], self.y1.at[1, :, :, after])
+        self.z_second.start()
+        after = pl.ds(AHEAD - AHEAD_CUT, LATER - LATER_CUT)
+        z_line.finish(self.z1.at[pl.ds(0, 2), :, after], self.z1.at[pl.ds(2, 2), :, after])
+        self.y_second.start()
 
     def turn_again(self):
         self.z_second.middle()
@@ -1371,9 +1470,14 @@
     def send_home(self):
         snd = self.snd
         total = jnp.concatenate([self.z2[...], self.y2[...], self.late[...]], axis=1)
-        blank = jnp.zeros((14, HALF + 128), F32)
+        blank = jnp.zeros((8, 128), F32)
         for k in range(8):
-            snd[k] = jnp.concatenate([total[18 * k : 18 * k + 18], blank], axis=0).astype(BF)
+            extra = total[18 * k + 16 : 18 * k + 18]
+            pieces = [extra[:, 128 * n : 128 * n + 128] for n in range(12)]
+            snd[k, :, : HALF + 128] = total[18 * k : 18 * k + 16].astype(BF)
+            for n, group in enumerate((pieces[:8], pieces[8:] + [blank])):
+                at = HALF + 128 + 128 * n
+                snd[k, :, at : at + 128] = jnp.concatenate(group, axis=0).astype(BF)
         place = self.place
         send, recv, here = self.marks
         row_half = lax.div(place.z, 2)
@@ -1442,24 +1546,35 @@
     y_out[...] = y_ref[...]
     dx_out[...] = dx_ref[...]
 
-    def tile(x_hi, n):
-        core, n = (n % 14) // 7, (n // 14) * 7 + n % 7
-        c, n = n // 11, n % 11
-        return home_ref[x_hi * 4 + core * 2 + c, :, 128 * n : 128 * n + 128].astype(F32)[:24]
+    def rows_at(slot, n):
+        spare, at = HALF + 128 + 128 * (n // 8), 2 * (n % 8)
+        more = home_ref[slot, :, spare : spare + 128].astype(F32)[at : at + 2]
+        return jnp.concatenate(
+            [home_ref[slot, :, 128 * n : 128 * n + 128].astype(F32), more], axis=0
+        )
+
+    def tile(x_hi, which, n):
+        core, n = n // 7, n % 7
+        if which < 2:
+            c, at = which, AHEAD_CUT + 128 * n if n < 4 else AHEAD + 128 * n
+        else:
+            c, n = n // 4, n % 4
+            at = 128 * n if n < 2 else CUT + 128 * (n - 2)
+        return rows_at(x_hi * 4 + core * 2 + c, at // 128)
 
     for which, out in enumerate((dwg_out, dwu_out, dwd_out)):
         for n in range(27):
             value = None
             for x_hi in range(2):
                 if 0 <= n - 13 * x_hi < 14:
-                    term = tile(x_hi, 14 * which + n - 13 * x_hi)
+                    term = tile(x_hi, which, n - 13 * x_hi)
                     value = term if value is None else value + term
             span = slice(128 * n, 128 * n + 128)
-            out[:, span] = value[:18]
+            out[:, span] = value
     for k in range(4):
         span = slice(128 * k, 128 * k + 128)
-        dwo_out[:, span] = home_ref[2 * k, :, HALF:].astype(F32)[:18]
-        dwq_out[:, span] = home_ref[2 * k + 1, :, HALF:].astype(F32)[:18]
+        dwo_out[:, span] = rows_at(2 * k, HALF // 128)
+        dwq_out[:, span] = rows_at(2 * k + 1, HALF // 128)
     for which in range(2):
         for j in range(4):
             out = (dwk_out, dwv_out)[j // 2]
@@ -1540,7 +1655,17 @@
         ),
         2,
     )
-    layer_output, d_mid, d_attn, d_heads, delta, d_gains, sums = feed_forward(
+    (
+        layer_output,
+        d_mid,
+        d_attn,
+        d_heads,
+        delta,
+        d_gains,
+        ahead_y,
+        ahead_z,
+        sums,
+    ) = feed_forward(
         (
             layer_input,
             o_heads,
@@ -1558,7 +1683,7 @@
         6,
     )
     d_input, home, w_both, gains = attention_backward(
-        (kv_all, sums, w_query, wq_other, w_key, w_value),
+        (kv_all, sums, ahead_y, ahead_z, w_query, wq_other, w_key, w_value),
         (
             q_all,
             d_heads,

time: 288 us -> 265 us (0.920)
  Pallas kernels: 281 us -> 258 us
    pallas_call x1, Pallas kernels: 130 us -> 112 us  [attention_backward(): pl.pallas_call(backward_kernel, out_shape=(shape((TOK, D), BF), shape((8,...]
    pallas_call x1, Pallas kernels: 81.8 us -> 76.4 us  [feed_forward(): pl.pallas_call(feed_kernel, out_shape=(shape((TOK, D), BF), shape((TOK, D...]
where the time goes in v6:
time: 265 us; the launch traced here: 261 us
  Pallas kernels  258 us (97%)
    pallas_call x1, Pallas kernels, attention_backward(): pl.pallas_call(backward_kernel, out_shape=(shape((TOK, D), BF), shape((8,...  112 us
    pallas_call x1, Pallas kernels, feed_forward(): pl.pallas_call(feed_kernel, out_shape=(shape((TOK, D), BF), shape((TOK, D...  76.4 us
    pallas_call x1, Pallas kernels, attention_forward(): pl.pallas_call(forward_kernel, out_shape=(shape((4, 2048, 2 * HD), BF), s...  65.8 us

profile of v6, /device:TPU:1, one launch (start us, length us, event | category | flops | bytes accessed | tf_op | source)
XLA Modules:
  0.0 260.9 jit_solution(7142640273999356860)
XLA Ops:
  0.7 0.8 dynamic-slice_convert_fusion
  1.4 1.0 multiply_sine_fusion
  2.4 65.8 %shard_map.289 = (bf16[4,2048,512]{2,1,0:T(8,128)(2,1)}, bf16[4,256,256]{2,1,0:T(8,128)(2,1)}, bf16[1152,512]{1,0:T(8,128)(2,1)}, bf16[512,1152]{1,0:T(8,128)(2,...) custom-call(bf16[128,1152]{1,0:T(8,128)(2,1)} %x_ref.5, ...), custom_call_target="tpu_custom_call" | custom-call | tf_op jit(solution)/shard_map/pallas_call | solution.py:528
  68.2 76.4 %shard_map.290 = (bf16[128,1152]{1,0:T(8,128)(2,1)}, f32[128,1152]{1,0:T(8,128)}, bf16[128,1152]{1,0:T(8,128)(2,1)}, bf16[4,128,256]{2,1,0:T(8,128)(2,1)}, f32[8...) custom-call(bf16[128,1152]{1,0:T(8,128)(2,1)} %x_ref.5, ...), custom_call_target="tpu_custom_call" | custom-call | tf_op jit(solution)/shard_map/pallas_call | solution.py:1304
  144.6 112.4 %shard_map.291 = (bf16[128,1152]{1,0:T(8,128)(2,1)}, bf16[8,16,1792]{2,1,0:T(8,128)(2,1)}, bf16[2,4,4,144,128]{4,3,2,1,0:T(8,128)(2,1)}, f32[8,1152]{1,0:T(8,128)}) custom-call(bf16[4,2048,512]{2,1,0:T(8,128)(2,1)} %get-tuple-element.52.kv_hbm, bf16[4,2,2,144,896]{4,3,2,1,0:T(8,128)(2,1)} %get-tuple-element.56.sums_hbm, ...), custom_call_target="tpu_custom_call" | custom-call | tf_op jit(solution)/shard_map/pallas_call | solution.py:971
  257.1 3.6 %shard_map.292 = (bf16[128,1152]{1,0:T(8,128)(2,1)}, bf16[128,1152]{1,0:T(8,128)(2,1)}, f32[18,512]{1,0:T(8,128)}, f32[1152,256]{1,0:T(8,128)}, f32[1152,256]{1,...) custom-call(bf16[8,16,1792]{2,1,0:T(8,128)(2,1)} %get-tuple-element., ...), custom_call_target="tpu_custom_call" | custom-call | tf_op jit(solution)/shard_map/pallas_call | solution.py:1591
  (1 shorter events, 0.0 us)

commit v7 on v6

--- a/solution.py
+++ b/solution.py
@@ -27,7 +27,8 @@
 LATER, LATER_CUT = 896, 512
 CUT = AHEAD_CUT + LATER_CUT
 HALF = AHEAD + LATER
-CHUNK = 256
+STRIPE = TOK // 4
+KEYS = 16 * STRIPE
 
 
 class Place:
@@ -270,71 +271,32 @@
             trade.wait_recv()
 
 
-PARTS = (
-    (0, 48, 0, ("x", "y", "z")),
-    (48, 48, 768, ("z", "x", "y")),
-    (96, 32, 1536, ("y", "z", "x")),
-)
-
-
-def part_views(place, buf, part):
-    _, rows, base, (first, second, third) = part
-    at1, at2, at3 = (getattr(place, axis) for axis in (first, second, third))
-
-    def block(lead, start, size):
-        return buf.at[lead, pl.ds(pl.multiple_of(base + start, 16), size)]
-
+def key_lines(place, ref):
+    def stage(axis, first, at):
+        return (
+            axis,
+            lambda j: ref.at[(pl.ds(first, 2), *at(j))],
+            lambda j: ref.at[(first, *at(j))],
+            lambda j: ref.at[(first + 1, *at(j))],
+        )
+
+    every = slice(None)
     return (
-        (first, lambda j: block(at3, (at2 * 4 + j) * rows, rows)),
-        (second, lambda j: block(at3, j * 4 * rows, 4 * rows)),
-        (third, lambda j: block(j, 0, 16 * rows)),
-    )
-
-
-def halves(view):
-    return (lambda j: view(j).at[:, pl.ds(0, HD)]), (lambda j: view(j).at[:, pl.ds(HD, HD)])
-
-
-def chunk_rows(n):
-    return [256 * n + 64 * i if n < 6 else 1536 + 128 * i + 64 * (n - 6) for i in range(4)]
+        (stage("x", 0, lambda j: (place.z, j)), stage("z", 0, lambda j: (j,))),
+        (stage("z", 2, lambda j: (j, place.x)), stage("x", 2, lambda j: (every, j))),
+    )
 
 
 def key_tokens():
-    out = np.zeros((4, 2048), np.int32)
-    for skip, rows, base, axes in PARTS:
-        for j in range(4):
-            for r in range(16 * rows):
-                spot = {axes[2]: j, axes[1]: r // (4 * rows), axes[0]: (r // rows) % 4}
-                x, y, z = spot["x"], spot["y"], spot["z"]
-                token = ((y * 2 + x // 2) * 4 + z) * 512 + (x % 2) * 128 + skip + r % rows
-                out[j, base + r] = token
-    order = np.zeros((8, CHUNK), np.int64)
-    for c in range(8):
-        for i in range(4):
-            start = chunk_rows(c)[i]
-            order[c, 64 * i : 64 * i + 64] = np.arange(start, start + 64)
-    return out[:, order]
+    z, x, row = np.meshgrid(np.arange(4), np.arange(4), np.arange(STRIPE), indexing="ij")
+    return ((x // 2) * 2048 + z * 512 + (x % 2) * 128 + row).reshape(1, KEYS).astype(np.int32)
 
 
 KEY_TOKENS = key_tokens()
 
 
-def set_lead(place, n, by):
-    return place.step("zyx"[n // 3], by)
-
-
-def read_sets(buf, key_ref, chunks, leads, key_leads):
-    keys, values, tokens = [], [], []
-    for n, lead, key_lead in zip(chunks, leads, key_leads):
-        rows = chunk_rows(n)
-        keys += [buf[lead, start : start + 64, :HD] for start in rows]
-        values += [buf[lead, start : start + 64, HD:] for start in rows]
-        tokens.append(key_ref[key_lead, n : n + 1])
-    return (
-        jnp.concatenate(keys, axis=0),
-        jnp.concatenate(values, axis=0),
-        jnp.concatenate(tokens, axis=1),
-    )
+def first_key(place, y):
+    return y * 4096 + place.core * 256 + STRIPE * place.y
 
 
 def contract(left, right, left_dim, right_dim):
@@ -349,8 +311,8 @@
     return jnp.concatenate([low * cosine - high * sine, high * cosine + low * sine], axis=1)
 
 
-def row_bounds(place, segments):
-    at = (place.y * 2 + lax.div(place.x, 2)) * 16 + place.z * 4 + lax.rem(place.x, 2)
+def row_bounds(place, segments, y):
+    at = (y * 2 + lax.div(place.x, 2)) * 16 + place.z * 4 + lax.rem(place.x, 2)
     rows = jnp.concatenate([segments[pl.ds(at, 1)], segments[pl.ds(at + 2, 1)]], axis=1)
     every = segments[...]
     first = jnp.zeros((1, ROWS), jnp.int32)
@@ -395,12 +357,12 @@
     wq_ref,
     wk_ref,
     wv_ref,
-    w_ref,
+    w_hbm,
     cos_ref,
     sin_ref,
     segments,
     key_ref,
-    buf,
+    kv_hbm,
     q_all,
     wq_other,
     w_other,
@@ -409,19 +371,25 @@
     q_pre,
     k_pre,
     h_out,
+    buf,
+    kv_own,
     o_sum,
     l_sum,
+    o_snd,
+    o_part,
     o_got,
+    o_done,
+    l_mine,
     l_got,
-    send,
-    recv,
+    l_core,
+    *rest,
 ):
+    *room, send, recv, local = rest
     place, net = Place(), Net(send, recv)
     core = place.core
     partner = place.partner()
     mine = pl.ds(pl.multiple_of(core * TOK, TOK), TOK)
     theirs = pl.ds(pl.multiple_of((1 - core) * TOK, TOK), TOK)
-    all_views = [part_views(place, buf, part) for part in PARTS]
 
     def keys_and_values():
         xf = x_ref[...].astype(F32)
@@ -431,25 +399,45 @@
         k_pre[...] = k
         k = turn(k * norm_scale(k) * across(g_key), cos_ref[...], sin_ref[...]).astype(BF)
         v = jnp.dot(h, wv_ref[...], preferred_element_type=F32).astype(BF)
-        for (skip, rows, _, _), views in zip(PARTS, all_views):
-            axis, view = views[0]
-            own = view(getattr(place, axis))
-            own[:, :HD] = k[skip : skip + rows]
-            own[:, HD:] = v[skip : skip + rows]
+        for j in range(4):
+            kv_own[j, :, :HD] = k[STRIPE * j : STRIPE * j + STRIPE]
+            kv_own[j, :, HD:] = v[STRIPE * j : STRIPE * j + STRIPE]
+        buf[place.y, place.z, place.x] = kv_own[place.y]
 
     greet(
-        ring(place, "x") + ring(place, "y") + ring(place, "z") + [partner],
+        ring(place, "x")
+        + ring(place, "y")
+        + ring(place, "z")
+        + [partner, place.toward("y", 2)],
         keys_and_values,
     )
     swap_wq = WeightSwap(net, place, wq_ref, wq_other)
-    swap_w = WeightSwap(net, place, w_ref, w_other)
-    stages = [
-        [RingGather(net, place, axis, view, *halves(view)) for axis, view in views]
-        for views in all_views
-    ]
-    for rings in stages:
-        rings[0].start()
+    swap_w = WeightSwap(net, place, w_hbm, w_other)
+    stripes = Direct(
+        net,
+        place,
+        "y",
+        lambda j: kv_own.at[j],
+        lambda j: buf.at[j, place.z, place.x],
+    )
+    stripes.start()
     swap_wq.start()
+    (first_a, then_a), (first_b, then_b) = (
+        [RingGather(net, place, *stage) for stage in part] for part in key_lines(place, buf)
+    )
+    q_ring = RingGather(
+        net,
+        place,
+        "y",
+        lambda j: q_all.at[j, :, mine],
+        lambda j: q_all.at[j, pl.ds(0, 2), mine],
+        lambda j: q_all.at[j, pl.ds(2, 2), mine],
+    )
+
+    def block_of(by):
+        return q_all.at[place.step("y", by), :, mine]
+
+    q_core = [net.copy(block_of(by), block_of(by), partner) for by in range(4)]
 
     def queries(which, w):
         q = jnp.dot(h_out[...], w[...], preferred_element_type=F32)
@@ -457,79 +445,131 @@
             u = q[:, HD * i : HD * i + HD]
             q_pre[2 * which + i] = u
             u = turn(u * norm_scale(u) * across(g_query), cos_ref[...], sin_ref[...])
-            q_all[2 * which + i, mine] = (u.astype(BF).astype(F32) * HD**-0.5).astype(BF)
+            q_all[place.y, 2 * which + i, mine] = (u.astype(BF).astype(F32) * HD**-0.5).astype(BF)
 
     queries(0, wq_ref)
-    for h in range(HEADS):
-        o_sum[h] = jnp.zeros((ROWS, HD), F32)
-        l_sum[h] = jnp.zeros((ROWS, 128), F32)
-    for rings in stages:
-        rings[0].forward()
-    for rings in stages:
-        rings[0].finish()
-        rings[1].start()
+    for by in range(4):
+        for h in range(HEADS):
+            o_sum[by, h] = jnp.zeros((ROWS, HD), F32)
+            l_sum[by, h] = jnp.zeros((ROWS, 128), F32)
+    stripes.wait()
+    first_a.start()
+    first_b.start()
     swap_wq.forward()
-    first, last = (down(row) for row in row_bounds(place, segments))
+    first_a.forward()
+    first_b.forward()
     swap_wq.finish()
     queries(1, wq_other)
-    swap_q = net.copy(q_all.at[:, mine], q_all.at[:, mine], partner)
-    net.go(swap_q)
-    for rings in stages:
-        rings[1].forward()
-    for rings in stages:
-        rings[1].finish()
-        rings[2].start()
+    q_ring.start()
+    net.go(q_core[0])
+    first_a.finish()
+    then_a.start()
+    first_b.finish()
+    then_b.start()
+    q_ring.forward()
+    net.go(q_core[1])
+    net.go(q_core[3])
+    then_a.forward()
+    then_b.forward()
+    q_ring.finish()
+    net.go(q_core[2])
+    then_a.finish()
+    then_b.finish()
     swap_w.start()
-    swap_q.wait_recv()
+    store = pltpu.make_async_copy(buf, kv_hbm, local.at[0])
+    store.start()
+
+    o_core = [net.copy(o_snd.at[by], o_got.at[by], partner) for by in range(4)]
 
     def attend(by):
-        leads = [set_lead(place, n, by) for n in range(8)]
-        keys, values, token = read_sets(buf, key_ref, range(8), leads, leads)
-        token = token + core * 256
-        allowed = jnp.concatenate(
-            [
-                (token[:, 128 * i : 128 * i + 128] <= last)
-                & (token[:, 128 * i : 128 * i + 128] >= first)
-                for i in range(16)
-            ],
-            axis=1,
-        )
+        y = place.step("y", by)
+        q_core[by].wait_recv()
+        first, last = (down(row) for row in row_bounds(place, segments, y))
+
+        def some_keys(key_y, carry):
+            keys = buf[key_y, :, :, :, :HD].reshape(KEYS, HD)
+            values = buf[key_y, :, :, :, HD:].reshape(KEYS, HD)
+            token = key_ref[...] + first_key(place, key_y)
+            allowed = jnp.concatenate(
+                [
+                    (token[:, 128 * i : 128 * i + 128] <= last)
+                    & (token[:, 128 * i : 128 * i + 128] >= first)
+                    for i in range(KEYS // 128)
+                ],
+                axis=1,
+            )
+            for h in range(HEADS):
+                weights = jnp.exp(contract(q_all[y, h], keys, 1, 1))
+                weights = jnp.where(allowed, weights, 0.0)
+                l_sum[by, h] += sum(
+                    weights[:, 128 * i : 128 * i + 128] for i in range(KEYS // 128)
+                )
+                o_sum[by, h] += jnp.dot(weights.astype(BF), values, preferred_element_type=F32)
+            return carry
+
+        lax.fori_loop(0, y + 1, some_keys, 0)
         for h in range(HEADS):
-            weights = jnp.exp(contract(q_all[h], keys, 1, 1))
-            weights = jnp.where(allowed, weights, 0.0)
-            l_sum[h] += sum(weights[:, 128 * i : 128 * i + 128] for i in range(16))
-            o_sum[h] += jnp.dot(weights.astype(BF), values, preferred_element_type=F32)
-
+            o_snd[by, h] = o_sum[by, h, theirs].astype(BF)
+            o_part[by, h] = o_sum[by, h, mine].astype(BF)
+            total = jnp.sum(l_sum[by, h], axis=1, keepdims=True)
+            l_mine[y, h : h + 1] = jnp.transpose(jnp.broadcast_to(total, (ROWS, 128)))[:1]
+        net.go(o_core[by])
+
+    def both_cores(by):
+        o_core[by].wait_recv()
+        add_to(o_part.at[by], o_got.at[by])
+
+    o_ring = RingScatter(
+        net,
+        place,
+        "y",
+        lambda by: o_part.at[by, pl.ds(0, 2)],
+        lambda by: o_part.at[by, pl.ds(2, 2)],
+        room,
+    )
     attend(0)
-    for rings in stages:
-        rings[2].forward()
+    attend(2)
+    attend(1)
+    both_cores(2)
+    o_ring.start_far()
     swap_w.forward()
-    lax.fori_loop(0, 2, lambda i, c: (attend(1 + 2 * i), c)[1], 0)
-    for rings in stages:
-        rings[2].finish()
-    attend(2)
+    attend(3)
+    l_swap = Direct(net, place, "y", lambda j: l_mine.at[j], lambda j: l_got.at[j])
+    l_swap.start()
+    l_got[place.y] = l_mine[place.y]
+    both_cores(1)
+    o_ring.start_right()
+    o_ring.middle_right()
+    both_cores(3)
+    o_ring.start_left()
+    o_ring.middle_left()
+    both_cores(0)
     swap_w.finish()
-    swap_o = net.copy(o_sum.at[:, theirs], o_got, partner)
-    swap_l = net.copy(l_sum.at[:, theirs], l_got, partner)
-    net.go(swap_l)
-    net.go(swap_o)
-    swap_l.wait_recv()
-    swap_o.wait_recv()
+    l_swap.wait()
+    l_core[core] = (l_got[0] + l_got[1]) + (l_got[2] + l_got[3])
+    l_over = net.copy(l_core.at[core], l_core.at[core], partner)
+    net.go(l_over)
+    l_over.wait_recv()
+    total = l_core[0] + l_core[1]
+    inverse = 1.0 / jnp.where(core == 0, total[:, :TOK], total[:, TOK:])
+    o_ring.finish(o_done.at[pl.ds(0, 2)], o_done.at[pl.ds(2, 2)])
     for h in range(HEADS):
-        total = jnp.sum(l_sum[h, mine] + l_got[h], axis=1, keepdims=True)
-        inverse = 1.0 / total
-        o_out[h] = (o_sum[h, mine] + o_got[h]) * inverse
-        inv_out[h] = jnp.broadcast_to(inverse, (TOK, 128))
+        scale = down(inverse[h : h + 1])
+        o_out[h] = o_done[h] * jnp.concatenate([scale, scale], axis=1)
+        inv_out[h] = scale
+    store.wait()
     net.drain()
 
 
 def attention_forward(args, call_id):
     shape = jax.ShapeDtypeStruct
+    anywhere = pl.BlockSpec(memory_space=pl.ANY)
+    halves = (2, TOK, HD)
     return pl.pallas_call(
         forward_kernel,
         out_shape=(
-            shape((4, 2048, 2 * HD), BF),
-            shape((HEADS, ROWS, HD), BF),
+            shape((4, 4, 4, STRIPE, 2 * HD), BF),
+            shape((4, HEADS, ROWS, HD), BF),
             shape((D, 2 * HD), BF),
             shape((2 * HD, D), BF),
             shape((HEADS, TOK, HD), F32),
@@ -538,20 +578,26 @@
             shape((TOK, HD), F32),
             shape((TOK, D), BF),
         ),
-        in_specs=[IN_VMEM] * len(args),
-        out_specs=[IN_VMEM] * 9,
+        in_specs=[IN_VMEM] * 7 + [anywhere] + [IN_VMEM] * 4,
+        out_specs=[anywhere] + [IN_VMEM] * 2 + [anywhere] + [IN_VMEM] * 5,
         scratch_shapes=[
-            pltpu.VMEM((HEADS, ROWS, HD), F32),
-            pltpu.VMEM((HEADS, ROWS, 128), F32),
+            pltpu.VMEM((4, 4, 4, STRIPE, 2 * HD), BF),
+            pltpu.VMEM((4, STRIPE, 2 * HD), BF),
+            pltpu.VMEM((4, HEADS, ROWS, HD), F32),
+            pltpu.VMEM((4, HEADS, ROWS, 128), F32),
+            pltpu.VMEM((4, HEADS, TOK, HD), BF),
+            pltpu.VMEM((4, HEADS, TOK, HD), BF),
+            pltpu.VMEM((4, HEADS, TOK, HD), BF),
             pltpu.VMEM((HEADS, TOK, HD), F32),
-            pltpu.VMEM((HEADS, TOK, 128), F32),
-            *sems(52),
+            pltpu.VMEM((4, 8, ROWS), F32),
+            pltpu.VMEM((4, 8, ROWS), F32),
+            pltpu.VMEM((2, 8, ROWS), F32),
+            *RingScatter.room_shapes(halves, halves),
+            *sems(64),
+            pltpu.SemaphoreType.DMA((1,)),
         ],
         compiler_params=params(call_id),
     )(*args)
-
-
-GRAD_SLOT = {2: 0, 0: 0, 1: 1, 3: 2}
 
 
 def kept_head(place, j):
@@ -593,19 +639,29 @@
     gains_ref,
     dx_out,
     home_out,
-    w_both,
+    late_out,
+    w_top,
+    w_low,
     gains_out,
     buf,
+    wq,
+    wq2,
     wk,
     wv,
     do_all,
     delta_all,
+    tokens,
     grads,
+    fin,
+    fin_got,
     dq_sum,
+    dq_snd,
+    dq_part,
     dq_got,
-    dkv,
+    dq_done,
     h_line,
     da_line,
+    turned,
     o_line,
     dq_line,
     dq_own,
@@ -617,15 +673,13 @@
     gain_got,
     kv_own,
     kv_line,
-    w_all,
+    turned_other,
     w_got,
     w_y,
     w_z,
-    w_line,
-    dh,
     *rest,
 ):
-    rooms, late_rooms, rest = rest[:54], rest[54:66], rest[66:]
+    rooms, dq_rooms, late_rooms, rest = rest[:24], rest[24:30], rest[30:42], rest[42:]
     *weight_refs, send, recv, send2, recv2, here = rest
     place, net = Place(), Net(send, recv)
     core, partner = place.core, place.partner()
@@ -633,46 +687,60 @@
         pltpu.make_async_copy(source, target, here.at[1 + i])
         for i, (source, target) in enumerate(
             (
-                (wq_hbm, buf.at[0, pl.ds(0, D)]),
-                (wq2_hbm, buf.at[1, pl.ds(0, D)]),
+                (kv_hbm, buf),
+                (wq_hbm, wq),
+                (wq2_hbm, wq2),
                 (wk_hbm, wk),
                 (wv_hbm, wv),
             )
         )
     ]
-    for load in w_loads[2:]:
+    for load in w_loads:
         load.start()
-
-    def set_loads(by, slot):
-        copies = []
-        for i, (_, rows, base, axes) in enumerate(PARTS):
-            span = pl.ds(base, 16 * rows)
-            source = kv_hbm.at[place.step(axes[2], by), span]
-            copies.append(
-                pltpu.make_async_copy(source, buf.at[slot, span], here.at[16 + 3 * slot + i])
-            )
-        return copies
-
-    sets = [set_loads(by, slot) for by, slot in ((2, 0), (1, 1), (3, 0), (0, 1))]
-    for copy in sets[0] + sets[1]:
-        copy.start()
     weights = WeightSums(place, net, sums_hbm, late_z, weight_refs, (send2, recv2, here))
     y1, z1 = weights.y1, weights.z1
     ahead_loads = [
-        pltpu.make_async_copy(ahead_y, y1.at[:, :, :, pl.ds(0, AHEAD_CUT)], here.at[6]),
-        pltpu.make_async_copy(ahead_z, z1.at[:, :, pl.ds(0, AHEAD - AHEAD_CUT)], here.at[7]),
+        pltpu.make_async_copy(ahead_y, y1.at[:, :, :, pl.ds(0, AHEAD_CUT)], here.at[16]),
+        pltpu.make_async_copy(ahead_z, z1.at[:, :, pl.ds(0, AHEAD - AHEAD_CUT)], here.at[17]),
     ]
     for load in ahead_loads:
         load.start()
-    greet(weights.friends + ring(place, "x") + ring(place, "y"))
+    across_x = [place.device(x=place.step("x", by), core=1 - core) for by in (1, 3)]
+    greet(
+        weights.friends
+        + ring(place, "x")
+        + ring(place, "y")
+        + across_x
+        + [place.toward("y", 2)]
+    )
     mine = pl.ds(pl.multiple_of(core * TOK, TOK), TOK)
     theirs = pl.ds(pl.multiple_of((1 - core) * TOK, TOK), TOK)
-    do_all[:, mine] = do_ref[...]
-    delta_all[core] = delta_ref[...]
-    swap_do = net.copy(do_all.at[:, mine], do_all.at[:, mine], partner)
-    swap_delta = net.copy(delta_all.at[core], delta_all.at[core], partner)
-    net.go(swap_do)
-    net.go(swap_delta)
+    do_all[place.y, :, mine] = do_ref[...]
+    delta_all[place.y, core] = delta_ref[...]
+    do_ring = RingGather(
+        net,
+        place,
+        "y",
+        lambda j: do_all.at[j, :, mine],
+        lambda j: do_all.at[j, pl.ds(0, 2), mine],
+        lambda j: do_all.at[j, pl.ds(2, 2), mine],
+    )
+
+    def block_of(by):
+        return do_all.at[place.step("y", by), :, mine]
+
+    do_core = [net.copy(block_of(by), block_of(by), partner) for by in range(4)]
+    delta_swap = Direct(
+        net,
+        place,
+        "y",
+        lambda j: delta_all.at[place.y, core],
+        lambda j: delta_all.at[j, core],
+    )
+    delta_core = net.copy(delta_all.at[:, core], delta_all.at[:, core], partner)
+    do_ring.start()
+    delta_swap.start()
+    net.go(do_core[0])
 
     half = TOK // 2
 
@@ -699,32 +767,31 @@
     dq_swap = Direct(net, place, "x", lambda j: dq_own.at[head_of(j)], lambda j: dq_line.at[j])
     line_da.start()
     o_swap.start()
-    for h in range(HEADS):
-        dq_sum[h] = jnp.zeros((HD, ROWS), F32)
-    stages = []
-    for i, part in enumerate(PARTS):
-        _, rows, base, (first, second, third) = part
-        at1, at2 = getattr(place, first), getattr(place, second)
-
-        def block(slot, start, size, base=base):
-            return grads.at[slot, pl.ds(pl.multiple_of(base + start, 16), size)]
-
-        views = (
-            lambda by, block=block, first=first, at2=at2, rows=rows: block(
-                0, (at2 * 4 + place.step(first, by)) * rows, rows
-            ),
-            lambda by, block=block, second=second, rows=rows: block(
-                0, place.step(second, by) * 4 * rows, 4 * rows
-            ),
-            lambda by, block=block, rows=rows: block(GRAD_SLOT[by], 0, 16 * rows),
-        )
-        rings = []
-        for level, axis in enumerate((first, second, third)):
-            spot = 6 * (3 * i + level)
-            rings.append(
-                RingScatter(net, place, axis, *halves(views[level]), rooms[spot : spot + 6])
+    key_rings = []
+    for i, (inner, outer) in enumerate(key_lines(place, grads)):
+        for k, (axis, _, lo, hi) in enumerate((outer, inner)):
+            spot = 12 * i + 6 * k
+            key_rings.append(
+                RingScatter(
+                    net,
+                    place,
+                    axis,
+                    stepped(place, axis, lo),
+                    stepped(place, axis, hi),
+                    rooms[spot : spot + 6],
+                )
             )
-        stages.append((rings, views))
+    first_a, then_a, first_b, then_b = key_rings
+    fin_swap = Direct(net, place, "y", lambda j: fin.at[j], lambda j: fin_got.at[j])
+    dq_core = net.copy(dq_snd, dq_got, partner)
+    dq_ring = RingScatter(
+        net,
+        place,
+        "y",
+        stepped(place, "y", lambda j: dq_part.at[j, pl.ds(0, 2)]),
+        stepped(place, "y", lambda j: dq_part.at[j, pl.ds(2, 2)]),
+        dq_rooms,
+    )
     late_first = RingScatter(
         net,
         place,
@@ -746,88 +813,106 @@
         late_rooms[6:],
     )
 
-    def late_term(c, rows, columns):
-        term = contract(rows[...].reshape(4 * TOK, D), columns[...].reshape(4 * TOK, HD), 0, 0)
-        term = term.astype(BF)
+    def late_term(c, turned, columns):
+        term = jnp.dot(
+            turned[...], columns[...].reshape(4 * TOK, HD), preferred_element_type=F32
+        ).astype(BF)
         for k in range(8):
             for which in range(2):
                 late_all[which, k // 2, k % 2, c] = term[
                     144 * k : 144 * k + 144, 128 * which : 128 * which + 128
                 ]
 
+    do_ring.forward()
+    net.go(do_core[1])
+    net.go(do_core[3])
     weights.first.begin()
     weights.first.go_on()
-    swap_do.wait_recv()
-    swap_delta.wait_recv()
-
-    first, last = row_bounds(place, segments)
-
-    def differ(chunks, by, slot):
-        key_leads = [set_lead(place, n, by) for n in chunks]
-        keys, values, token = read_sets(buf, key_ref, chunks, [slot] * len(chunks), key_leads)
-        token = down(token + core * 256)
+    delta_swap.wait()
+    net.go(delta_core)
+    tokens[...] = down(key_ref[...])
+    bounds = [row_bounds(place, segments, y) for y in range(4)]
+    do_ring.finish()
+    net.go(do_core[2])
+    w_loads[0].wait()
+    for copy in do_core:
+        copy.wait_recv()
+    delta_core.wait_recv()
+
+    def differ(key_y):
+        keys = buf[key_y, :, :, :, :HD].reshape(KEYS, HD)
+        values = buf[key_y, :, :, :, HD:].reshape(KEYS, HD)
+        token = tokens[...] + first_key(place, key_y)
         token = jnp.concatenate([token, token], axis=1)
-        allowed = (token <= last) & (token >= first)
         d_keys = d_values = None
-        for h in range(HEADS):
-            probs = jnp.exp(contract(keys, q_all[h], 1, 1))
-            probs = jnp.where(allowed, probs, 0.0)
-            delta = jnp.concatenate([delta_all[0, h : h + 1], delta_all[1, h : h + 1]], axis=1)
-            d_scores = (probs * (contract(values, do_all[h], 1, 1) - delta)).astype(BF)
-            value_term = jnp.dot(probs.astype(BF), do_all[h], preferred_element_type=F32)
-            key_term = jnp.dot(d_scores, q_all[h], preferred_element_type=F32)
-            d_values = value_term if h == 0 else d_values + value_term
-            d_keys = key_term if h == 0 else d_keys + key_term
-            dq_sum[h] += contract(keys, d_scores, 0, 0)
-        d_keys, d_values = d_keys.astype(BF), d_values.astype(BF)
-        for m, n in enumerate(chunks):
-            for i, start in enumerate(chunk_rows(n)):
-                spot = 256 * m + 64 * i
-                grads[GRAD_SLOT[by], start : start + 64, :HD] = d_keys[spot : spot + 64]
-                grads[GRAD_SLOT[by], start : start + 64, HD:] = d_values[spot : spot + 64]
-
-    def visit(step, after):
-        by, slot = ((2, 0), (1, 1), (3, 0), (0, 1))[step]
-        for copy in sets[step]:
-            copy.wait()
-        for chunks in ((0, 1, 2), (3, 4, 5), (6, 7)):
-            differ(chunks, by, slot)
-        for copy in after:
-            copy.start()
-
-    visit(0, sets[2])
-    for rings, _ in stages:
-        rings[2].start_far()
-    visit(1, sets[3])
-    for rings, _ in stages:
-        rings[2].start_right()
-    for rings, _ in stages:
-        rings[2].middle_right()
-    weights.first.turn()
+        for y in range(key_y, 4):
+            first, last = bounds[y]
+            allowed = (token <= last) & (token >= first)
+            for h in range(HEADS):
+                probs = jnp.exp(contract(keys, q_all[y, h], 1, 1))
+                probs = jnp.where(allowed, probs, 0.0)
+                delta = jnp.concatenate(
+                    [delta_all[y, 0, h : h + 1], delta_all[y, 1, h : h + 1]], axis=1
+                )
+                d_scores = (probs * (contract(values, do_all[y, h], 1, 1) - delta)).astype(BF)
+                value_term = jnp.dot(probs.astype(BF), do_all[y, h], preferred_element_type=F32)
+                key_term = jnp.dot(d_scores, q_all[y, h], preferred_element_type=F32)
+                d_values = value_term if d_values is None else d_values + value_term
+                d_keys = key_term if d_keys is None else d_keys + key_term
+                query_term = contract(keys, d_scores, 0, 0)
+                if y == key_y:
+                    dq_sum[y, h] = query_term
+                else:
+                    dq_sum[y, h] += query_term
+        grads[key_y, :, :, :, :HD] = d_keys.astype(BF).reshape(4, 4, STRIPE, HD)
+        grads[key_y, :, :, :, HD:] = d_values.astype(BF).reshape(4, 4, STRIPE, HD)
+
+    differ(3)
+    differ(2)
+    first_b.start()
     line_da.forward()
     line_h.start()
-    visit(2, w_loads[0:1])
-    for rings, _ in stages:
-        rings[2].start_left()
-    for rings, _ in stages:
-        rings[2].middle_left()
-    for rings, _ in stages:
-        net.settle(rings[2].a)
-        net.settle(rings[2].b)
-    visit(3, w_loads[1:2])
-    swap_dq = net.copy(dq_sum.at[:, :, theirs], dq_got, partner)
-    net.go(swap_dq)
+    differ(1)
+    first_b.middle()
+    differ(0)
+    first_a.start()
+    for y in range(4):
+        for h in range(HEADS):
+            dq_snd[y, h] = dq_sum[y, h, :, theirs].astype(BF)
+            dq_part[y, h] = dq_sum[y, h, :, mine].astype(BF)
+    net.go(dq_core)
+    weights.first.turn()
+    dq_core.wait_recv()
+    for y in range(4):
+        add_to(dq_part.at[y], dq_got.at[y])
+    dq_ring.start()
+    first_a.middle()
+    first_b.finish(first_b.lo(0), first_b.hi(0))
+    then_b.start()
+    first_a.finish(first_a.lo(0), first_a.hi(0))
+    then_a.start()
+    for load in ahead_loads:
+        load.wait()
+    weights.next()
     line_h.forward()
     line_da.finish()
     o_swap.wait()
-    late_term(0, da_line, o_line)
-    for load in w_loads:
+    turned[...] = jnp.transpose(da_line[...].reshape(4 * TOK, D))
+    late_term(0, turned, o_line)
+    dq_ring.middle()
+    then_b.middle()
+    then_a.middle()
+    then_b.finish(fin.at[2], fin.at[3])
+    then_a.finish(fin.at[0], fin.at[1])
+    fin_got[place.y] = fin[place.y]
+    fin_swap.start()
+    for load in w_loads[1:]:
         load.wait()
 
-    swap_dq.wait_recv()
+    dq_ring.finish(dq_done.at[pl.ds(0, 2)], dq_done.at[pl.ds(2, 2)])
     d_query = jnp.zeros((1, HD), F32)
     for h in range(HEADS):
-        e = jnp.transpose(dq_sum[h, :, mine] + dq_got[h]) * HD**-0.5
+        e = jnp.transpose(dq_done[h]) * HD**-0.5
         e = turn_back(e.astype(BF).astype(F32), cos_ref[...], sin_ref[...])
         u = q_pre[h]
         du, gain = norm_back(u, norm_scale(u), across(g_query), e)
@@ -835,44 +920,15 @@
         dq_own[h] = du.astype(BF)
     dq_line[place.x] = dq_own[head_of(place.x)]
     dq_swap.start()
-    for load in ahead_loads:
-        load.wait()
-    weights.next()
-
-    def finish_keys(level):
-        for (rings, views), (skip, rows, _, _) in zip(stages, PARTS):
-            lo, hi = halves(views[level])
-            if level:
-                rings[level].finish(lo(0), hi(0))
-                rings[level - 1].start()
-            else:
-                out = dkv.at[pl.ds(skip, rows)]
-                rings[level].finish(out.at[:, pl.ds(0, HD)], out.at[:, pl.ds(HD, HD)])
-
-    finish_keys(2)
-    d_h = sum(
-        contract(dq_own[h], buf[h // 2, :D, 256 * (h % 2) : 256 * (h % 2) + 256], 1, 1)
-        for h in range(HEADS)
-    )
-    dh[...] = d_h
     line_h.finish()
-    dq_swap.wait()
-    late_term(1, h_line, dq_line)
-    late_swap = net.copy(late_all.at[1 - core], late_got, partner)
-    net.go(late_swap)
-    for rings, _ in stages:
-        rings[1].middle()
-    late_swap.wait_recv()
-    for y in range(4):
-        add_to(late_got.at[y], late_all.at[core, y])
-    late_first.start()
-    finish_keys(1)
-    weights.turn_again()
-    for rings, _ in stages:
-        rings[0].middle()
-    late_first.middle()
-    finish_keys(0)
-
+    turned[...] = jnp.transpose(h_line[...].reshape(4 * TOK, D))
+    turned_swap = net.copy(
+        turned.at[pl.ds(pl.multiple_of((1 - core) * 576, 16), 576)], turned_other, partner
+    )
+    net.go(turned_swap)
+    fin_swap.wait()
+
+    dkv = jnp.concatenate([fin_got[j] for j in range(4)], axis=0)
     e = turn_back(dkv[:, :HD].astype(BF).astype(F32), cos_ref[...], sin_ref[...])
     u = k_pre[...]
     dk, d_key = norm_back(u, norm_scale(u), across(g_key), e)
@@ -880,16 +936,27 @@
     for i in range(2):
         kv_own[i] = dk[:, 128 * i : 128 * i + 128]
         kv_own[2 + i] = dv[:, 128 * i : 128 * i + 128]
-    kv_line[place.x] = kv_own[place.x]
-    kv_swap = Direct(net, place, "x", lambda j: kv_own.at[j], lambda j: kv_line.at[j])
+    kv_line[core, place.x] = kv_own[place.x]
+    kv_swap = Direct(net, place, "x", lambda j: kv_own.at[j], lambda j: kv_line.at[core, j])
     kv_swap.start()
-    d_h = dh[...] + contract(dk, wk[...], 1, 1) + contract(dv, wv[...], 1, 1)
+    kv_across = []
+    for by in range(4):
+        j = place.step("x", by)
+        device = place.device(x=j, core=1 - core)
+        kv_across.append(net.copy(kv_own.at[j], kv_line.at[core, place.x], device))
+        net.go(kv_across[by])
+    weights.turn_again()
+    dq_swap.wait()
+    late_term(1, turned, dq_line)
+    late_swap = net.copy(late_all.at[1 - core], late_got, partner)
+    net.go(late_swap)
+    d_h = contract(dk, wk[...], 1, 1) + contract(dv, wv[...], 1, 1)
+    for h in range(HEADS):
+        w = (wq, wq2)[h // 2]
+        d_h = d_h + contract(dq_own[h], w[:, 256 * (h % 2) : 256 * (h % 2) + 256], 1, 1)
     xf = x_ref[...].astype(F32)
     dx, d_attn = norm_back(xf, norm_scale(xf), across(g_attn), d_h)
     dx_out[...] = (dmid_ref[...] + dx).astype(BF)
-    late_first.finish(late_y.at[0], late_y.at[1])
-    late_second.start()
-
     def gain_swap(level, axis):
         return Direct(
             net, place, axis, lambda j: gain_got.at[level, at(axis)], lambda j: gain_got.at[level, j]
@@ -907,25 +974,32 @@
         [d_attn, gains_ref[0:3], norms, jnp.zeros((3, D), F32)], axis=0
     )
     swaps[0].start()
+    turned_swap.wait_recv()
     kv_swap.wait()
-    term = contract(h_line[...].reshape(4 * TOK, D), kv_line[...].reshape(4 * TOK, 128), 0, 0)
+    for copy in kv_across:
+        copy.wait_recv()
+    term = jnp.dot(
+        turned[pl.ds(pl.multiple_of(core * 576, 16), 576)],
+        kv_line[core].reshape(4 * TOK, 128),
+        preferred_element_type=F32,
+    )
+    term += jnp.dot(
+        turned_other[...], kv_line[1 - core].reshape(4 * TOK, 128), preferred_element_type=F32
+    )
     term = term.astype(BF)
-    for k in range(8):
-        w_all[k // 4, k % 4] = term[144 * k : 144 * k + 144]
-    w_swap = net.copy(w_all.at[1 - core], w_got, partner)
-    net.go(w_swap)
-    late_second.middle()
+    for k in range(4):
+        w_got[k] = term[144 * k : 144 * k + 144]
+    w_scatter = Direct(net, place, "y", lambda j: w_got.at[j], lambda j: w_y.at[j])
+    w_scatter.start()
+    w_y[place.y] = w_got[place.y]
+    late_swap.wait_recv()
+    for y in range(4):
+        add_to(late_got.at[y], late_all.at[core, y])
+    late_first.start()
     swaps[0].wait()
     gain_got[1, place.y] = gain_sum(0)
     swaps[1].start()
-    w_swap.wait_recv()
-    add_to(w_got, w_all.at[core])
-    w_scatter = Direct(net, place, "y", lambda j: w_got.at[j], lambda j: w_y.at[j])
-    w_scatter.start()
-    w_y[place.y] = w_got[place.y]
     weights.last()
-    late_second.finish(late_z.at[pl.ds(0, 80)], late_z.at[pl.ds(80, 64)])
-    weights.send_home()
     swaps[1].wait()
     gain_got[2, place.z] = gain_sum(1)
     swaps[2].start()
@@ -933,37 +1007,55 @@
     sum_to(w_z.at[place.z], [w_y.at[j] for j in range(4)])
     w_sums = Direct(net, place, "z", lambda j: w_z.at[place.z], lambda j: w_z.at[j])
     w_sums.start()
+    late_first.middle()
     swaps[2].wait()
     gain_got[3, core] = gain_sum(2)
     gain_last = net.copy(gain_got.at[3, core], gain_got.at[3, core], partner)
     net.go(gain_last)
     w_sums.wait()
-    sum_to(w_line.at[place.x, place.y], [w_z.at[j] for j in range(4)])
-    y_back = Direct(
-        net, place, "y", lambda j: w_line.at[place.x, place.y], lambda j: w_line.at[place.x, j]
-    )
-    y_back.start()
+    upper, lower = w_top.at[core], w_low.at[core]
+    sum_to(upper.at[place.x, place.y], [w_z.at[j, pl.ds(0, 80)] for j in range(4)])
+    sum_to(lower.at[place.x, place.y], [w_z.at[j, pl.ds(80, 64)] for j in range(4)])
+
+    def spread(axis, view):
+        return Direct(net, place, axis, lambda j: view(at(axis)), view)
+
+    first_way = [
+        spread("y", lambda j: upper.at[place.x, j]),
+        spread("x", lambda j: lower.at[j, place.y]),
+    ]
+    second_way = [spread("x", lambda j: upper.at[j]), spread("y", lambda j: lower.at[:, j])]
+    for line in first_way:
+        line.start()
+    late_first.finish(late_y.at[0], late_y.at[1])
+    late_second.start()
+    for line, then in zip(first_way, second_way):
+        line.wait()
+        then.start()
+    late_second.middle()
+    gain_last.wait_recv()
+    gains_out[...] = gain_got[3, 0] + gain_got[3, 1]
+    over = [net.copy(upper, upper, partner), net.copy(lower, lower, partner)]
+    for line, copy in zip(second_way, over):
+        line.wait()
+        net.go(copy)
+    late_second.finish(late_z.at[pl.ds(0, 80)], late_z.at[pl.ds(80, 64)])
+    weights.send_late()
+    for copy in over:
+        copy.wait_recv()
     weights.arrive()
     home_out[...] = weights.rcv[...]
-    y_back.wait()
-    x_back = Direct(net, place, "x", lambda j: w_line.at[place.x], lambda j: w_line.at[j])
-    x_back.start()
-    gain_last.wait_recv()
-    gains_out[...] = gain_got[3, 0] + gain_got[3, 1]
-    x_back.wait()
-    w_both[core] = w_line[...]
-    w_last = net.copy(w_line, w_both.at[core], partner)
-    net.go(w_last)
-    w_last.wait_recv()
+    late_out[...] = weights.late_rcv[...]
     net.drain()
 
 
 def attention_backward(hbm, small, call_id):
     shape = jax.ShapeDtypeStruct
     rooms = []
-    for _, rows, _, _ in PARTS:
-        for blocks in (1, 4, 16):
-            rooms += RingScatter.room_shapes((blocks * rows, HD), (blocks * rows, HD))
+    for _ in range(2):
+        rooms += RingScatter.room_shapes((4, STRIPE, 2 * HD), (4, STRIPE, 2 * HD))
+        rooms += RingScatter.room_shapes((STRIPE, 2 * HD), (STRIPE, 2 * HD))
+    rooms += RingScatter.room_shapes((2, HD, TOK), (2, HD, TOK))
     late_rooms = [
         *RingScatter.room_shapes((2, 144, 128), (2, 144, 128)),
         *RingScatter.room_shapes((80, 128), (64, 128)),
@@ -972,24 +1064,34 @@
         backward_kernel,
         out_shape=(
             shape((TOK, D), BF),
-            shape((8, 16, HALF + 384), BF),
-            shape((2, 4, 4, 144, 128), BF),
+            shape((8, 16, HALF + 256), BF),
+            shape((8, 16, 256), BF),
+            shape((2, 4, 4, 80, 128), BF),
+            shape((2, 4, 4, 64, 128), BF),
             shape((8, D), F32),
         ),
         in_specs=[pl.BlockSpec(memory_space=pl.ANY)] * len(hbm) + [IN_VMEM] * len(small),
-        out_specs=[IN_VMEM] * 4,
+        out_specs=[IN_VMEM] * 6,
         scratch_shapes=[
-            pltpu.VMEM((2, 2048, 2 * HD), BF),
+            pltpu.VMEM((4, 4, 4, STRIPE, 2 * HD), BF),
+            pltpu.VMEM((D, 2 * HD), BF),
+            pltpu.VMEM((D, 2 * HD), BF),
             pltpu.VMEM((D, HD), BF),
             pltpu.VMEM((D, HD), BF),
-            pltpu.VMEM((HEADS, ROWS, HD), BF),
-            pltpu.VMEM((2, 8, TOK), F32),
-            pltpu.VMEM((3, 2048, 2 * HD), BF),
-            pltpu.VMEM((HEADS, HD, ROWS), F32),
+            pltpu.VMEM((4, HEADS, ROWS, HD), BF),
+            pltpu.VMEM((4, 2, 8, TOK), F32),
+            pltpu.VMEM((KEYS, 128), jnp.int32),
+            pltpu.VMEM((4, 4, 4, STRIPE, 2 * HD), BF),
+            pltpu.VMEM((4, STRIPE, 2 * HD), F32),
+            pltpu.VMEM((4, STRIPE, 2 * HD), F32),
+            pltpu.VMEM((4, HEADS, HD, ROWS), F32),
+            pltpu.VMEM((4, HEADS, HD, TOK), BF),
+            pltpu.VMEM((4, HEADS, HD, TOK), BF),
+            pltpu.VMEM((4, HEADS, HD, TOK), BF),
             pltpu.VMEM((HEADS, HD, TOK), F32),
-            pltpu.VMEM((TOK, 2 * HD), F32),
             pltpu.VMEM((4, TOK, D), BF),
             pltpu.VMEM((4, TOK, D), BF),
+            pltpu.VMEM((D, 4 * TOK), BF),
             pltpu.VMEM((4, TOK, HD), BF),
             pltpu.VMEM((4, TOK, HD), BF),
             pltpu.VMEM((4, TOK, HD), BF),
@@ -1000,18 +1102,16 @@
             pltpu.VMEM((144, 128), F32),
             pltpu.VMEM((4, 4, 8, D), F32),
             pltpu.VMEM((4, TOK, 128), BF),
-            pltpu.VMEM((4, TOK, 128), BF),
-            pltpu.VMEM((2, 4, 144, 128), BF),
+            pltpu.VMEM((2, 4, TOK, 128), BF),
+            pltpu.VMEM((576, 4 * TOK), BF),
             pltpu.VMEM((4, 144, 128), BF),
             pltpu.VMEM((4, 144, 128), BF),
             pltpu.VMEM((4, 144, 128), BF),
-            pltpu.VMEM((4, 4, 144, 128), BF),
-            pltpu.VMEM((TOK, D), F32),
             *rooms,
             *late_rooms,
             *WeightSums.scratch(),
             *sems(160),
-            *sems(8),
+            *sems(16),
             pltpu.SemaphoreType.DMA((24,)),
         ],
         compiler_params=params(call_id),
@@ -1246,13 +1346,13 @@
     net.go(ahead_swap)
     each(blocks, backward, 1)
     h_sums[0].middle()
-    each(3, back_project, 1)
-    h_sums[1].start()
     ahead_swap.wait_recv()
     for i in range(2):
         fill(ahead_got, i, core, f_turned, act, None, True)
     ahead.begin()
     ahead.go_on()
+    each(3, back_project, 1)
+    h_sums[1].start()
     for i in range(2):
         fill_later(snd, i, 1 - core, False)
         net.go(swaps[2 * i])
@@ -1400,7 +1500,8 @@
 
 class WeightSums:
     def __init__(self, place, net, sums, late, refs, marks):
-        y_here, z_here, y1, z1, z2, y2, snd, rcv, *rooms = refs
+        y_here, z_here, y1, z1, z2, y2, snd, late_snd, rcv, late_rcv, *rooms = refs
+        self.late_snd, self.late_rcv = late_snd, late_rcv
         self.place, self.late, self.snd, self.rcv, self.marks = place, late, snd, rcv, marks
         self.y1, self.z1, self.y2, self.z2 = y1, z1, y2, z2
         self.x_hi, self.x_lo = lax.div(place.x, 2), lax.rem(place.x, 2)
@@ -1442,8 +1543,10 @@
             pltpu.VMEM((4, 144, rest), BF),
             pltpu.VMEM((144, CUT), F32),
             pltpu.VMEM((144, rest), F32),
-            pltpu.VMEM((8, 16, HALF + 384), BF),
-            pltpu.VMEM((8, 16, HALF + 384), BF),
+            pltpu.VMEM((8, 16, HALF + 256), BF),
+            pltpu.VMEM((8, 16, 256), BF),
+            pltpu.VMEM((8, 16, HALF + 256), BF),
+            pltpu.VMEM((8, 16, 256), BF),
             *FirstSums.room_shapes(LATER_CUT, LATER - LATER_CUT),
             *RingScatter.room_shapes((144, 384), (144, 384)),
             *RingScatter.room_shapes((144, 384), (144, 256)),
@@ -1466,18 +1569,30 @@
         z2, y2 = self.z2, self.y2
         self.z_second.finish(z2.at[:, pl.ds(0, 384)], z2.at[:, pl.ds(384, 384)])
         self.y_second.finish(y2.at[:, pl.ds(0, 384)], y2.at[:, pl.ds(384, 256)])
-
-    def send_home(self):
-        snd = self.snd
-        total = jnp.concatenate([self.z2[...], self.y2[...], self.late[...]], axis=1)
-        blank = jnp.zeros((8, 128), F32)
+        total = jnp.concatenate([z2[...], y2[...]], axis=1)
+        self.pack(total, self.snd)
+        self.exchange(self.snd, self.rcv, 0)
+
+    def send_late(self):
+        self.pack(self.late[...], self.late_snd)
+        self.exchange(self.late_snd, self.late_rcv, 8)
+
+    @staticmethod
+    def pack(total, snd):
+        width = total.shape[1]
+        count = width // 128
         for k in range(8):
             extra = total[18 * k + 16 : 18 * k + 18]
-            pieces = [extra[:, 128 * n : 128 * n + 128] for n in range(12)]
-            snd[k, :, : HALF + 128] = total[18 * k : 18 * k + 16].astype(BF)
-            for n, group in enumerate((pieces[:8], pieces[8:] + [blank])):
-                at = HALF + 128 + 128 * n
+            pieces = [extra[:, 128 * n : 128 * n + 128] for n in range(count)]
+            snd[k, :, :width] = total[18 * k : 18 * k + 16].astype(BF)
+            for n in range(0, count, 8):
+                group = pieces[n : n + 8]
+                if len(group) < 8:
+                    group.append(jnp.zeros((16 - 2 * len(group), 128), F32))
+                at = width + 16 * n
                 snd[k, :, at : at + 128] = jnp.concatenate(group, axis=0).astype(BF)
+
+    def exchange(self, snd, rcv, mark):
         place = self.place
         send, recv, here = self.marks
         row_half = lax.div(place.z, 2)
@@ -1487,9 +1602,9 @@
         for k in range(8):
             copy = pltpu.make_async_remote_copy(
                 src_ref=snd.at[k],
-                dst_ref=self.rcv.at[self.slot],
-                send_sem=send.at[k],
-                recv_sem=recv.at[self.slot],
+                dst_ref=rcv.at[self.slot],
+                send_sem=send.at[mark + k],
+                recv_sem=recv.at[mark + self.slot],
                 device_id=place.device(x=row_half * 2 + self.x_lo, z=k // 2, core=k % 2),
                 device_id_type=MESH,
             )
@@ -1501,34 +1616,37 @@
 
             @pl.when(is_here)
             def _(k=k):
-                keep = pltpu.make_async_copy(snd.at[k], self.rcv.at[self.slot], here.at[0])
+                keep = pltpu.make_async_copy(snd.at[k], rcv.at[self.slot], here.at[0])
                 keep.start()
                 keep.wait()
 
     def arrive(self):
         send, recv, _ = self.marks
-        for m in range(8):
-            arrival = pltpu.make_async_remote_copy(
-                src_ref=self.snd.at[m],
-                dst_ref=self.rcv.at[m],
-                send_sem=send.at[m],
-                recv_sem=recv.at[m],
-                device_id=self.place.partner(),
-                device_id_type=MESH,
-            )
-
-            @pl.when(jnp.logical_not(self.stays & (self.slot == m)))
-            def _(arrival=arrival):
-                arrival.wait_recv()
-
-            @pl.when(jnp.logical_not(self.stays & (self.own == m)))
-            def _(arrival=arrival):
-                arrival.wait_send()
+        for mark, snd, rcv in ((0, self.snd, self.rcv), (8, self.late_snd, self.late_rcv)):
+            for m in range(8):
+                arrival = pltpu.make_async_remote_copy(
+                    src_ref=snd.at[m],
+                    dst_ref=rcv.at[m],
+                    send_sem=send.at[mark + m],
+                    recv_sem=recv.at[mark + m],
+                    device_id=self.place.partner(),
+                    device_id_type=MESH,
+                )
+
+                @pl.when(jnp.logical_not(self.stays & (self.slot == m)))
+                def _(arrival=arrival):
+                    arrival.wait_recv()
+
+                @pl.when(jnp.logical_not(self.stays & (self.own == m)))
+                def _(arrival=arrival):
+                    arrival.wait_send()
 
 
 def last_kernel(
     home_ref,
-    w_ref,
+    late_ref,
+    top_ref,
+    low_ref,
     gains_ref,
     y_ref,
     dx_ref,
@@ -1546,11 +1664,11 @@
     y_out[...] = y_ref[...]
     dx_out[...] = dx_ref[...]
 
-    def rows_at(slot, n):
-        spare, at = HALF + 128 + 128 * (n // 8), 2 * (n % 8)
-        more = home_ref[slot, :, spare : spare + 128].astype(F32)[at : at + 2]
+    def rows_at(ref, slot, n):
+        spare = (HALF if ref is home_ref else 128) + 128 * (n // 8)
+        more = ref[slot, :, spare : spare + 128].astype(F32)[2 * (n % 8) : 2 * (n % 8) + 2]
         return jnp.concatenate(
-            [home_ref[slot, :, 128 * n : 128 * n + 128].astype(F32), more], axis=0
+            [ref[slot, :, 128 * n : 128 * n + 128].astype(F32), more], axis=0
         )
 
     def tile(x_hi, which, n):
@@ -1560,7 +1678,7 @@
         else:
             c, n = n // 4, n % 4
             at = 128 * n if n < 2 else CUT + 128 * (n - 2)
-        return rows_at(x_hi * 4 + core * 2 + c, at // 128)
+        return rows_at(home_ref, x_hi * 4 + core * 2 + c, at // 128)
 
     for which, out in enumerate((dwg_out, dwu_out, dwd_out)):
         for n in range(27):
@@ -1573,14 +1691,16 @@
             out[:, span] = value
     for k in range(4):
         span = slice(128 * k, 128 * k + 128)
-        dwo_out[:, span] = rows_at(2 * k, HALF // 128)
-        dwq_out[:, span] = rows_at(2 * k + 1, HALF // 128)
+        dwo_out[:, span] = rows_at(late_ref, 2 * k, 0)
+        dwq_out[:, span] = rows_at(late_ref, 2 * k + 1, 0)
     for which in range(2):
         for j in range(4):
             out = (dwk_out, dwv_out)[j // 2]
             for y in range(4):
-                rows = slice(576 * which + 144 * y, 576 * which + 144 * y + 144)
-                out[rows, 128 * (j % 2) : 128 * (j % 2) + 128] = w_ref[which, j, y].astype(F32)
+                span = slice(128 * (j % 2), 128 * (j % 2) + 128)
+                at = 576 * which + 144 * y
+                out[at : at + 80, span] = top_ref[which, j, y].astype(F32)
+                out[at + 80 : at + 144, span] = low_ref[which, j, y].astype(F32)
     for out, row, start in zip(gain_outs, (0, 4, 4, 1, 2, 3), (0, 0, HD, 0, 0, 0)):
         size = out.shape[0]
         out[...] = gains_ref[row : row + 1, start : start + size].reshape(size)
@@ -1602,7 +1722,7 @@
             shape((18, 2 * HID), F32),
             *(shape((size,), F32) for size in (D, HD, HD, D, D, D)),
         ),
-        in_specs=[IN_VMEM] * 5,
+        in_specs=[IN_VMEM] * len(args),
         out_specs=[IN_VMEM] * 15,
         compiler_params=pltpu.CompilerParams(vmem_limit_bytes=VMEM_BYTES),
     )(*args)
@@ -1682,7 +1802,7 @@
         ),
         6,
     )
-    d_input, home, w_both, gains = attention_backward(
+    d_input, home, late, w_top, w_low, gains = attention_backward(
         (kv_all, sums, ahead_y, ahead_z, w_query, wq_other, w_key, w_value),
         (
             q_all,
@@ -1707,7 +1827,7 @@
         8,
     )
     y, dx, d_wq, d_wk, d_wv, d_wo, d_wg, d_wu, d_wd, *d_norms = last_layout(
-        home, w_both, gains, layer_output, d_input
+        home, late, w_top, w_low, gains, layer_output, d_input
     )
     return (y, dx, d_wq, d_wk, d_wv, d_wo.T, d_wg, d_wu, d_wd.T, *d_norms)
 

time: 265 us -> 257 us (0.970)
  the two profiles are of different devices: /device:TPU:1 before, /device:TPU:7 now
where the time goes in v7:
time: 257 us; the launch traced here: 252 us
  Pallas kernels  249 us (97%)
    pallas_call x1, Pallas kernels, attention_backward(): pl.pallas_call(backward_kernel, out_shape=(shape((TOK, D), BF), shape((8,...  111 us
    pallas_call x1, Pallas kernels, feed_forward(): pl.pallas_call(feed_kernel, out_shape=(shape((TOK, D), BF), shape((TOK, D...  79.3 us
    pallas_call x1, Pallas kernels, attention_forward(): pl.pallas_call(forward_kernel, out_shape=(shape((4, 4, 4, STRIPE, 2 * HD)...  55.7 us

profile of v7, /device:TPU:7, one launch (start us, length us, event | category | flops | bytes accessed | tf_op | source)
XLA Modules:
  0.0 252.0 jit_solution(13641531685202220727)
XLA Ops:
  0.7 0.8 dynamic-slice_convert_fusion
  1.4 1.0 multiply_sine_fusion
  2.4 55.7 %shard_map.289 = (bf16[4,4,4,32,512]{4,3,2,1,0:T(8,128)(2,1)}, bf16[4,4,256,256]{3,2,1,0:T(8,128)(2,1)}, bf16[1152,512]{1,0:T(8,128)(2,1)}, bf16[512,1152]{1,0:T...) custom-call(bf16[128,1152]{1,0:T(8,128)(2,1)} %x_ref.5, ...), custom_call_target="tpu_custom_call" | custom-call | tf_op jit(solution)/shard_map/pallas_call | solution.py:568
  58.1 79.3 %shard_map.290 = (bf16[128,1152]{1,0:T(8,128)(2,1)}, f32[128,1152]{1,0:T(8,128)}, bf16[128,1152]{1,0:T(8,128)(2,1)}, bf16[4,128,256]{2,1,0:T(8,128)(2,1)}, f32[8...) custom-call(bf16[128,1152]{1,0:T(8,128)(2,1)} %x_ref.5, ...), custom_call_target="tpu_custom_call" | custom-call | tf_op jit(solution)/shard_map/pallas_call | solution.py:1404
  137.4 110.7 %shard_map.291 = (bf16[128,1152]{1,0:T(8,128)(2,1)}, bf16[8,16,1664]{2,1,0:T(8,128)(2,1)}, bf16[8,16,256]{2,1,0:T(8,128)(2,1)}, bf16[2,4,4,80,128]{4,3,2,1,0:T(8...) custom-call(bf16[4,4,4,32,512]{4,3,2,1,0:T(8,128)(2,1)} %get-tuple-element.54.kv_hbm, ...), custom_call_target="tpu_custom_call" | custom-call | tf_op jit(solution)/shard_map/pallas_call | solution.py:1063
  248.2 3.6 %shard_map.292 = (bf16[128,1152]{1,0:T(8,128)(2,1)}, bf16[128,1152]{1,0:T(8,128)(2,1)}, f32[18,512]{1,0:T(8,128)}, f32[1152,256]{1,0:T(8,128)}, f32[1152,256]{1,...) custom-call(bf16[8,16,1664]{2,1,0:T(8,128)(2,1)} %get-tuple-element., ...), custom_call_target="tpu_custom_call" | custom-call | tf_op jit(solution)/shard_map/pallas_call | solution.py:1711
  (1 shorter events, 0.0 us)
